TPU v7x, 128 devices: a whole 4x4x4 slice. The times are simulated.
128 devices in a mesh: seq: 16 (over y, z), head: 8 (over x, core).
Axes of the slice: x: 4, y: 4, z: 4, core: 2. Of those that a mesh axis runs over, the one named last changes fastest.
Arguments:
- block_input: bfloat16 [8192, 2048], P('seq', 'head'), may hold values from -6 to 6
- log_decay: float32 [8192, 16], P('seq', 'head'), may hold values from -2.2 to 0, as said below
- first_gain: float32 [2048], replicated, may hold values from 0.5 to 1.5
- query_weight: bfloat16 [2048, 2048], P(None, 'head'), may hold values from -0.125 to 0.125
- key_weight: bfloat16 [2048, 2048], P(None, 'head'), may hold values from -0.125 to 0.125
- value_weight: bfloat16 [2048, 4096], P(None, 'head'), may hold values from -0.125 to 0.125
- gate_weight: bfloat16 [2048, 4096], P(None, 'head'), may hold values from -0.125 to 0.125
- beta_weight: bfloat16 [2048, 16], P(None, 'head'), may hold values from -0.125 to 0.125
- query_conv: float32 [2048, 4], P('head'), may hold values from -3 to 3
- key_conv: float32 [2048, 4], P('head'), may hold values from -3 to 3
- value_conv: float32 [4096, 4], P('head'), may hold values from -3 to 3
- mixer_gain: float32 [4096], P('head'), may hold values from 0.5 to 1.5
- mixer_weight: bfloat16 [2048, 4096], P(None, 'head'), may hold values from -0.09375 to 0.09375
- second_gain: float32 [2048], replicated, may hold values from 0.5 to 1.5
- swiglu_gate: bfloat16 [2048, 5632], P(None, 'head'), may hold values from -0.125 to 0.125
- swiglu_up: bfloat16 [2048, 5632], P(None, 'head'), may hold values from -0.125 to 0.125
- swiglu_down: bfloat16 [2048, 5632], P(None, 'head'), may hold values from -0.078125 to 0.078125
- cotangent: bfloat16 [8192, 2048], P('seq', 'head'), may hold values from -6 to 6
Outputs:
- output: bfloat16 [8192, 2048], P('seq', 'head')
- grad_input: float32 [8192, 2048], P('seq', 'head')
- grad_first_gain: float32 [2048], P('seq')
- grad_query_weight: float32 [2048, 2048], P('seq', 'head')
- grad_key_weight: float32 [2048, 2048], P('seq', 'head')
- grad_value_weight: float32 [2048, 4096], P('seq', 'head')
- grad_gate_weight: float32 [2048, 4096], P('seq', 'head')
- grad_beta_weight: float32 [2048, 16], P('seq', 'head')
- grad_query_conv: float32 [2048, 4], P('head')
- grad_key_conv: float32 [2048, 4], P('head')
- grad_value_conv: float32 [4096, 4], P('head')
- grad_mixer_gain: float32 [4096], P('head')
- grad_mixer_weight: float32 [2048, 4096], P('seq', 'head')
- grad_second_gain: float32 [2048], P('seq')
- grad_swiglu_gate: float32 [2048, 5632], P('seq', 'head')
- grad_swiglu_up: float32 [2048, 5632], P('seq', 'head')
- grad_swiglu_down: float32 [2048, 5632], P('seq', 'head')
Inputs may be any that keep to these rules, and one draw needn't show every extreme that they name: `log_decay`: every entry is negative.
All inputs are finite; a program needn't handle non-finite values.
Results may differ from a plain program's by a relative error of at most 0.025.
Values may be sent and summed in bfloat16 or wider, within the bound.
No kernel may reach another device: no remote copies, remote signals or barrier semaphores. Data moves between devices by JAX's collectives and lax.ppermute only.
A program may use at most 192 MiB of HBM per device.

v0:
```python
from functools import partial

import jax
import jax.numpy as jnp
from jax import lax
from jax.experimental import pallas as pl
from jax.experimental.pallas import tpu as pltpu
from jax.sharding import Mesh
from jax.sharding import PartitionSpec as P

DK = 128
DV = 256
CH = 128
EPS_NORM = 1e-06
EPS_GATE = 1e-05
FLOAT = jnp.float32
HALF = jnp.bfloat16
NN = (((1,), (0,)), ((), ()))
NT = (((1,), (1,)), ((), ()))
TN = (((0,), (0,)), ((), ()))


def mm(a, b, dims=NN):
    return lax.dot_general(a.astype(HALF), b.astype(HALF), dims, preferred_element_type=FLOAT)


def halves(a):
    high = a.astype(HALF)
    return high, (a - high.astype(FLOAT)).astype(HALF)


def mm2(a, b, dims=NN):
    high, low = halves(b)
    return mm(a, high, dims) + mm(a, low, dims)


def mm3(a, b, dims=NN):
    a_high, a_low = halves(a)
    b_high, b_low = halves(b)
    return mm(a_high, b_high, dims) + (mm(a_high, b_low, dims) + mm(a_low, b_high, dims))


def sigmoid(v):
    return 1.0 / (1.0 + jnp.exp(-v))


def square_masks():
    rows = lax.broadcasted_iota(jnp.int32, (CH, CH), 0)
    cols = lax.broadcasted_iota(jnp.int32, (CH, CH), 1)
    return rows, cols


def decay_matrix(gcol, grow):
    rows, cols = square_masks()
    return jnp.where(rows >= cols, jnp.exp(jnp.minimum(gcol - grow, 0.0)), 0.0)


def conv_of(wide, taps, start, count, lanes):
    total = wide[HALO - 3 + start : HALO - 3 + start + count, lanes] * taps[0:1, lanes]
    for j in range(1, 4):
        total = total + wide[HALO - 3 + j + start : HALO - 3 + j + start + count, lanes] * taps[j : j + 1, lanes]
    return total


def prepare_kernel(heads, chunks, proj, halo, taps, logits, gcol, grow, q_out, k_out, v_out, t_out, n_out, b_out, w_out, u_out, p_out, pay, token, wide):
    token[...] = jnp.zeros(token.shape, FLOAT)
    rows, cols = square_masks()
    differ = rows ^ cols
    eye = jnp.where(rows == cols, 1.0, 0.0)
    wide[:HALO, :] = halo[...].astype(FLOAT)
    wide[HALO:, :] = proj[...].astype(FLOAT)
    kq = heads * DK
    work = [(h, c) for h in range(heads) for c in range(chunks)]
    low, keys, sides = {}, {}, {}
    for h, c in work:
        span = slice(c * CH, (c + 1) * CH)
        ql, kl, vl = (
            slice(h * DK, (h + 1) * DK),
            slice(kq + h * DK, kq + (h + 1) * DK),
            slice(2 * kq + h * DV, 2 * kq + (h + 1) * DV),
        )
        cq = conv_of(wide, taps, c * CH, CH, ql)
        query = (cq * sigmoid(cq)).astype(HALF)
        ck = conv_of(wide, taps, c * CH, CH, kl)
        act = ck * sigmoid(ck)
        key = (act * lax.rsqrt(jnp.sum(act * act, axis=-1, keepdims=True) + EPS_NORM)).astype(HALF)
        cv = conv_of(wide, taps, c * CH, CH, vl)
        value = (cv * sigmoid(cv)).astype(HALF)
        q_out[span, ql] = query
        k_out[span, ql] = key
        v_out[span, h * DV : (h + 1) * DV] = value
        beta = sigmoid(logits[span, h : h + 1])
        g = gcol[span, h : h + 1]
        spread = decay_matrix(g, grow[h * chunks + c : h * chunks + c + 1, :])
        inner = mm(key, key, NT)
        low[h, c] = jnp.where(rows > cols, beta * spread * inner, 0.0)
        p_out[h * chunks + c] = (spread * mm(query, key, NT)).astype(HALF)
        keys[h, c] = key
        sides[h, c] = jnp.concatenate([(beta * jnp.exp(g)) * key.astype(FLOAT), beta * value.astype(FLOAT)], axis=1)
    tri = {at: eye - jnp.where(differ < 2, low[at], 0.0) for at in work}
    size = 2
    while size < CH:
        part = {at: mm3(jnp.where((differ >= size) & (differ < 2 * size), low[at], 0.0), tri[at]) for at in work}
        tri = {at: tri[at] - mm3(tri[at], part[at]) for at in work}
        size *= 2
    steps = {}
    for h, c in work:
        at = h * chunks + c
        t_out[at] = tri[h, c].astype(HALF)
        solved = mm3(tri[h, c], sides[h, c])
        w_out[at] = solved[:, :DK].astype(HALF)
        u_out[at] = solved[:, DK:].astype(HALF)
        g = gcol[c * CH : (c + 1) * CH, h : h + 1]
        last = gcol[(c + 1) * CH - 1 : (c + 1) * CH, h : h + 1]
        step = mm2(keys[h, c], jnp.exp(last - g) * solved, TN)
        n_out[at] = step[:, :DK].astype(HALF)
        b_out[at] = step[:, DK:]
        steps[h, c] = (jnp.exp(last), step)
    zero = jnp.zeros((DK, DK), FLOAT)
    for h in range(heads):
        decay, step = steps[h, 0]
        total = jnp.concatenate([decay * eye - step[:, :DK], step[:, DK:]], axis=1)
        whole = decay
        for c in range(1, chunks):
            decay, step = steps[h, c]
            total = decay * total - mm3(step[:, :DK], total) + jnp.concatenate([zero, step[:, DK:]], axis=1)
            whole = whole * decay
        pack_map(pay, h, total, whole, eye)


def whole_decay(pay, j, h):
    return pay[j, h, DK : DK + 1, 0:1].astype(FLOAT) + pay[j, h, DK + 8 : DK + 9, 0:1].astype(FLOAT)


def apply_whole(pay, j, h, state, dims):
    return whole_decay(pay, j, h) * state + mm(pay[j, h, :DK, :DK], state, dims)


def pack_map(pay, h, total, whole, eye):
    pay[h, :DK, :] = jnp.concatenate([total[:, :DK] - whole * eye, total[:, DK:]], axis=1).astype(HALF)
    rest = jnp.broadcast_to(whole, (8, DK + DV))
    first = rest.astype(HALF).astype(FLOAT)
    pay[h, DK:, :] = jnp.concatenate([first, rest - first], axis=0).astype(HALF)


def group_kernel(heads, mine, p0, p1, p2, p3, before, group, near):
    me = mine[3]
    for k, piece in enumerate((p0, p1, p2, p3)):
        near[ring_place(me, k)] = piece[...]
    rows, cols = square_masks()
    eye = jnp.where(rows == cols, 1.0, 0.0)
    zero = jnp.zeros((DK, DK), FLOAT)
    start = jnp.concatenate([eye, jnp.zeros((DK, DV), FLOAT)], axis=1)
    totals, keeps, wholes = [start] * heads, [start] * heads, [jnp.ones((1, 1), FLOAT)] * heads
    for j in range(near.shape[0]):
        for h in range(heads):
            added = jnp.concatenate([zero, near[j, h, :DK, DK:].astype(FLOAT)], axis=1)
            if j == 0:
                moved = jnp.concatenate([whole_decay(near, j, h) * eye + near[j, h, :DK, :DK].astype(FLOAT), added[:, DK:]], axis=1)
            else:
                moved = apply_whole(near, j, h, totals[h], NN) + added
            totals[h] = moved
            wholes[h] = wholes[h] * whole_decay(near, j, h)
            keeps[h] = jnp.where(me == j + 1, moved, keeps[h])
    for h in range(heads):
        before[h] = keeps[h]
        pack_map(group, h, totals[h], wholes[h], eye)


def group_back_kernel(heads, mine, near, p0, p1, p2, p3, after, group, ends, token):
    token[...] = jnp.zeros(token.shape, FLOAT)
    me = mine[3]
    for k, piece in enumerate((p0, p1, p2, p3)):
        ends[ring_place(me, k)] = piece[...]
    rows, cols = square_masks()
    eye = jnp.where(rows == cols, 1.0, 0.0)
    zero = jnp.zeros((DK, DK), FLOAT)
    start = jnp.concatenate([eye, jnp.zeros((DK, DV), FLOAT)], axis=1)
    totals, keeps = [start] * heads, [start] * heads
    for j in reversed(range(near.shape[0])):
        for h in range(heads):
            keeps[h] = jnp.where(me == j, totals[h], keeps[h])
            added = jnp.concatenate([zero, ends[j, h].astype(FLOAT)], axis=1)
            totals[h] = apply_whole(near, j, h, totals[h], TN) + added
    for h in range(heads):
        after[h] = keeps[h]
        group[h] = totals[h][:, DK:].astype(HALF)


def spread_rows(core, total, own, other, rows, lanes):
    for x in range(4):
        mine = pl.ds(pl.multiple_of((2 * x + core) * rows, rows), rows)
        away = pl.ds(pl.multiple_of((2 * x + 1 - core) * rows, rows), rows)
        own[x, :, lanes] = total[mine, :].astype(HALF)
        other[x, :, lanes] = total[away, :].astype(HALF)


def mix_kernel(heads, chunks, mine, p0, p1, p2, p3, before, q, k, w, u, p, n, b, gcol, gate, gain, weight, s_out, vn_out, o_out, gated, other, own, pay, total):
    ranks = pay.shape[0]
    me = mine[2]
    for at, piece in enumerate((p0, p1, p2, p3)):
        pay[ring_place(me, at)] = piece[...]
    states = [jnp.zeros((DK, DV), FLOAT) for h in range(heads)]
    for j in range(ranks - 1):
        passed = j < me
        for h in range(heads):
            moved = apply_whole(pay, j, h, states[h], NN) + pay[j, h, :DK, DK:].astype(FLOAT)
            states[h] = jnp.where(passed, moved, states[h])
    for h in range(heads):
        states[h] = mm3(before[h, :, :DK], states[h]) + before[h, :, DK:]
    for c in range(chunks):
        span = slice(c * CH, (c + 1) * CH)
        for h in range(heads):
            at = h * chunks + c
            state = states[h].astype(HALF)
            s_out[at] = state
            g = gcol[span, h : h + 1]
            last = gcol[(c + 1) * CH - 1 : (c + 1) * CH, h : h + 1]
            vn = (u[at].astype(FLOAT) - mm(w[at], state)).astype(HALF)
            vn_out[at] = vn
            out = jnp.exp(g) * mm(q[span, h * DK : (h + 1) * DK], state) + mm(p[at], vn)
            vl = slice(h * DV, (h + 1) * DV)
            o_out[span, vl] = out
            factor = lax.rsqrt(jnp.mean(out * out, axis=-1, keepdims=True) + EPS_GATE)
            pre = gate[span, vl]
            gated[span, vl] = (out * factor * gain[:, vl] * (pre * sigmoid(pre))).astype(HALF)
            if c + 1 < chunks:
                states[h] = jnp.exp(last) * states[h] - mm(n[at], state) + b[at]
    width = weight.shape[0]
    tile = total.shape[1]
    rows = own.shape[1]
    for at in range(0, width, tile):
        lanes = slice(at, at + tile)
        total[...] = mm(gated[...], weight[lanes, :], NT)
        spread_rows(mine[1], total, own, other, rows, lanes)


def gate_back_kernel(heads, chunks, d_gated, out, gate, gain, q, w, p, n, gcol, do_out, dvn_out, e_out, dpre_out, dgain_out, sums_out, pay):
    dgain = [jnp.zeros((1, DV), FLOAT) for h in range(heads)]
    ends = [None] * heads
    for c in reversed(range(chunks)):
        span = slice(c * CH, (c + 1) * CH)
        for h in range(heads):
            at = h * chunks + c
            vl = slice(h * DV, (h + 1) * DV)
            dg, o, pre, gn = d_gated[span, vl], out[span, vl], gate[span, vl], gain[:, vl]
            sig = sigmoid(pre)
            factor = lax.rsqrt(jnp.mean(o * o, axis=-1, keepdims=True) + EPS_GATE)
            m = o * factor
            s = pre * sig
            dgm = dg * m
            dgain[h] = dgain[h] + jnp.sum(dgm * s, axis=0, keepdims=True)
            dpre = dgm * gn * (sig * (1.0 + pre * (1.0 - sig)))
            dpre_out[span, vl] = dpre.astype(HALF)
            row_sum = jnp.sum(dpre * pre, axis=-1, keepdims=True)
            sums_out[span, :] = row_sum if h == 0 else sums_out[span, :] + row_sum
            e = dg * gn * s
            dout = factor * (e - m * jnp.mean(e * m, axis=-1, keepdims=True))
            do_out[span, vl] = dout.astype(HALF)
            g = gcol[span, h : h + 1]
            last = gcol[(c + 1) * CH - 1 : (c + 1) * CH, h : h + 1]
            dvn = mm(p[at], dout, TN)
            dvn_out[at] = dvn
            source = mm(q[span, h * DK : (h + 1) * DK], jnp.exp(g) * dout, TN) - mm(w[at], dvn, TN)
            e_out[at] = source
            if ends[h] is None:
                ends[h] = source
            else:
                ends[h] = jnp.exp(last) * ends[h] - mm(n[at], ends[h], TN) + source
    for h in range(heads):
        pay[h] = ends[h].astype(HALF)
        dgain_out[0:1, h * DV : (h + 1) * DV] = dgain[h]


def back_kernel(heads, chunks, mine, pay, p0, p1, p2, p3, after, q, k, v, logits, gate_sums, gcol, grow, tri, states, vns, dos, dvns, es, ns, proj, halo, taps, dproj_out, dlogit_out, logit_rows, dtaps_out, sums_out, wide, dconv, late, rowsum):
    ranks = pay.shape[0]
    tokens = chunks * CH
    me = mine[2]
    for at, piece in enumerate((p0, p1, p2, p3)):
        late[ring_place(me, at)] = piece[...]
    kq = heads * DK
    width = 2 * kq + heads * DV
    rows, cols = square_masks()
    grads = [jnp.zeros((DK, DV), FLOAT) for h in range(heads)]
    for j in reversed(range(1, ranks)):
        passed = j > me
        for h in range(heads):
            moved = apply_whole(pay, j, h, grads[h], TN) + late[j, h].astype(FLOAT)
            grads[h] = jnp.where(passed, moved, grads[h])
    for h in range(heads):
        grads[h] = mm3(after[h, :, :DK], grads[h]) + after[h, :, DK:]
    wide[:HALO, :] = halo[...].astype(FLOAT)
    wide[HALO:, :] = proj[...].astype(FLOAT)
    logit_rows[...] = jnp.zeros(logit_rows.shape, FLOAT)
    dconv[0:HALO, :] = jnp.zeros((HALO, width), FLOAT)
    dconv[HALO + tokens :, :] = jnp.zeros((8, width), FLOAT)
    for c in reversed(range(chunks)):
        span = slice(c * CH, (c + 1) * CH)
        for h in range(heads):
            at = h * chunks + c
            ql, kl, vl, ol = (
                slice(h * DK, (h + 1) * DK),
                slice(kq + h * DK, kq + (h + 1) * DK),
                slice(2 * kq + h * DV, 2 * kq + (h + 1) * DV),
                slice(h * DV, (h + 1) * DV),
            )
            grad = grads[h].astype(HALF)
            query, key, value = q[span, ql], k[span, ql], v[span, ol]
            state, vn, dout = states[at], vns[at], dos[span, ol]
            logit = logits[span, h : h + 1]
            beta = sigmoid(logit)
            g = gcol[span, h : h + 1]
            last = gcol[(c + 1) * CH - 1 : (c + 1) * CH, h : h + 1]
            eg, ed = jnp.exp(g), jnp.exp(last - g)
            spread = decay_matrix(g, grow[at : at + 1, :])
            strict = jnp.where(rows > cols, spread, 0.0)
            inner = mm(key, key, NT)
            dvn = dvns[at] + ed * mm(key, grad)
            dr = mm(tri[at], dvn, TN)
            drh = dr.astype(HALF)
            ks = mm(key, state)
            dval = beta * dr
            both = mm(jnp.concatenate([dout, drh], axis=0), state, NT)
            dkeep = mm(vn, grad, NT)
            pair = mm(jnp.concatenate([dout, drh], axis=0), vn, NT)
            dqk = spread * pair[:CH]
            da = -(strict * pair[CH:])
            dkk = beta * da
            dbeta = jnp.sum(dr * (value.astype(FLOAT) - eg * ks), axis=-1, keepdims=True) + jnp.sum(
                da * inner, axis=-1, keepdims=True
            )
            dqkh = dqk.astype(HALF)
            dkkh = dkk.astype(HALF)
            dquery = eg * both[:CH] + mm(dqkh, key)
            dkey = (
                ed * dkeep
                - (beta * eg) * both[CH:]
                + mm(dqkh, query, TN)
                + mm(dkkh, key)
                + mm(dkkh, key, TN)
            )
            if c > 0:
                grads[h] = jnp.exp(last) * grads[h] - mm(ns[at], grad, TN) + es[at]
            dlogit = dbeta * beta * (1.0 - beta)
            dlogit_out[span, h : h + 1] = dlogit
            logit_rows[h : h + 1, HALO + c * CH : HALO + (c + 1) * CH] = jnp.broadcast_to(dlogit, (CH, DK)).T[0:1]
            extra_sum = dlogit * logit
            far_span = slice(HALO + c * CH, HALO + (c + 1) * CH)
            sums_out[far_span, :] = (gate_sums[span, :] if h == 0 else sums_out[far_span, :]) + extra_sum
            there = slice(HALO + c * CH, HALO + (c + 1) * CH)
            cq = conv_of(wide, taps, c * CH, CH, ql)
            sig = sigmoid(cq)
            dconv[there, ql] = dquery * (sig * (1.0 + cq * (1.0 - sig)))
            cv = conv_of(wide, taps, c * CH, CH, vl)
            sig = sigmoid(cv)
            dconv[there, vl] = dval * (sig * (1.0 + cv * (1.0 - sig)))
            ck = conv_of(wide, taps, c * CH, CH, kl)
            sig = sigmoid(ck)
            act = ck * sig
            unit = lax.rsqrt(jnp.sum(act * act, axis=-1, keepdims=True) + EPS_NORM)
            u = act * unit
            dact = unit * (dkey - u * jnp.sum(dkey * u, axis=-1, keepdims=True))
            dconv[there, kl] = dact * (sig * (1.0 + ck * (1.0 - sig)))
    dtaps_out[4:8, :] = jnp.zeros((4, width), FLOAT)
    rowsum[...] = jnp.zeros((HALO + tokens, 1), FLOAT)
    for at in range(0, width, DK):
        lanes = slice(at, at + DK)
        for j in range(4):
            dtaps_out[j : j + 1, lanes] = jnp.sum(
                dconv[HALO : HALO + tokens, lanes] * wide[HALO - 3 + j : HALO - 3 + j + tokens, lanes], axis=0, keepdims=True
            )
        total = dconv[3 : 3 + HALO + tokens, lanes] * taps[0:1, lanes]
        for j in range(1, 4):
            total = total + dconv[3 - j : 3 - j + HALO + tokens, lanes] * taps[j : j + 1, lanes]
        small = total.astype(HALF)
        dproj_out[:, lanes] = small
        rowsum[...] += jnp.sum(small.astype(FLOAT) * wide[:, lanes], axis=-1, keepdims=True)
    sums_out[HALO:, :] += rowsum[HALO:, :]
    sums_out[:HALO, :] = rowsum[:HALO, :]


def out(shape, dtype):
    return jax.ShapeDtypeStruct(shape, dtype)


def cost(micros):
    return pl.CostEstimate(flops=int(micros * 1.1e7), bytes_accessed=0, transcendentals=0)


def run(kernel, shapes, args, scratch=(), scalars=0, after=(), micros=1.0, megs=12, kept=()):
    vmem = pl.BlockSpec(memory_space=pltpu.VMEM)
    smem = pl.BlockSpec(memory_space=pltpu.SMEM)
    count = len(args)

    def body(*refs):
        kernel(*refs[:count], *refs[count + len(after) :])

    return pl.pallas_call(
        body,
        out_shape=tuple(pltpu.HBM(a.shape, a.dtype) if i in kept else a for i, a in enumerate(shapes)),
        in_specs=[smem] * scalars + [vmem] * (count - scalars) + [pl.BlockSpec(memory_space=pl.ANY)] * len(after),
        out_specs=[pl.BlockSpec() if i in kept else vmem for i in range(len(shapes))],
        scratch_shapes=list(scratch),
        compiler_params=pltpu.CompilerParams(vmem_limit_bytes=megs * 2**20),
        cost_estimate=cost(micros),
    )(*args, *after)


def passed(arrays, after):
    count = len(arrays)
    anywhere = pl.BlockSpec(memory_space=pl.ANY)

    def body(*refs):
        token = refs[-1]
        token[...] = jnp.zeros(token.shape, FLOAT)

    *same, token = pl.pallas_call(
        body,
        out_shape=tuple(out(a.shape, a.dtype) for a in arrays) + (out((8, DK), FLOAT),),
        in_specs=[anywhere] * (count + len(after)),
        out_specs=[anywhere] * count + [pl.BlockSpec(memory_space=pltpu.VMEM)],
        input_output_aliases={i: i for i in range(count)},
        compiler_params=pltpu.CompilerParams(vmem_limit_bytes=2**20),
        cost_estimate=cost(0.1),
    )(*arrays, *after)
    return same, token


def prepare_shapes(heads, chunks):
    tokens, pairs = chunks * CH, heads * chunks
    return (
        out((tokens, heads * DK), HALF),
        out((tokens, heads * DK), HALF),
        out((tokens, heads * DV), HALF),
        out((pairs, CH, CH), HALF),
        out((pairs, DK, DK), HALF),
        out((pairs, DK, DV), FLOAT),
        out((pairs, CH, DK), HALF),
        out((pairs, CH, DV), HALF),
        out((pairs, CH, CH), HALF),
        out((heads, DK + 16, DK + DV), HALF),
    )


def mix_shapes(heads, chunks):
    tokens, pairs = chunks * CH, heads * chunks
    return (
        out((pairs, DK, DV), HALF),
        out((pairs, CH, DV), HALF),
        out((tokens, heads * DV), FLOAT),
        out((tokens, heads * DV), HALF),
        out((4, heads, DK + 16, DK + DV), HALF),
    )


def gate_back_shapes(heads, chunks):
    tokens, pairs = chunks * CH, heads * chunks
    return (
        out((tokens, heads * DV), HALF),
        out((pairs, CH, DV), FLOAT),
        out((pairs, DK, DV), FLOAT),
        out((tokens, heads * DV), HALF),
        out((1, heads * DV), FLOAT),
        out((tokens, 1), FLOAT),
        out((heads, DK, DV), HALF),
    )


def back_shapes(heads, chunks):
    tokens = chunks * CH
    width = heads * (2 * DK + DV)
    return (
        out((HALO + tokens, width), HALF),
        out((tokens, heads), FLOAT),
        out((HALO, HALO + tokens), FLOAT),
        out((8, width), FLOAT),
        out((HALO + tokens, 1), FLOAT),
    )


def back_scratch(heads, chunks):
    tokens = chunks * CH
    width = heads * (2 * DK + DV)
    return (pltpu.VMEM((HALO + tokens, width), FLOAT), pltpu.VMEM((HALO + tokens + 8, width), FLOAT), pltpu.VMEM((4, heads, DK, DV), HALF), pltpu.VMEM((HALO + tokens, 1), FLOAT))


def group_shapes(heads):
    pay = (heads, DK + 16, DK + DV)
    return (out((heads, DK, DK + DV), FLOAT), out(pay, HALF), out((4, *pay), HALF))


def group_back_shapes(heads):
    return (
        out((heads, DK, DK + DV), FLOAT),
        out((heads, DK, DV), HALF),
        out((4, heads, DK, DV), HALF),
    )


HEAD = ("x", "c")
SEQ = ("y", "z")
PLANE = ("y", "z", "c")
HALO = 16
EXTRA = 64
TURNS = (0, 1, -1, 2)


def rotated(array, axis, distance):
    size = lax.axis_size(axis)
    return lax.ppermute(array, axis, [(i, (i + distance) % size) for i in range(size)])


def ring_pieces(array, axis):
    return [array] + [rotated(array, axis, -d) for d in TURNS[1:]]


def join_kernel(mine, *refs):
    for k in range(4):
        refs[4][ring_place(mine[0], k)] = refs[k][...]


def head_gather(array, mine, after=()):
    shapes = (out((4, *array.shape), array.dtype),)
    own = run(join_kernel, shapes, (mine, *ring_pieces(array, "x")), scalars=1, after=after)[0]
    return own, rotated(own, "c", 1)


def head_tiles(mine, own, other):
    core = mine[1]
    return [(2 * x + which, ref, x) for which, ref in ((core, own), (1 - core, other)) for x in range(4)]


def turned(array, first, distance):
    pairs = []
    for y in range(4):
        for z in range(4):
            for core in range(2):
                along_z = (core == 0) == first
                to = (y, (z + distance) % 4) if along_z else ((y + distance) % 4, z)
                pairs.append(((y * 4 + z) * 2 + core, (to[0] * 4 + to[1]) * 2 + core))
    return lax.ppermute(array, PLANE, pairs)


def ring_place(mine, k):
    return lax.rem(mine + TURNS[k] + 4, 4)


def lane_block(at, width):
    return pl.ds(pl.multiple_of(at * width, width), width)


def setup_kernel(query, key, value, gate, decay, in_out, gate_out, gcol, grow, token):
    at = 0
    for weight in (query, key, value):
        count = weight.shape[1]
        in_out[at : at + count, :] = weight[...].T
        at += count
    gate_out[...] = gate[...].T
    rows, cols = square_masks()
    heads, tokens = decay.shape
    chunks = tokens // CH
    for h in range(heads):
        for c in range(chunks):
            span = slice(c * CH, (c + 1) * CH)
            flat = jnp.broadcast_to(decay[h : h + 1, span], (CH, CH))
            grow[h * chunks + c : h * chunks + c + 1, :] = jnp.sum(
                jnp.where(rows <= cols, flat.T, 0.0), axis=0, keepdims=True
            )
            gcol[span, h : h + 1] = jnp.sum(jnp.where(cols <= rows, flat, 0.0), axis=1, keepdims=True)
    token[...] = jnp.zeros(token.shape, FLOAT)


def first_norm_kernel(mine, gain, beta_rows, cot, own, other, normed, factor, rows_out, logits, cot_out, halo_out):
    width = own.shape[2]
    rows = rows_out.shape[0]
    own_rows = lane_block(mine[0] * 2 + mine[1], rows)
    square = 0.0
    for _, ref, x in head_tiles(mine, own, other):
        wide = ref[x].astype(FLOAT)
        square = square + jnp.sum(wide * wide, axis=-1, keepdims=True)
    scale = lax.rsqrt(square / (8 * width) + EPS_NORM)
    factor[...] = scale
    total = 0.0
    for head, ref, x in head_tiles(mine, own, other):
        lanes = lane_block(head, width)
        small = (ref[x].astype(FLOAT) * scale * gain[:, lanes]).astype(HALF)
        normed[:, lanes] = small
        total = total + mm(small, beta_rows[:, lanes], NT)
        rows_out[:, lanes] = ref[x, own_rows, :].astype(FLOAT)
    logits[...] = total
    cot_out[...] = cot[...]
    halo_out[...] = normed[normed.shape[0] - HALO :, :]


def product_grad_kernel(mine, own, other, weight, whole, rows_out, grad, token):
    width = own.shape[2]
    rows = rows_out.shape[0]
    own_rows = lane_block(mine[0] * 2 + mine[1], rows)
    for head, ref, x in head_tiles(mine, own, other):
        lanes = lane_block(head, width)
        whole[:, lanes] = ref[x]
        rows_out[:, lanes] = ref[x, own_rows, :]
    grad[...] = mm(weight[...], whole[...], NT)
    token[...] = jnp.zeros(token.shape, FLOAT)


def hidden_kernel(rows_in, gain, first, second, third, fourth, hidden, unit, factor, normed):
    total = rows_in[...] + first[...] + second[...].astype(FLOAT) + third[...].astype(FLOAT) + fourth[...].astype(FLOAT)
    hidden[...] = total
    scale = lax.rsqrt(jnp.mean(total * total, axis=-1, keepdims=True) + EPS_NORM)
    factor[...] = scale
    unit[...] = total * scale
    normed[...] = (total * scale * gain[...]).astype(HALF)


def second_back_kernel(unit, factor, gain, cot_rows, first, second, third, fourth, d_hidden, gain_part, token):
    token[...] = jnp.zeros(token.shape, FLOAT)
    total = first[...] + second[...].astype(FLOAT) + third[...].astype(FLOAT) + fourth[...].astype(FLOAT)
    n = unit[...]
    gain_part[...] = jnp.sum(total * n, axis=0, keepdims=True)
    e = total * gain[...]
    mean = jnp.mean(e * n, axis=-1, keepdims=True)
    d_hidden[...] = (cot_rows[...].astype(FLOAT) + factor[...] * (e - n * mean)).astype(HALF)


def ffn_kernel(mine, own_in, other_in, gate_rows, up_rows, d_product, normed, product, d_gate, d_up, other, own, token, total):
    rows = own_in.shape[1]
    for head, ref, x in head_tiles(mine, own_in, other_in):
        normed[lane_block(head, rows), :] = ref[x]
    cols = gate_rows.shape[0]
    step = cols // 2
    for at in range(0, cols, step):
        span = slice(at, at + step)
        gate = mm(gate_rows[span, :], normed[...], NT)
        up = mm(up_rows[span, :], normed[...], NT)
        sig = sigmoid(gate)
        act = gate * sig
        product[span, :] = (act * up).astype(HALF)
        grad = d_product[span, :]
        dg = (grad * up * (sig * (1.0 + gate * (1.0 - sig)))).astype(HALF)
        du = (grad * act).astype(HALF)
        d_gate[span, :] = dg
        d_up[span, :] = du
    token[...] = jnp.zeros(token.shape, FLOAT)
    gate_turned = d_gate[...].T
    up_turned = d_up[...].T
    width = normed.shape[1]
    tile = width // 4
    core = mine[1]
    for at in range(0, width, tile):
        lanes = slice(at, at + tile)
        total[...] = mm(gate_turned, gate_rows[:, lanes]) + mm(up_turned, up_rows[:, lanes])
        spread_rows(core, total, own, other, rows, lanes)


def join_rows_kernel(mine, own, other, whole, own_cols):
    rows = own.shape[1]
    lanes = lane_block(mine[0] * 2 + mine[1], own_cols.shape[1])
    for head, ref, x in head_tiles(mine, own, other):
        whole[lane_block(head, rows), :] = ref[x]
        own_cols[lane_block(head, rows), :] = ref[x, :, lanes]


def split_sum_kernel(mine, own, arrived, *outs):
    for k in range(4):
        at = ring_place(mine[0], k)
        outs[k][...] = (own[at].astype(FLOAT) + arrived[at].astype(FLOAT)).astype(outs[k].dtype)
    outs[4][...] = jnp.zeros(outs[4].shape, FLOAT)


def tile_sum_kernel(own, arrived, total):
    total[...] = (own[...].astype(FLOAT) + arrived[...].astype(FLOAT)).astype(HALF)


def head_scatter(own, other, mine, with_token=False, after=()):
    arrived = rotated(other, "c", 1)
    shape = own.shape[1:]
    shapes = (out(shape, FLOAT),) + (out(shape, HALF),) * 3 + (out((8, DK), FLOAT),)
    total, *sent, token = run(split_sum_kernel, shapes, (mine, own, arrived), scalars=1, after=after)
    parts = [total] + [rotated(part, "x", d) for d, part in zip(TURNS[1:], sent)]
    return (parts, token) if with_token else parts


def added(parts):
    total = parts[0]
    for part in parts[1:]:
        total = total + part.astype(FLOAT)
    return total


def dest_block(mine, k, o):
    core = mine[1]
    place = ring_place(jnp.where(core == 0, mine[3], mine[2]), k)
    return jnp.where(core == 0, o * 4 + place, place * 4 + o)


def store_tile(outs, k, o, early, value):
    count = early.shape[0]
    if k < 3:
        outs[k][o, :count, :] = early
        outs[k][o, count:, :] = value
    else:
        spare = outs[3].shape[1] - count
        outs[3][o, :count, :] = early
        outs[3][o, count:, :] = value[:spare]
        outs[4][o] = value[spare:]


def mixer_grad_kernel(mine, d_branch, gated, normed, d_pre, gate_rows, *refs):
    outs, (gain_out, gated_turned, pre_turned) = refs[:4], refs[4:]
    gated_turned[...] = gated[...].T
    pre_turned[...] = d_pre[...].T
    for k in range(4):
        for o in (0, 2):
            blocks = [lane_block(dest_block(mine, k, o + i), DK) for i in range(2)]
            mixer = mm(gated_turned[...], jnp.concatenate([d_branch[:, at] for at in blocks], axis=1))
            gate = mm(pre_turned[...], jnp.concatenate([normed[:, at] for at in blocks], axis=1))
            for i, at in enumerate(blocks):
                half = slice(i * DK, (i + 1) * DK)
                outs[k][o + i] = jnp.concatenate([mixer[:, half], gate[:, half]], axis=0).astype(HALF)
                gain_out[:, at] = jnp.sum(gate[:, half] * gate_rows[:, at].astype(FLOAT), axis=0, keepdims=True)


def in_grad_kernel(mine, normed, halo, dproj, d_logit, taps, mixer_gain, gate_gain, second_gain, first_gain, in_rows, beta_rows, *refs):
    early, outs, (token, turned_refs, extra) = refs[:4], refs[4:9], refs[9:]
    token[...] = jnp.zeros(token.shape, FLOAT)
    cols = dproj.shape[1]
    heads = 2
    turned_refs[:cols, :] = dproj[...].T
    turned_refs[cols:, :] = d_logit[...].astype(HALF)
    extra[...] = jnp.zeros(extra.shape, FLOAT)
    per_tap = cols // DK
    for j in range(4):
        for i in range(per_tap):
            extra[j * per_tap + i : j * per_tap + i + 1, :] = taps[j : j + 1, i * DK : (i + 1) * DK]
    for i in range(mixer_gain.shape[1] // DK):
        extra[32 + i : 33 + i, :] = mixer_gain[:, i * DK : (i + 1) * DK]
    for k in range(4):
        for o in (0, 2):
            blocks = [lane_block(dest_block(mine, k, o + i), DK) for i in range(2)]
            left = jnp.concatenate(
                [jnp.concatenate([halo[:, at], normed[:, at]], axis=0) for at in blocks], axis=1
            )
            grads = mm(turned_refs[...], left)
            for i, at in enumerate(blocks):
                half = slice(i * DK, (i + 1) * DK)
                beta = grads[cols : cols + heads, half]
                gain = (
                    jnp.sum(grads[:cols, half] * in_rows[:, at].astype(FLOAT), axis=0, keepdims=True)
                    + jnp.sum(beta * beta_rows[:heads, at].astype(FLOAT), axis=0, keepdims=True)
                    + gate_gain[:, at]
                )
                extra[36 : 36 + heads, :] = beta
                extra[40:41, :] = gain / first_gain[:, at]
                extra[41:42, :] = second_gain[:, at]
                store_tile(
                    outs, k, o + i, early[k][o + i], jnp.concatenate([grads[:cols, half], extra[...]], axis=0).astype(HALF)
                )


def ffn_grad_kernel(turns, mine, cot, normed, d_gate, d_up, product, *refs):
    outs, token = refs[:-1], refs[-1]
    token[...] = jnp.zeros(token.shape, FLOAT)
    cols = d_gate.shape[0]
    half_rows = 3 * cols // 2
    for k in turns:
        for o in (0, 2):
            blocks = [lane_block(dest_block(mine, k, o + i), DK) for i in range(2)]
            lefts = [jnp.concatenate([ref[:, at] for at in blocks], axis=1) for ref in (normed, cot)]
            for n, (right, left) in enumerate(((d_gate, lefts[0]), (d_up, lefts[0]), (product, lefts[1]))):
                both = mm(right[...], left).astype(HALF)
                for i in range(2):
                    tile = both[:, i * DK : (i + 1) * DK]
                    first = n * cols
                    if k < 3:
                        outs[turns.index(k)][o + i, first : first + cols, :] = tile
                    elif first + cols <= half_rows:
                        outs[0][o + i, first : first + cols, :] = tile
                    elif first >= half_rows:
                        outs[1][o + i, first - half_rows : first - half_rows + cols, :] = tile
                    else:
                        outs[0][o + i, first:, :] = tile[: half_rows - first]
                        outs[1][o + i, : first + cols - half_rows, :] = tile[half_rows - first :]


def ffn_grads(turns, mine, cot, normed, d_gate, d_up, product, after):
    rows = 3 * d_gate.shape[0]
    if turns == (3,):
        shapes = (out((4, rows // 2, DK), HALF),) * 2
    else:
        shapes = (out((4, rows, DK), HALF),) * len(turns)
    return run(
        partial(ffn_grad_kernel, turns),
        shapes + (out((8, DK), FLOAT),),
        (mine, cot, normed, d_gate, d_up, product),
        scalars=1,
        after=(after,),
    )


def gain_rows(ref):
    first = ref.shape[1] - EXTRA + 40
    return ref[:, first : first + 8, :].astype(FLOAT)


def last_relay_kernel(own, plus, minus, first, second, plus_out, minus_out, token, rows):
    relay_kernel(plus, minus, first, second, plus_out, minus_out, token)
    for i, ref in enumerate((own, plus_out, minus_out)):
        rows[i] = gain_rows(ref)


def quad_sum_kernel(tiles, own, plus, minus):
    for i, target in enumerate((own, plus, minus)):
        target[...] = (tiles[0, i] + tiles[1, i]) + (tiles[2, i] + tiles[3, i])


def gains_over_chips(rows):
    tiles = lax.all_to_all(jnp.broadcast_to(rows[None], (4, *rows.shape)), "x", 0, 0, tiled=True)
    own, plus, minus = run(quad_sum_kernel, (out((4, 8, DK), FLOAT),) * 3, (tiles,))
    return own, turned(plus, True, 1), turned(minus, True, -1)


def relay_kernel(plus, minus, first, second, plus_out, minus_out, token):
    half = first.shape[1]
    plus_out[:, :half, :] = (plus[:, :half, :].astype(FLOAT) + first[...].astype(FLOAT)).astype(HALF)
    plus_out[:, half:, :] = plus[:, half:, :]
    minus_out[:, :half, :] = minus[:, :half, :]
    minus_out[:, half:, :] = (minus[:, half:, :].astype(FLOAT) + second[...].astype(FLOAT)).astype(HALF)
    token[...] = jnp.zeros(token.shape, FLOAT)


def relayed(parts, after, micros):
    shape = out(parts[1].shape, HALF)
    first, second = turned(parts[3], True, 1), turned(parts[4], True, -1)
    plus, minus, token = run(
        relay_kernel,
        (shape, shape, out((8, DK), FLOAT)),
        (parts[1], parts[2], first, second),
        after=after,
        micros=micros,
    )
    return (parts[0], turned(plus, True, 1), turned(minus, True, -1)), token


def last_sum_kernel(mine, own, plus, minus, own_rows, plus_rows, minus_rows, *outs):
    seq_sum_kernel(0, mine, own, plus, minus, *outs)
    rank = jnp.where(mine[1] == 0, mine[2], mine[3])
    first = outs[0].shape[0] - EXTRA + 32
    for k in range(4):
        place = ring_place(rank, k)
        old = own[place, first : first + 16, :].astype(FLOAT)
        old = old + plus[place, first : first + 16, :].astype(FLOAT) + minus[place, first : first + 16, :].astype(FLOAT)
        new = own_rows[place] + plus_rows[place] + minus_rows[place]
        outs[k][first : first + 16, :] = jnp.concatenate([old[:8], new], axis=0).astype(outs[k].dtype)


def seq_sum_kernel(early, mine, *refs):
    rank = jnp.where(mine[1] == 0, mine[2], mine[3])
    group, before = refs[:3], refs[3 : 3 + 4 * early]
    outs = refs[3 + 4 * early : 7 + 4 * early]
    refs[-1][...] = jnp.zeros(refs[-1].shape, FLOAT)
    for k in range(4):
        place = ring_place(rank, k)
        at = 0
        for i in range(early):
            source = before[4 * i + k]
            outs[k][at : at + source.shape[0], :] = source[...]
            at += source.shape[0]
        total = group[0][place].astype(FLOAT) + group[1][place].astype(FLOAT) + group[2][place].astype(FLOAT)
        outs[k][at:, :] = total.astype(outs[k].dtype)


def seq_sums(group, before, mine, after, micros):
    count = group[0].shape[1] + sum(sums[0].shape[0] for sums in before)
    shapes = (out((count, DK), FLOAT),) + (out((count, DK), HALF),) * 3
    shapes += (out((8, DK), FLOAT),)
    flat = [piece for sums in before for piece in sums]
    return run(
        partial(seq_sum_kernel, len(before)), shapes, (mine, *group, *flat), scalars=1, after=after, micros=micros
    )


def second_round(sums):
    return [sums[0]] + [turned(sums[i], False, TURNS[i]) for i in range(1, 4)]


def unpack_kernel(own, first, second, third, *outs):
    total = own[...] + first[...].astype(FLOAT) + second[...].astype(FLOAT) + third[...].astype(FLOAT)
    at = 0
    for target in outs[:5]:
        count = target.shape[1]
        target[...] = total[at : at + count, :].T
        at += count
    extra = total[at:, :]
    per_tap = 8
    first = 0
    for target in outs[5:8]:
        blocks = target.shape[1] // DK
        for j in range(4):
            for i in range(blocks):
                row = j * per_tap + first + i
                target[j : j + 1, i * DK : (i + 1) * DK] = extra[row : row + 1, :]
        first += blocks
    for i in range(outs[8].shape[1] // DK):
        outs[8][:, i * DK : (i + 1) * DK] = extra[32 + i : 33 + i, :]
    outs[9][...] = extra[36:38, :]
    outs[10][...] = extra[40:48, :]


def ffn_unpack_kernel(own, first, second, third, gate, up, down, token):
    cols = gate.shape[0]
    token[...] = jnp.zeros(token.shape, FLOAT)
    for n, target in enumerate((gate, up, down)):
        span = slice(n * cols, (n + 1) * cols)
        target[...] = (
            own[span, :]
            + first[span, :].astype(FLOAT)
            + second[span, :].astype(FLOAT)
            + third[span, :].astype(FLOAT)
        )


def output_kernel(own, first, second, third, total, token):
    token[...] = jnp.zeros(token.shape, FLOAT)
    total[...] = (
        own[...] + first[...].astype(FLOAT) + second[...].astype(FLOAT) + third[...].astype(FLOAT)
    ).astype(HALF)


def tile_of(i, mine):
    return (i % 4) * 2 + jnp.where(i < 4, 1 - mine[1], mine[1])


def whole_block(shape):
    return pl.BlockSpec(shape, lambda i, mine: (0,) * len(shape))


def tile_outs(rows, width):
    return [
        pl.BlockSpec((1, rows, width), lambda i, mine: (jnp.minimum(i, 3), 0, 0)),
        pl.BlockSpec((1, rows, width), lambda i, mine: (jnp.maximum(i - 4, 0), 0, 0)),
    ]


def down_kernel(mine, product, weight, hidden, other, own, token, scratch):
    step = pl.program_id(0)
    rows = hidden.shape[0]

    @pl.when(step == 0)
    def _():
        scratch[...] = product[...].T

    part = mm(scratch[...], weight[...])
    here = lane_block(mine[0] * 2 + mine[1], rows)
    for target, wanted in ((other, step < 4), (own, step >= 4)):

        @pl.when(wanted)
        def _():
            target[0] = part.astype(HALF)
            target[0, here, :] = (target[0, here, :].astype(FLOAT) + hidden[...]).astype(HALF)

    token[...] = jnp.zeros(token.shape, FLOAT)


def down_tiles(mine, product, weight, hidden):
    cols, tokens = product.shape
    width = weight.shape[1] // 8
    spec = pltpu.PrefetchScalarGridSpec(
        num_scalar_prefetch=1,
        grid=(8,),
        in_specs=[
            whole_block(product.shape),
            pl.BlockSpec((cols, width), lambda i, mine: (0, tile_of(i, mine))),
            pl.BlockSpec((hidden.shape[0], width), lambda i, mine: (0, tile_of(i, mine))),
        ],
        out_specs=tile_outs(tokens, width) + [whole_block((8, DK))],
        scratch_shapes=[pltpu.VMEM((tokens, cols), HALF)],
    )
    tiles = out((4, tokens, width), HALF)
    return pl.pallas_call(
        down_kernel,
        grid_spec=spec,
        out_shape=(tiles, tiles, out((8, DK), FLOAT)),
        compiler_params=pltpu.CompilerParams(vmem_limit_bytes=16 * 2**20),
        cost_estimate=cost(4.0),
    )(mine, product, weight, hidden)


def d_first_kernel(mine, dproj, d_pre, d_logit, sums, in_rows, gate_rows, beta_rows, after, other, own, token, sum_rows):
    step = pl.program_id(0)
    tokens = d_pre.shape[0]
    width = own.shape[2]

    @pl.when(step == 0)
    def _():
        row = jnp.broadcast_to(sums[HALO:, :], (tokens, DK)).T
        sum_rows[...] = jnp.zeros(sum_rows.shape, FLOAT)
        for i in range(tokens // width):
            sum_rows[i : i + 1, :] = row[0:1, i * width : (i + 1) * width]
        sum_rows[2:3, 0:HALO] = jnp.broadcast_to(sums[:HALO, :], (HALO, DK)).T[0:1, :]

    part = mm(dproj[...], in_rows[...])
    late = mm(d_pre[...], gate_rows[...])
    for h in range(2):
        late = late + d_logit[:, h : h + 1] * beta_rows[h : h + 1, :].astype(FLOAT)
    for target, wanted in ((other, step < 4), (own, step >= 4)):

        @pl.when(wanted)
        def _():
            target[0, :HALO, :] = part[:HALO].astype(HALF)
            target[0, HALO : HALO + tokens, :] = (part[HALO:] + late).astype(HALF)
            target[0, HALO + tokens :, :] = sum_rows[...].astype(HALF)

    token[...] = jnp.zeros(token.shape, FLOAT)


def d_first_tiles(mine, dproj, d_pre, d_logit, sums, in_rows, gate_rows, beta_rows, after):
    tokens = d_pre.shape[0]
    width = in_rows.shape[1] // 8
    count = tokens + 2 * HALO

    def tile(rows):
        return pl.BlockSpec((rows, width), lambda i, mine: (0, tile_of(i, mine)))

    spec = pltpu.PrefetchScalarGridSpec(
        num_scalar_prefetch=1,
        grid=(8,),
        in_specs=[whole_block(a.shape) for a in (dproj, d_pre, d_logit, sums)]
        + [tile(in_rows.shape[0]), tile(gate_rows.shape[0]), tile(beta_rows.shape[0])]
        + [pl.BlockSpec(memory_space=pl.ANY)],
        out_specs=tile_outs(count, width) + [whole_block((8, DK))],
        scratch_shapes=[pltpu.VMEM((HALO, width), FLOAT)],
    )
    tiles = out((4, count, width), HALF)
    return pl.pallas_call(
        d_first_kernel,
        grid_spec=spec,
        out_shape=(tiles, tiles, out((8, DK), FLOAT)),
        compiler_params=pltpu.CompilerParams(vmem_limit_bytes=16 * 2**20),
        cost_estimate=cost(6.0),
    )(mine, dproj, d_pre, d_logit, sums, in_rows, gate_rows, beta_rows, after)


def first_total_kernel(tiles, total, pack):
    whole = sum(tiles[x].astype(FLOAT) for x in range(4))
    total[...] = whole
    pack[:HALO, :] = whole[:HALO]
    at = whole.shape[0] - HALO
    pack[HALO:, :] = whole[at : at + 8]


def input_grad_kernel(mine, total, arrived, block_input, factor, gain, d_branch, grad):
    tokens, width = block_input.shape
    columns = []
    for i in range(tokens // width):
        row = total[HALO + tokens + i : HALO + tokens + i + 1, :]
        columns.append(jnp.broadcast_to(row, (DK, width)).T[:, 0:1])
    late_row = jnp.broadcast_to(arrived[HALO + 2 : HALO + 3, :], (DK, width)).T[:HALO, 0:1]
    mean = jnp.concatenate(columns, axis=0) / (8 * width)
    scale = factor[...]
    unit = block_input[...].astype(FLOAT) * scale
    gain_own = gain[:, lane_block(mine[0] * 2 + mine[1], width)]
    grad[...] = d_branch[...].astype(FLOAT) + scale * (total[HALO : HALO + tokens, :] * gain_own - unit * mean)
    last = slice(tokens - HALO, tokens)
    grad[last, :] += scale[last] * (arrived[:HALO, :] * gain_own - unit[last] * (late_row / (8 * width)))


def next_block(array, distance):
    size = 16
    route = [(i, i + distance) for i in range(size) if 0 <= i + distance < size]
    return lax.ppermute(array, SEQ, route)


def dot_nt(a, b):
    return lax.dot_general(a, b, NT, preferred_element_type=FLOAT)


def shards(
    block_input,
    log_decay,
    first_gain,
    query_weight,
    key_weight,
    value_weight,
    gate_weight,
    beta_weight,
    query_conv,
    key_conv,
    value_conv,
    mixer_gain,
    mixer_weight,
    second_gain,
    swiglu_gate,
    swiglu_up,
    swiglu_down,
    cotangent,
):
    heads = log_decay.shape[1]
    tokens, width = block_input.shape
    model = 8 * width
    chunks = tokens // CH
    rows = tokens // 8
    kq, vd = heads * DK, heads * DV
    cols = 2 * kq + vd
    hidden_cols = swiglu_gate.shape[1]
    mine = jnp.stack([lax.axis_index(name) for name in ("x", "c", "y", "z")]).astype(jnp.int32)

    token_out = out((8, DK), FLOAT)
    in_rows, gate_rows, gcol, grow, token = run(
        setup_kernel,
        (
            out((cols, model), HALF),
            out((vd, model), HALF),
            out((tokens, heads), FLOAT),
            out((heads * chunks, CH), FLOAT),
            token_out,
        ),
        (query_weight, key_weight, value_weight, gate_weight, log_decay.T),
        micros=3.0,
    )
    beta_rows = jnp.pad(beta_weight.T, ((0, HALO - heads), (0, 0)))
    taps = jnp.concatenate([query_conv.T, key_conv.T, value_conv.T], axis=1)
    gain_row = mixer_gain.reshape(1, -1)
    first_row = first_gain.reshape(1, -1)

    first_normed, first_factor, my_rows, logits, cot, halo_rows = run(
        first_norm_kernel,
        (
            out((tokens, model), HALF),
            out((tokens, 1), FLOAT),
            out((rows, model), FLOAT),
            out((tokens, HALO), FLOAT),
            out((tokens, width), HALF),
            out((HALO, model), HALF),
        ),
        (mine, first_row, beta_rows, cotangent, *head_gather(block_input, mine, (token,))),
        scalars=1,
        micros=3.0,
    )
    halo_normed = next_block(halo_rows, 1)
    proj = dot_nt(first_normed, in_rows).astype(HALF)
    halo_proj = dot_nt(halo_normed, in_rows).astype(HALF)
    gate_pre = dot_nt(first_normed, gate_rows)
    q, k, v, tri, n, b, w, u, p, pay, pay_token = run(
        partial(prepare_kernel, heads, chunks),
        prepare_shapes(heads, chunks) + (token_out,),
        (proj, halo_proj, taps, logits, gcol, grow),
        [pltpu.VMEM((HALO + tokens, cols), FLOAT)],
        micros=8.0,
        kept=range(9),
        megs=20,
    )
    near_pieces = ring_pieces(pay, "z")
    cot_tiles = head_gather(cot, mine, (pay_token,))
    whole_cot, cot_rows, d_product, token = run(
        product_grad_kernel,
        (out((tokens, model), HALF), out((rows, model), HALF), out((hidden_cols, tokens), FLOAT), token_out),
        (mine, *cot_tiles, swiglu_down.T),
        scalars=1,
        micros=4.0,
    )
    before, group, near = run(
        partial(group_kernel, heads), group_shapes(heads), (mine, *near_pieces), scalars=1, after=(gate_pre[:8, :DK],), micros=2.0
    )
    half_tiles = out((4, rows, model), HALF)
    states, vns, mixed, gated, branch_other, branch_own, far = run(
        partial(mix_kernel, heads, chunks),
        mix_shapes(heads, chunks)[:4] + (half_tiles, half_tiles) + mix_shapes(heads, chunks)[4:],
        (mine, *ring_pieces(group, "y"), before, q, k, w, u, p, n, b, gcol, gate_pre, gain_row, mixer_weight),
        [pltpu.VMEM((tokens, model // 4), FLOAT)],
        scalars=1,
        after=(token,),
        kept=(0, 1, 2, 6),
        megs=16,
        micros=4.0,
    )
    branch = head_scatter(branch_own, branch_other, mine)
    wide_rows = out((rows, model), FLOAT)
    second_row = second_gain.reshape(1, -1)
    hidden, second_unit, second_factor, own_normed = run(
        hidden_kernel,
        (wide_rows, wide_rows, out((rows, 1), FLOAT), out((rows, model), HALF)),
        (my_rows, second_row, *branch),
    )
    turned_out = out((hidden_cols, tokens), HALF)
    second_normed, product, d_gate, d_up, second_other, second_own, ffn_token = run(
        ffn_kernel,
        (out((tokens, model), HALF), turned_out, turned_out, turned_out, half_tiles, half_tiles, token_out),
        (
            mine,
            *head_gather(own_normed, mine),
            swiglu_gate.T,
            swiglu_up.T,
            d_product,
        ),
        [pltpu.VMEM((tokens, model // 4), FLOAT)],
        scalars=1,
        micros=9.0,
        megs=20,
    )
    second_parts, token = head_scatter(second_own, second_other, mine, True)
    grad_args = (mine, whole_cot, second_normed, d_gate, d_up, product)
    *ffn_ends, token = ffn_grads((3,), *grad_args, token)
    ffn_plus, ffn_minus, token = ffn_grads((1, 2), *grad_args, token)
    d_hidden, second_gain_part, back_token = run(
        second_back_kernel,
        (out((rows, model), HALF), out((1, model), FLOAT), token_out),
        (second_unit, second_factor, second_row, cot_rows, *second_parts),
        after=(token,),
    )
    ffn_group, ffn_token = relayed([None, ffn_plus, ffn_minus, *ffn_ends], (back_token,), 3.0)
    down_other, down_own, down_token = down_tiles(mine, product, swiglu_down.T, hidden)
    d_branch, d_branch_own = run(
        join_rows_kernel,
        (out((tokens, model), HALF), out((tokens, width), HALF)),
        (mine, *head_gather(d_hidden, mine, (down_token, ffn_token))),
        scalars=1,
    )
    d_gated = jnp.dot(d_branch, mixer_weight, preferred_element_type=FLOAT)
    dos, dvns, es, d_gate_pre, gain_part, gate_sums, ends = run(
        partial(gate_back_kernel, heads, chunks),
        gate_back_shapes(heads, chunks),
        (d_gated, mixed, gate_pre, gain_row, q, w, p, n, gcol),
        micros=4.0,
    )
    ffn_own, token = ffn_grads((0,), *grad_args, gate_sums[:8])
    *ffn_sums, ffn_token = seq_sums((ffn_own, *ffn_group[1:]), (), mine, (), 3.0)
    tile = out((4, 2 * vd, DK), HALF)
    *mixer_parts, gate_gain = run(
        mixer_grad_kernel,
        (tile,) * 4 + (out((1, model), FLOAT),),
        (mine, d_branch, gated, first_normed, d_gate_pre, gate_rows),
        [pltpu.VMEM((vd, tokens), HALF), pltpu.VMEM((vd, tokens), HALF)],
        scalars=1,
        micros=5.0,
    )
    after, group_end, _, group_token = run(
        partial(group_back_kernel, heads),
        group_back_shapes(heads) + (token_out,),
        (mine, near, *ring_pieces(ends, "z")),
        scalars=1,
        after=(gate_gain, ffn_token),
        micros=2.0,
    )
    end_pieces = ring_pieces(group_end, "y")
    passed_sums, ffn_token = passed(ffn_sums, tuple(end_pieces[1:]))
    dproj, d_logit, logit_rows, taps_part, sums = run(
        partial(back_kernel, heads, chunks),
        back_shapes(heads, chunks),
        (mine, far, *end_pieces, after, q, k, v, logits, gate_sums, gcol, grow, tri, states, vns, dos, dvns, es, n, proj, halo_proj, taps),
        back_scratch(heads, chunks),
        scalars=1,
        after=(ffn_token,),
        micros=11.0,
        megs=30,
    )
    ffn_grad_out = out((hidden_cols, DK), FLOAT)
    grad_gate, grad_up, grad_down, ffn_token = run(
        ffn_unpack_kernel, (ffn_grad_out,) * 3 + (token_out,), second_round(passed_sums), after=(sums[:8],)
    )
    packed = 2 * vd + cols + EXTRA
    tile, half_tile = out((4, packed, DK), HALF), out((4, packed // 2, DK), HALF)
    *in_parts, in_token = run(
        in_grad_kernel,
        (tile,) * 3 + (half_tile,) * 2 + (token_out,),
        (mine, first_normed, halo_normed, dproj, logit_rows, taps_part, gain_part, gate_gain, second_gain_part, first_row, in_rows, beta_rows, *mixer_parts),
        [pltpu.VMEM((cols + HALO, HALO + tokens), HALF), pltpu.VMEM((EXTRA, DK), FLOAT)],
        scalars=1,
        after=(ffn_token,),
        micros=6.0,
        megs=16,
    )
    first_other, first_own, first_token = d_first_tiles(
        mine, dproj, d_gate_pre, d_logit, sums, in_rows, gate_rows, beta_rows, in_token
    )
    output, out_token = run(
        output_kernel,
        (out((tokens, width), HALF), token_out),
        head_scatter(down_own, down_other, mine, after=(in_token,)),
    )
    tile = out((4, packed, DK), HALF)
    plus, minus, in_token, rows_left = run(
        last_relay_kernel,
        (tile, tile, token_out, out((3, 4, 8, DK), FLOAT)),
        (*in_parts[:3], turned(in_parts[3], True, 1), turned(in_parts[4], True, -1)),
        after=(first_token, out_token),
    )
    in_group = (in_parts[0], turned(plus, True, 1), turned(minus, True, -1))
    first_sum = run(
        tile_sum_kernel,
        (out((4, tokens + 2 * HALO, width), HALF),),
        (first_own, rotated(first_other, "c", 1)),
        after=(in_token,),
    )[0]
    first_tiles = lax.all_to_all(first_sum, "x", 0, 0, tiled=True)
    total, pack = run(
        first_total_kernel,
        (out((tokens + 2 * HALO, width), FLOAT), out((HALO + 8, width), FLOAT)),
        (first_tiles,),
    )
    *sums_out, sum_token = run(
        last_sum_kernel,
        (out((packed, DK), FLOAT),) + (out((packed, DK), HALF),) * 3 + (token_out,),
        (mine, *in_group, *gains_over_chips(rows_left)),
        scalars=1,
    )
    totals = [sums_out[0]] + [turned(sums_out[i], False, TURNS[i]) for i in range(1, 4)]
    grad_mixer_weight, grad_gate_weight, grad_query, grad_key, grad_value, *taps_grad, gain_grad, beta_grad, both = run(
        unpack_kernel,
        tuple(out((DK, count), FLOAT) for count in (vd, vd, kq, kq, vd)) + tuple(out((rows_, count), FLOAT) for rows_, count in ((4, kq), (4, kq), (4, vd), (1, vd), (heads, DK), (8, DK))),
        totals,
    )
    grad_input = run(
        input_grad_kernel,
        (out((tokens, width), FLOAT),),
        (mine, total, next_block(pack, -1), block_input, first_factor, first_row, d_branch_own),
        scalars=1,
    )[0]
    both = both + rotated(both, "c", 1)
    return (
        output,
        grad_input,
        both[0],
        grad_query,
        grad_key,
        grad_value,
        grad_gate_weight,
        beta_grad.T,
        taps_grad[0].T,
        taps_grad[1].T,
        taps_grad[2].T,
        gain_grad.reshape(-1),
        grad_mixer_weight,
        both[1],
        grad_gate.T,
        grad_up.T,
        grad_down.T,
    )


def solution(mesh):
    torus = Mesh(mesh.devices.reshape(4, 4, 4, 2), SEQ + HEAD)
    in_specs = (
        P(SEQ, HEAD),
        P(SEQ, HEAD),
        P(),
        P(None, HEAD),
        P(None, HEAD),
        P(None, HEAD),
        P(None, HEAD),
        P(None, HEAD),
        P(HEAD, None),
        P(HEAD, None),
        P(HEAD, None),
        P(HEAD),
        P(None, HEAD),
        P(),
        P(None, HEAD),
        P(None, HEAD),
        P(None, HEAD),
        P(SEQ, HEAD),
    )
    out_specs = (
        P(SEQ, HEAD),
        P(SEQ, HEAD),
        P(SEQ),
        P(SEQ, HEAD),
        P(SEQ, HEAD),
        P(SEQ, HEAD),
        P(SEQ, HEAD),
        P(SEQ, HEAD),
        P(HEAD, None),
        P(HEAD, None),
        P(HEAD, None),
        P(HEAD),
        P(SEQ, HEAD),
        P(SEQ),
        P(SEQ, HEAD),
        P(SEQ, HEAD),
        P(SEQ, HEAD),
    )
    return jax.shard_map(
        shards, mesh=torus, in_specs=in_specs, out_specs=out_specs, check_vma=False
    )
```

profile of v0, /device:TPU:1, one launch (start us, length us, event | category | flops | bytes accessed | tf_op | source)
XLA Modules:
  0.0 303.6 jit_solution(6921107597772126577)
XLA Ops:
  0.7 3.7 %collective-permute-start.2 = (bf16[512,256]{1,0:T(8,128)(2,1)}, bf16[512,256]{1,0:T(8,128)(2,1)S(1)}, u32[]{:S(2)}, u32[]{:S(2)}) collective-permute-start(bf16[512,256]{1,0:T(8,128)(2,1)} %refs_3_.5), channel_id=1, source_target_pairs={{0,4},{2,6},{4,0},{6,2},{1,5},{3,7},{5,1},{7,3},{8,12},{10,14},{12... | collective-permute-start | bytes 786440 | tf_op jit(solution)/shard_map/ppermute | solution.py:510
  28.4 3.7 %collective-permute-start.4 = (bf16[16,2048]{1,0:T(8,128)(2,1)S(1)}, bf16[16,2048]{1,0:T(8,128)(2,1)S(1)}, u32[]{:S(2)}, u32[]{:S(2)}) collective-permute-start(bf16[16,2048]{1,0:T(8,128)(2,1)S(1)} %get-tuple-element.166), channel_id=1, source_target_pairs={{0,8},{8,16},{16,24},{24,32},{32,40},{40,48},{48,56},{56,64},{64,7... | collective-permute-start | bytes 196616 | tf_op jit(solution)/shard_map/ppermute | solution.py:1071
  35.8 8.9 %shard_map.308 = (bf16[512,256]{1,0:T(8,128)(2,1)}, bf16[512,256]{1,0:T(8,128)(2,1)}, bf16[512,512]{1,0:T(8,128)(2,1)}, bf16[8,128,128]{2,1,0:T(8,128)(2,1)}, bf...) custom-call(bf16[512,1024]{1,0:T(8,128)(2,1)S(1)} %convolution_conve, ...), custom_call_target="tpu_custom_call" | custom-call | flops 88000000 | tf_op jit(solution)/shard_map/pallas_call | solution.py:398
  46.9 3.3 %collective-permute-start.7 = (bf16[2,144,384]{2,1,0:T(8,128)(2,1)S(1)}, bf16[2,144,384]{2,1,0:T(8,128)(2,1)S(1)}, u32[]{:S(2)}, u32[]{:S(2)}) collective-permute-start(bf16[2,144,384]{2,1,0:T(8,128)(2,1)S(1)} %get-tuple-element.170.refs_1_), channel_id=1, source_target_pairs={{0,16},{8,24},{16,0},{24,8},{1,17},{9,25},{17,1},{25,9},{2,18},{10... | collective-permute-start | bytes 663560 | tf_op jit(solution)/shard_map/ppermute | solution.py:510
  55.9 4.9 %collective-permute-done.6.refs_3_ = bf16[2,144,384]{2,1,0:T(8,128)(2,1)S(1)} collective-permute-done((bf16[2,144,384]{2,1,0:T(8,128)(2,1)S(1)}, bf16[2,144,384]{2,1,0:T(8,128)(2,1)S(1)}, u32[]{:S(2)}, u32[]{:S(2)}) %collective-permute-start.6) | collective-permute-done | bytes 221216 | tf_op jit(solution)/shard_map/ppermute | solution.py:510
  62.5 4.1 %collective-permute-start.10 = (bf16[2,144,384]{2,1,0:T(8,128)(2,1)S(1)}, bf16[2,144,384]{2,1,0:T(8,128)(2,1)S(1)}, u32[]{:S(2)}, u32[]{:S(2)}) collective-permute-start(bf16[2,144,384]{2,1,0:T(8,128)(2,1)S(1)} %get-tuple-element.172.refs_1_), channel_id=1, source_target_pairs={{0,64},{32,96},{64,0},{96,32},{1,65},{33,97},{65,1},{97,33},{2,66}... | collective-permute-start | bytes 663560 | tf_op jit(solution)/shard_map/ppermute | solution.py:510
  72.0 5.2 %collective-permute-done.9.refs_3_ = bf16[2,144,384]{2,1,0:T(8,128)(2,1)S(1)} collective-permute-done((bf16[2,144,384]{2,1,0:T(8,128)(2,1)S(1)}, bf16[2,144,384]{2,1,0:T(8,128)(2,1)S(1)}, u32[]{:S(2)}, u32[]{:S(2)}) %collective-permute-start.9) | collective-permute-done | bytes 221216 | tf_op jit(solution)/shard_map/ppermute | solution.py:510
  77.3 5.7 %shard_map.312 = (bf16[8,128,256]{2,1,0:T(8,128)(2,1)}, bf16[8,128,256]{2,1,0:T(8,128)(2,1)}, f32[512,512]{1,0:T(8,128)}, bf16[512,512]{1,0:T(8,128)(2,1)S(1)}, ...) custom-call(s32[4]{0:T(128)S(1)} %pad_add_fusion.refs_0_.mine, ...), custom_call_target="tpu_custom_call" | custom-call | flops 44000000 | tf_op jit(solution)/shard_map/pallas_call | solution.py:398
  90.2 11.7 %collective-permute-done.16.refs_3_ = bf16[64,2048]{1,0:T(8,128)(2,1)S(1)} collective-permute-done((bf16[64,2048]{1,0:T(8,128)(2,1)S(1)}, bf16[64,2048]{1,0:T(8,128)(2,1)S(1)}, u32[]{:S(2)}, u32[]{:S(2)}) %collective-permute-start.16) | collective-permute-done | bytes 262176 | tf_op jit(solution)/shard_map/ppermute | solution.py:510
  105.3 5.1 %collective-permute-done.21.refs_4_ = bf16[64,2048]{1,0:T(8,128)(2,1)S(1)} collective-permute-done((bf16[64,2048]{1,0:T(8,128)(2,1)S(1)}, bf16[64,2048]{1,0:T(8,128)(2,1)S(1)}, u32[]{:S(2)}, u32[]{:S(2)}) %collective-permute-start.21) | collective-permute-done | bytes 262176 | tf_op jit(solution)/shard_map/ppermute | solution.py:510
  110.4 7.2 %collective-permute-done.20.refs_3_ = bf16[64,2048]{1,0:T(8,128)(2,1)S(1)} collective-permute-done((bf16[64,2048]{1,0:T(8,128)(2,1)S(1)}, bf16[64,2048]{1,0:T(8,128)(2,1)S(1)}, u32[]{:S(2)}, u32[]{:S(2)}) %collective-permute-start.20) | collective-permute-done | bytes 262176 | tf_op jit(solution)/shard_map/ppermute | solution.py:510
  121.3 8.3 %shard_map.316 = (bf16[512,2048]{1,0:T(8,128)(2,1)S(1)}, bf16[704,512]{1,0:T(8,128)(2,1)S(1)}, bf16[704,512]{1,0:T(8,128)(2,1)S(1)}, bf16[704,512]{1,0:T(8,128)(...) custom-call(s32[4]{0:T(128)S(1)} %pad_add_fusion.refs_0_.mine, ...), custom_call_target="tpu_custom_call" | custom-call | flops 99000000 | tf_op jit(solution)/shard_map/pallas_call | solution.py:398
  141.2 3.0 shard_map.320
  145.8 6.5 %collective-permute-done.27.refs_7_ = bf16[64,2048]{1,0:T(8,128)(2,1)S(1)} collective-permute-done((bf16[64,2048]{1,0:T(8,128)(2,1)S(1)}, bf16[64,2048]{1,0:T(8,128)(2,1)S(1)}, u32[]{:S(2)}, u32[]{:S(2)}) %collective-permute-start.27) | collective-permute-done | bytes 262176 | tf_op jit(solution)/shard_map/ppermute | solution.py:510
  160.5 4.8 %shard_map.317 = (bf16[4,512,256]{2,1,0:T(8,128)(2,1)S(1)}, bf16[4,512,256]{2,1,0:T(8,128)(2,1)S(1)}, f32[8,128]{1,0:T(8,128)S(1)}) custom-call(s32[4]{0:T(128)S(1)} %pad_add_fusion.refs_0_.mine, bf16[704,512]{1,0:T(8,128)(2,1)S(1)} %get-tuple-element.192.product.refs_5_, bf16[704,2048]{1,0:T(8,128)(2,1)S(1)} %bitcast.36, ...), custom_call_target="tpu_custom_call" | custom-call | flops 44000000 | tf_op jit(solution)/shard_map/pallas_call | solution.py:980
  165.3 7.4 %collective-permute-done.29.refs_3_ = bf16[64,2048]{1,0:T(8,128)(2,1)S(1)} collective-permute-done((bf16[64,2048]{1,0:T(8,128)(2,1)S(1)}, bf16[64,2048]{1,0:T(8,128)(2,1)S(1)}, u32[]{:S(2)}, u32[]{:S(2)}) %collective-permute-start.29) | collective-permute-done | bytes 262176 | tf_op jit(solution)/shard_map/ppermute | solution.py:510
  180.4 2.7 collective-permute-start.36
  188.2 3.3 %shard_map.326 = (bf16[4,1024,128]{2,1,0:T(8,128)(2,1)S(1)}, bf16[4,1024,128]{2,1,0:T(8,128)(2,1)S(1)}, bf16[4,1024,128]{2,1,0:T(8,128)(2,1)S(1)}, bf16[4,1024,128]{2,1,0:T(8,128)(2,1)S(1)}, f32[1,2048]{1,0:T(1,128)S(1)}) custom-call(s32[4]{0:T(128)S(1)} %pad_add_fusion.refs_0_.mine, bf16[512,2048]{1,0:T(8,128)(2,1)S(1)} %get-tuple-element.222.refs_1_, ...), custom_call_target="tpu_custom_call" | custom-call | flops 55000000 | tf_op jit(solution)/shard_map/pallas_call | solution.py:398
  197.2 2.7 collective-permute-done.41.refs_6_.refs_5_
  200.0 3.7 %collective-permute-done.40.refs_5_.refs_4_ = bf16[2,128,256]{2,1,0:T(8,128)(2,1)S(1)} collective-permute-done((bf16[2,128,256]{2,1,0:T(8,128)(2,1)S(1)}, bf16[2,128,256]{2,1,0:T(8,128)(2,1)S(1)}, u32[]{:S(2)}, u32[]{:S(2)}) %collective-permute-start.40) | collective-permute-done | bytes 131104 | tf_op jit(solution)/shard_map/ppermute | solution.py:510
  207.9 9.7 %shard_map.331 = (bf16[528,1024]{1,0:T(8,128)(2,1)S(1)}, f32[512,2]{1,0:T(8,128)S(1)}, f32[16,528]{1,0:T(8,128)S(1)}, f32[8,1024]{1,0:T(8,128)S(1)}, f32[528,1]{1,0:T(8,128)S(1)}) custom-call(s32[4]{0:T(128)S(1)} %pad_add_fusion.refs_0_.mine, bf16[4,2,144,384]{3,2,1,0:T(8,128)(2,1)S(1)} %copy-done.18, bf16[2,128,256]{2,1,0:T(8,128)(2,1)S(1)} %get-tuple-element.233.refs_2_, ...), custom_call_target="tpu_custom_call" | custom-call | flops 121000000 | tf_op jit(solution)/shard_map/pallas_call | solution.py:398
  220.5 4.9 %shard_map.333 = (bf16[4,2112,128]{2,1,0:T(8,128)(2,1)S(1)}, bf16[4,2112,128]{2,1,0:T(8,128)(2,1)S(1)}, bf16[4,2112,128]{2,1,0:T(8,128)(2,1)S(1)}, bf16[4,1056,1...) custom-call(s32[4]{0:T(128)S(1)} %pad_add_fusion.refs_0_.mine, ...), custom_call_target="tpu_custom_call" | custom-call | flops 66000000 | tf_op jit(solution)/shard_map/pallas_call | solution.py:398
  232.1 7.9 %shard_map.336 = (bf16[4,544,256]{2,1,0:T(8,128)(2,1)}, bf16[4,544,256]{2,1,0:T(8,128)(2,1)S(1)}, f32[8,128]{1,0:T(8,128)S(1)}) custom-call(s32[4]{0:T(128)S(1)} %pad_add_fusion.refs_0_.mine, bf16[528,1024]{1,0:T(8,128)(2,1)S(1)} %get-tuple-element.247.refs_3_.dproj, bf16[512,512]{1,0:T(8,128)(2,1)S(1)} %get-tuple-element.226.refs_4_.d_pre, ...), custom_call_target="tpu_custom_call" | custom-call | flops 66000000 | tf_op jit(solution)/shard_map/pallas_call | solution.py:1035
  242.7 2.9 shard_map.337
  248.2 3.7 %collective-permute-start.48 = (bf16[4,544,256]{2,1,0:T(8,128)(2,1)}, bf16[4,544,256]{2,1,0:T(8,128)(2,1)}, u32[]{:S(2)}, u32[]{:S(2)}) collective-permute-start(bf16[4,544,256]{2,1,0:T(8,128)(2,1)} %get-tuple-element.270), channel_id=1, source_target_pairs={{0,1},{1,0},{2,3},{3,2},{4,5},{5,4},{6,7},{7,6},{8,9},{9,8},{10,11... | collective-permute-start | bytes 3342344 | tf_op jit(solution)/shard_map/ppermute | solution.py:510
  252.6 4.0 %all-to-all-start.1 = ((f32[4,3,4,8,128]{4,3,2,1,0:T(8,128)}), f32[4,3,4,8,128]{4,3,2,1,0:T(8,128)}, u32[]{:S(2)}, u32[]{:S(2)}) async-start(f32[4,3,4,8,128]{4,3,2,1,0:T(8,128)} %broadcast_in_dim.2), calls=%async_computation.1 | async-start | bytes 393216 | tf_op jit(solution)/shard_map/all_to_all | solution.py:818
  259.1 3.2 %all-to-all-done.1.refs_0_ = f32[4,3,4,8,128]{4,3,2,1,0:T(8,128)} async-done(((f32[4,3,4,8,128]{4,3,2,1,0:T(8,128)}), f32[4,3,4,8,128]{4,3,2,1,0:T(8,128)}, u32[]{:S(2)}, u32[]{:S(2)}) %all-to-all-start.1) | async-done | bytes 196640 | tf_op jit(solution)/shard_map/all_to_all | solution.py:818
  262.3 3.5 %all-to-all-start = ((bf16[4,544,256]{2,1,0:T(8,128)(2,1)}), bf16[4,544,256]{2,1,0:T(8,128)(2,1)S(1)}, u32[]{:S(2)}, u32[]{:S(2)}) async-start(bf16[4,544,256]{2,1,0:T(8,128)(2,1)} %shard_map.338), calls=%async_computation | async-start | bytes 2228224 | tf_op jit(solution)/shard_map/all_to_all | solution.py:1295
  269.6 3.6 %collective-permute-done.54.refs_5_ = f32[4,8,128]{2,1,0:T(8,128)S(1)} collective-permute-done((f32[4,8,128]{2,1,0:T(8,128)S(1)}, f32[4,8,128]{2,1,0:T(8,128)S(1)}, u32[]{:S(2)}, u32[]{:S(2)}) %collective-permute-start.54) | collective-permute-done | bytes 16416 | tf_op jit(solution)/shard_map/ppermute | solution.py:541
  273.1 4.0 %shard_map.342 = (f32[2112,128]{1,0:T(8,128)S(1)}, bf16[2112,128]{1,0:T(8,128)(2,1)}, bf16[2112,128]{1,0:T(8,128)(2,1)}, bf16[2112,128]{1,0:T(8,128)(2,1)}, f32[8,128]{1,0:T(8,128)}) custom-call(s32[4]{0:T(128)S(1)} %pad_add_fusion.refs_0_.mine, bf16[4,2112,128]{2,1,0:T(8,128)(2,1)S(1)} %get-tuple-element.271.refs_0_.refs_1_, ...), custom_call_target="tpu_custom_call" | custom-call | flops 11000000 | tf_op jit(solution)/shard_map/pallas_call | solution.py:398
  285.8 4.6 %collective-permute-done.56.refs_1_ = bf16[2112,128]{1,0:T(8,128)(2,1)S(1)} collective-permute-done((bf16[2112,128]{1,0:T(8,128)(2,1)}, bf16[2112,128]{1,0:T(8,128)(2,1)S(1)}, u32[]{:S(2)}, u32[]{:S(2)}) %collective-permute-start.56) | collective-permute-done | bytes 540704 | tf_op jit(solution)/shard_map/ppermute | solution.py:541
  290.4 5.5 %collective-permute-done.57.refs_2_ = bf16[2112,128]{1,0:T(8,128)(2,1)S(1)} collective-permute-done((bf16[2112,128]{1,0:T(8,128)(2,1)}, bf16[2112,128]{1,0:T(8,128)(2,1)S(1)}, u32[]{:S(2)}, u32[]{:S(2)}) %collective-permute-start.57) | collective-permute-done | bytes 540704 | tf_op jit(solution)/shard_map/ppermute | solution.py:541
  (218 shorter events, 138.6 us)
Async XLA Ops:
  0.7 14.8 %collective-permute-start.2 = (bf16[512,256]{1,0:T(8,128)(2,1)}, bf16[512,256]{1,0:T(8,128)(2,1)S(1)}, u32[]{:S(2)}, u32[]{:S(2)}) collective-permute-start(bf16[512,256]{1,0:T(8,128)(2,1)} %refs_3_.5), channel_id=1, source_target_pairs={{0,4},{2,6},{4,0},{6,2},{1,5},{3,7},{5,1},{7,3},{8,12},{10,14},{12... | collective-permute-start | bytes 786440 | tf_op jit(solution)/shard_map/ppermute | solution.py:510
  4.3 12.6 %collective-permute-start.1 = (bf16[512,256]{1,0:T(8,128)(2,1)}, bf16[512,256]{1,0:T(8,128)(2,1)S(1)}, u32[]{:S(2)}, u32[]{:S(2)}) collective-permute-start(bf16[512,256]{1,0:T(8,128)(2,1)} %refs_3_.5), channel_id=1, source_target_pairs={{0,2},{2,4},{4,6},{6,0},{1,3},{3,5},{5,7},{7,1},{8,10},{10,12},{12... | collective-permute-start | bytes 786440 | tf_op jit(solution)/shard_map/ppermute | solution.py:510
  4.6 12.3 %collective-permute-start = (bf16[512,256]{1,0:T(8,128)(2,1)}, bf16[512,256]{1,0:T(8,128)(2,1)S(1)}, u32[]{:S(2)}, u32[]{:S(2)}) collective-permute-start(bf16[512,256]{1,0:T(8,128)(2,1)} %refs_3_.5), channel_id=1, source_target_pairs={{0,6},{2,0},{4,2},{6,4},{1,7},{3,1},{5,3},{7,5},{8,14},{10,8},{12,... | collective-permute-start | bytes 786440 | tf_op jit(solution)/shard_map/ppermute | solution.py:510
  24.0 20.7 %collective-permute-start.13 = (bf16[512,256]{1,0:T(8,128)(2,1)S(1)}, bf16[512,256]{1,0:T(8,128)(2,1)S(1)}, u32[]{:S(2)}, u32[]{:S(2)}) collective-permute-start(bf16[512,256]{1,0:T(8,128)(2,1)S(1)} %get-tuple-element.181.refs_1_), channel_id=1, source_target_pairs={{0,4},{2,6},{4,0},{6,2},{1,5},{3,7},{5,1},{7,3},{8,12},{10,14},{12... | collective-permute-start | bytes 786440 | tf_op jit(solution)/shard_map/ppermute | solution.py:510
  25.8 18.9 %collective-permute-start.12 = (bf16[512,256]{1,0:T(8,128)(2,1)S(1)}, bf16[512,256]{1,0:T(8,128)(2,1)S(1)}, u32[]{:S(2)}, u32[]{:S(2)}) collective-permute-start(bf16[512,256]{1,0:T(8,128)(2,1)S(1)} %get-tuple-element.181.refs_1_), channel_id=1, source_target_pairs={{0,2},{2,4},{4,6},{6,0},{1,3},{3,5},{5,7},{7,1},{8,10},{10,12},{12... | collective-permute-start | bytes 786440 | tf_op jit(solution)/shard_map/ppermute | solution.py:510
  26.9 17.8 %collective-permute-start.11 = (bf16[512,256]{1,0:T(8,128)(2,1)S(1)}, bf16[512,256]{1,0:T(8,128)(2,1)S(1)}, u32[]{:S(2)}, u32[]{:S(2)}) collective-permute-start(bf16[512,256]{1,0:T(8,128)(2,1)S(1)} %get-tuple-element.181.refs_1_), channel_id=1, source_target_pairs={{0,6},{2,0},{4,2},{6,4},{1,7},{3,1},{5,3},{7,5},{8,14},{10,8},{12,... | collective-permute-start | bytes 786440 | tf_op jit(solution)/shard_map/ppermute | solution.py:510
  45.3 23.9 %collective-permute-start.14 = (bf16[4,512,256]{2,1,0:T(8,128)(2,1)S(1)}, bf16[4,512,256]{2,1,0:T(8,128)(2,1)S(1)}, u32[]{:S(2)}, u32[]{:S(2)}) collective-permute-start(bf16[4,512,256]{2,1,0:T(8,128)(2,1)S(1)} %shard_map.310.refs_1_), channel_id=1, source_target_pairs={{0,1},{1,0},{2,3},{3,2},{4,5},{5,4},{6,7},{7,6},{8,9},{9,8},{10,11... | collective-permute-start | bytes 3145736 | tf_op jit(solution)/shard_map/ppermute | solution.py:510
  87.5 14.3 %collective-permute-start.16 = (bf16[64,2048]{1,0:T(8,128)(2,1)S(1)}, bf16[64,2048]{1,0:T(8,128)(2,1)S(1)}, u32[]{:S(2)}, u32[]{:S(2)}) collective-permute-start(bf16[64,2048]{1,0:T(8,128)(2,1)S(1)} %get-tuple-element.187), channel_id=1, source_target_pairs={{0,2},{2,4},{4,6},{6,0},{1,3},{3,5},{5,7},{7,1},{8,10},{10,12},{12... | collective-permute-start | bytes 786440 | tf_op jit(solution)/shard_map/ppermute | solution.py:510
  87.5 14.3 %collective-permute-start.17 = (bf16[64,2048]{1,0:T(8,128)(2,1)S(1)}, bf16[64,2048]{1,0:T(8,128)(2,1)S(1)}, u32[]{:S(2)}, u32[]{:S(2)}) collective-permute-start(bf16[64,2048]{1,0:T(8,128)(2,1)S(1)} %get-tuple-element.188), channel_id=1, source_target_pairs={{0,6},{2,0},{4,2},{6,4},{1,7},{3,1},{5,3},{7,5},{8,14},{10,8},{12,... | collective-permute-start | bytes 786440 | tf_op jit(solution)/shard_map/ppermute | solution.py:510
  102.6 15.0 %collective-permute-start.20 = (bf16[64,2048]{1,0:T(8,128)(2,1)S(1)}, bf16[64,2048]{1,0:T(8,128)(2,1)S(1)}, u32[]{:S(2)}, u32[]{:S(2)}) collective-permute-start(bf16[64,2048]{1,0:T(8,128)(2,1)S(1)} %get-tuple-element.190.refs_1_), channel_id=1, source_target_pairs={{0,2},{2,4},{4,6},{6,0},{1,3},{3,5},{5,7},{7,1},{8,10},{10,12},{12... | collective-permute-start | bytes 786440 | tf_op jit(solution)/shard_map/ppermute | solution.py:510
  105.2 12.4 %collective-permute-start.19 = (bf16[64,2048]{1,0:T(8,128)(2,1)S(1)}, bf16[64,2048]{1,0:T(8,128)(2,1)S(1)}, u32[]{:S(2)}, u32[]{:S(2)}) collective-permute-start(bf16[64,2048]{1,0:T(8,128)(2,1)S(1)} %get-tuple-element.190.refs_1_), channel_id=1, source_target_pairs={{0,6},{2,0},{4,2},{6,4},{1,7},{3,1},{5,3},{7,5},{8,14},{10,8},{12,... | collective-permute-start | bytes 786440 | tf_op jit(solution)/shard_map/ppermute | solution.py:510
  134.9 17.8 %collective-permute-start.31 = (bf16[4,1056,128]{2,1,0:T(8,128)(2,1)S(1)}, bf16[4,1056,128]{2,1,0:T(8,128)(2,1)S(1)}, u32[]{:S(2)}, u32[]{:S(2)}) collective-permute-start(bf16[4,1056,128]{2,1,0:T(8,128)(2,1)S(1)} %get-tuple-element.218), channel_id=1, source_target_pairs={{0,8},{1,33},{8,16},{9,41},{16,24},{17,49},{24,0},{25,57},{32,40},... | collective-permute-start | bytes 3244040 | tf_op jit(solution)/shard_map/ppermute | solution.py:541
  136.0 16.7 %collective-permute-start.32 = (bf16[4,1056,128]{2,1,0:T(8,128)(2,1)S(1)}, bf16[4,1056,128]{2,1,0:T(8,128)(2,1)S(1)}, u32[]{:S(2)}, u32[]{:S(2)}) collective-permute-start(bf16[4,1056,128]{2,1,0:T(8,128)(2,1)S(1)} %get-tuple-element.219), channel_id=1, source_target_pairs={{0,24},{1,97},{8,0},{9,105},{16,8},{17,113},{24,16},{25,121},{32,5... | collective-permute-start | bytes 3244040 | tf_op jit(solution)/shard_map/ppermute | solution.py:541
  140.3 11.9 %collective-permute-start.27 = (bf16[64,2048]{1,0:T(8,128)(2,1)S(1)}, bf16[64,2048]{1,0:T(8,128)(2,1)S(1)}, u32[]{:S(2)}, u32[]{:S(2)}) collective-permute-start(bf16[64,2048]{1,0:T(8,128)(2,1)S(1)} %get-tuple-element.206), channel_id=1, source_target_pairs={{0,4},{2,6},{4,0},{6,2},{1,5},{3,7},{5,1},{7,3},{8,12},{10,14},{12... | collective-permute-start | bytes 786440 | tf_op jit(solution)/shard_map/ppermute | solution.py:510
  154.4 37.0 %collective-permute-start.37 = (bf16[4,2112,128]{2,1,0:T(8,128)(2,1)S(1)}, bf16[4,2112,128]{2,1,0:T(8,128)(2,1)S(1)}, u32[]{:S(2)}, u32[]{:S(2)}) collective-permute-start(bf16[4,2112,128]{2,1,0:T(8,128)(2,1)S(1)} %get-tuple-element.230), channel_id=1, source_target_pairs={{0,8},{1,33},{8,16},{9,41},{16,24},{17,49},{24,0},{25,57},{32,40},... | collective-permute-start | bytes 6488072 | tf_op jit(solution)/shard_map/ppermute | solution.py:541
  154.8 36.6 %collective-permute-start.38 = (bf16[4,2112,128]{2,1,0:T(8,128)(2,1)}, bf16[4,2112,128]{2,1,0:T(8,128)(2,1)S(1)}, u32[]{:S(2)}, u32[]{:S(2)}) collective-permute-start(bf16[4,2112,128]{2,1,0:T(8,128)(2,1)} %get-tuple-element.231), channel_id=1, source_target_pairs={{0,24},{1,97},{8,0},{9,105},{16,8},{17,113},{24,16},{25,121},{32,5... | collective-permute-start | bytes 6488072 | tf_op jit(solution)/shard_map/ppermute | solution.py:541
  157.5 15.2 %collective-permute-start.29 = (bf16[64,2048]{1,0:T(8,128)(2,1)S(1)}, bf16[64,2048]{1,0:T(8,128)(2,1)S(1)}, u32[]{:S(2)}, u32[]{:S(2)}) collective-permute-start(bf16[64,2048]{1,0:T(8,128)(2,1)S(1)} %get-tuple-element.214.refs_1_), channel_id=1, source_target_pairs={{0,2},{2,4},{4,6},{6,0},{1,3},{3,5},{5,7},{7,1},{8,10},{10,12},{12... | collective-permute-start | bytes 786440 | tf_op jit(solution)/shard_map/ppermute | solution.py:510
  158.7 14.0 %collective-permute-start.28 = (bf16[64,2048]{1,0:T(8,128)(2,1)S(1)}, bf16[64,2048]{1,0:T(8,128)(2,1)S(1)}, u32[]{:S(2)}, u32[]{:S(2)}) collective-permute-start(bf16[64,2048]{1,0:T(8,128)(2,1)S(1)} %get-tuple-element.214.refs_1_), channel_id=1, source_target_pairs={{0,6},{2,0},{4,2},{6,4},{1,7},{3,1},{5,3},{7,5},{8,14},{10,8},{12,... | collective-permute-start | bytes 786440 | tf_op jit(solution)/shard_map/ppermute | solution.py:510
  180.4 12.5 %collective-permute-start.36 = (bf16[2,128,256]{2,1,0:T(8,128)(2,1)S(1)}, bf16[2,128,256]{2,1,0:T(8,128)(2,1)S(1)}, u32[]{:S(2)}, u32[]{:S(2)}) collective-permute-start(bf16[2,128,256]{2,1,0:T(8,128)(2,1)S(1)} %get-tuple-element.224.refs_2_), channel_id=1, source_target_pairs={{0,16},{8,24},{16,0},{24,8},{1,17},{9,25},{17,1},{25,9},{2,18},{10... | collective-permute-start | bytes 393224 | tf_op jit(solution)/shard_map/ppermute | solution.py:510
  203.7 15.7 %collective-permute-start.42 = (bf16[2112,128]{1,0:T(8,128)(2,1)S(1)}, bf16[2112,128]{1,0:T(8,128)(2,1)S(1)}, u32[]{:S(2)}, u32[]{:S(2)}) collective-permute-start(bf16[2112,128]{1,0:T(8,128)(2,1)S(1)} %get-tuple-element.257), channel_id=1, source_target_pairs={{0,32},{1,9},{8,40},{9,17},{16,48},{17,25},{24,56},{25,1},{32,64},... | collective-permute-start | bytes 1622024 | tf_op jit(solution)/shard_map/ppermute | solution.py:541
  203.8 15.5 %collective-permute-start.43 = (bf16[2112,128]{1,0:T(8,128)(2,1)S(1)}, bf16[2112,128]{1,0:T(8,128)(2,1)S(1)}, u32[]{:S(2)}, u32[]{:S(2)}) collective-permute-start(bf16[2112,128]{1,0:T(8,128)(2,1)S(1)} %get-tuple-element.258), channel_id=1, source_target_pairs={{0,96},{1,25},{8,104},{9,1},{16,112},{17,9},{24,120},{25,17},{32,0... | collective-permute-start | bytes 1622024 | tf_op jit(solution)/shard_map/ppermute | solution.py:541
  206.5 12.8 %collective-permute-start.44 = (bf16[2112,128]{1,0:T(8,128)(2,1)S(1)}, bf16[2112,128]{1,0:T(8,128)(2,1)S(1)}, u32[]{:S(2)}, u32[]{:S(2)}) collective-permute-start(bf16[2112,128]{1,0:T(8,128)(2,1)S(1)} %get-tuple-element.259), channel_id=1, source_target_pairs={{0,64},{1,17},{8,72},{9,25},{16,80},{17,1},{24,88},{25,9},{32,96},... | collective-permute-start | bytes 1622024 | tf_op jit(solution)/shard_map/ppermute | solution.py:541
  206.5 21.6 %collective-permute-start.23 = (bf16[4,512,256]{2,1,0:T(8,128)(2,1)S(1)}, bf16[4,512,256]{2,1,0:T(8,128)(2,1)S(1)}, u32[]{:S(2)}, u32[]{:S(2)}) collective-permute-start(bf16[4,512,256]{2,1,0:T(8,128)(2,1)S(1)} %get-tuple-element.195), channel_id=1, source_target_pairs={{0,1},{1,0},{2,3},{3,2},{4,5},{5,4},{6,7},{7,6},{8,9},{9,8},{10,11... | collective-permute-start | bytes 3145736 | tf_op jit(solution)/shard_map/ppermute | solution.py:510
  225.3 17.3 %collective-permute-start.49 = (bf16[4,1056,128]{2,1,0:T(8,128)(2,1)S(1)}, bf16[4,1056,128]{2,1,0:T(8,128)(2,1)S(1)}, u32[]{:S(2)}, u32[]{:S(2)}) collective-permute-start(bf16[4,1056,128]{2,1,0:T(8,128)(2,1)S(1)} %get-tuple-element.274), channel_id=1, source_target_pairs={{0,8},{1,33},{8,16},{9,41},{16,24},{17,49},{24,0},{25,57},{32,40},... | collective-permute-start | bytes 3244040 | tf_op jit(solution)/shard_map/ppermute | solution.py:541
  225.4 17.3 %collective-permute-start.50 = (bf16[4,1056,128]{2,1,0:T(8,128)(2,1)S(1)}, bf16[4,1056,128]{2,1,0:T(8,128)(2,1)S(1)}, u32[]{:S(2)}, u32[]{:S(2)}) collective-permute-start(bf16[4,1056,128]{2,1,0:T(8,128)(2,1)S(1)} %get-tuple-element.275), channel_id=1, source_target_pairs={{0,24},{1,97},{8,0},{9,105},{16,8},{17,113},{24,16},{25,121},{32,5... | collective-permute-start | bytes 3244040 | tf_op jit(solution)/shard_map/ppermute | solution.py:541
  245.5 27.6 %collective-permute-start.52 = (bf16[4,2112,128]{2,1,0:T(8,128)(2,1)}, bf16[4,2112,128]{2,1,0:T(8,128)(2,1)}, u32[]{:S(2)}, u32[]{:S(2)}) collective-permute-start(bf16[4,2112,128]{2,1,0:T(8,128)(2,1)} %get-tuple-element.283), channel_id=1, source_target_pairs={{0,8},{1,33},{8,16},{9,41},{16,24},{17,49},{24,0},{25,57},{32,40},... | collective-permute-start | bytes 6488072 | tf_op jit(solution)/shard_map/ppermute | solution.py:541
  245.5 27.6 %collective-permute-start.53 = (bf16[4,2112,128]{2,1,0:T(8,128)(2,1)}, bf16[4,2112,128]{2,1,0:T(8,128)(2,1)}, u32[]{:S(2)}, u32[]{:S(2)}) collective-permute-start(bf16[4,2112,128]{2,1,0:T(8,128)(2,1)} %get-tuple-element.284), channel_id=1, source_target_pairs={{0,24},{1,97},{8,0},{9,105},{16,8},{17,113},{24,16},{25,121},{32,5... | collective-permute-start | bytes 6488072 | tf_op jit(solution)/shard_map/ppermute | solution.py:541
  262.3 22.0 %all-to-all-start = ((bf16[4,544,256]{2,1,0:T(8,128)(2,1)}), bf16[4,544,256]{2,1,0:T(8,128)(2,1)S(1)}, u32[]{:S(2)}, u32[]{:S(2)}) async-start(bf16[4,544,256]{2,1,0:T(8,128)(2,1)} %shard_map.338), calls=%async_computation | async-start | bytes 2228224 | tf_op jit(solution)/shard_map/all_to_all | solution.py:1295
  278.1 12.3 %collective-permute-start.56 = (bf16[2112,128]{1,0:T(8,128)(2,1)}, bf16[2112,128]{1,0:T(8,128)(2,1)S(1)}, u32[]{:S(2)}, u32[]{:S(2)}) collective-permute-start(bf16[2112,128]{1,0:T(8,128)(2,1)} %get-tuple-element.290), channel_id=1, source_target_pairs={{0,32},{1,9},{8,40},{9,17},{16,48},{17,25},{24,56},{25,1},{32,64},... | collective-permute-start | bytes 1622024 | tf_op jit(solution)/shard_map/ppermute | solution.py:541
  280.6 15.3 %collective-permute-start.57 = (bf16[2112,128]{1,0:T(8,128)(2,1)}, bf16[2112,128]{1,0:T(8,128)(2,1)S(1)}, u32[]{:S(2)}, u32[]{:S(2)}) collective-permute-start(bf16[2112,128]{1,0:T(8,128)(2,1)} %get-tuple-element.291), channel_id=1, source_target_pairs={{0,96},{1,25},{8,104},{9,1},{16,112},{17,9},{24,120},{25,17},{32,0... | collective-permute-start | bytes 1622024 | tf_op jit(solution)/shard_map/ppermute | solution.py:541
  283.2 14.2 %collective-permute-start.58 = (bf16[2112,128]{1,0:T(8,128)(2,1)}, bf16[2112,128]{1,0:T(8,128)(2,1)S(1)}, u32[]{:S(2)}, u32[]{:S(2)}) collective-permute-start(bf16[2112,128]{1,0:T(8,128)(2,1)} %get-tuple-element.292), channel_id=1, source_target_pairs={{0,64},{1,17},{8,72},{9,25},{16,80},{17,1},{24,88},{25,9},{32,96},... | collective-permute-start | bytes 1622024 | tf_op jit(solution)/shard_map/ppermute | solution.py:541
  284.5 16.6 %collective-permute-start.51 = (f32[24,256]{1,0:T(8,128)S(1)}, f32[24,256]{1,0:T(8,128)S(1)}, u32[]{:S(2)}, u32[]{:S(2)}) collective-permute-start(f32[24,256]{1,0:T(8,128)S(1)} %get-tuple-element.280), channel_id=1, source_target_pairs={{8,0},{16,8},{24,16},{32,24},{40,32},{48,40},{56,48},{64,56},{72,6... | collective-permute-start | bytes 73736 | tf_op jit(solution)/shard_map/ppermute | solution.py:1071
  (67 other events, 565.6 us)
where the time goes:
time: 309 us; the launch traced here: 304 us
  Pallas kernels  98.2 us (32%)
  starting transfers between devices  94.3 us (31%)
  waiting for transfers between devices  92.5 us (30%)
  local copies, waits for them, and re-layouts  10.7 us (3%)
  matrix products  6.09 us (2%)
    pallas_call x36, Pallas kernels, run(): pl.pallas_call(body, out_shape=tuple((pltpu.HBM(a.shape, a.dtype) if i in...  85.5 us
    ppermute x42, waiting for transfers between devices, rotated(): lax.ppermute(array, axis, [(i, (i + distance) % size) for i in range(size)])  72.5 us
    ppermute x42, starting transfers between devices, rotated(): lax.ppermute(array, axis, [(i, (i + distance) % size) for i in range(size)])  58.7 us
    ppermute x16, starting transfers between devices, turned(): return lax.ppermute(array, PLANE, pairs)  23 us
    ppermute x16, waiting for transfers between devices, turned(): return lax.ppermute(array, PLANE, pairs)  16.9 us
    unnamed x74, local copies, waits for them, and re-layouts  9.46 us
    pallas_call x1, Pallas kernels, d_first_tiles(): pl.pallas_call(d_first_kernel, grid_spec=spec, out_shape=(tiles, tiles, o...  7.9 us
  transfers between devices with their start and end apart: 62, of which 26 were waited for; matrix products, arithmetic and copies ran while one was open for 2% of the time, Pallas kernels for 23%

commit v1 on v0

--- a/solution.py
+++ b/solution.py
@@ -62,7 +62,24 @@
     return total
 
 
-def prepare_kernel(heads, chunks, proj, halo, taps, logits, gcol, grow, q_out, k_out, v_out, t_out, n_out, b_out, w_out, u_out, p_out, pay, token, wide):
+def query_kernel(heads, chunks, proj, halo, taps, k, gcol, grow, q_out, p_out, token, wide):
+    token[...] = jnp.zeros(token.shape, FLOAT)
+    kq = heads * DK
+    wide[:HALO, :] = halo[:, :kq].astype(FLOAT)
+    wide[HALO:, :] = proj[:, :kq].astype(FLOAT)
+    for h in range(heads):
+        for c in range(chunks):
+            span = slice(c * CH, (c + 1) * CH)
+            lanes = slice(h * DK, (h + 1) * DK)
+            at = h * chunks + c
+            cq = conv_of(wide, taps, c * CH, CH, lanes)
+            query = (cq * sigmoid(cq)).astype(HALF)
+            q_out[span, lanes] = query
+            spread = decay_matrix(gcol[span, h : h + 1], grow[at : at + 1, :])
+            p_out[at] = (spread * mm(query, k[span, lanes], NT)).astype(HALF)
+
+
+def prepare_kernel(heads, chunks, proj, halo, taps, logits, gcol, grow, k_out, v_out, t_out, n_out, b_out, w_out, u_out, pay, token, wide):
     token[...] = jnp.zeros(token.shape, FLOAT)
     rows, cols = square_masks()
     differ = rows ^ cols
@@ -79,14 +96,11 @@
             slice(kq + h * DK, kq + (h + 1) * DK),
             slice(2 * kq + h * DV, 2 * kq + (h + 1) * DV),
         )
-        cq = conv_of(wide, taps, c * CH, CH, ql)
-        query = (cq * sigmoid(cq)).astype(HALF)
         ck = conv_of(wide, taps, c * CH, CH, kl)
         act = ck * sigmoid(ck)
         key = (act * lax.rsqrt(jnp.sum(act * act, axis=-1, keepdims=True) + EPS_NORM)).astype(HALF)
         cv = conv_of(wide, taps, c * CH, CH, vl)
         value = (cv * sigmoid(cv)).astype(HALF)
-        q_out[span, ql] = query
         k_out[span, ql] = key
         v_out[span, h * DV : (h + 1) * DV] = value
         beta = sigmoid(logits[span, h : h + 1])
@@ -94,7 +108,6 @@
         spread = decay_matrix(g, grow[h * chunks + c : h * chunks + c + 1, :])
         inner = mm(key, key, NT)
         low[h, c] = jnp.where(rows > cols, beta * spread * inner, 0.0)
-        p_out[h * chunks + c] = (spread * mm(query, key, NT)).astype(HALF)
         keys[h, c] = key
         sides[h, c] = jnp.concatenate([(beta * jnp.exp(g)) * key.astype(FLOAT), beta * value.astype(FLOAT)], axis=1)
     tri = {at: eye - jnp.where(differ < 2, low[at], 0.0) for at in work}
@@ -143,7 +156,8 @@
     pay[h, DK:, :] = jnp.concatenate([first, rest - first], axis=0).astype(HALF)
 
 
-def group_kernel(heads, mine, p0, p1, p2, p3, before, group, near):
+def group_kernel(heads, mine, p0, p1, p2, p3, before, group, near, token):
+    token[...] = jnp.zeros(token.shape, FLOAT)
     me = mine[3]
     for k, piece in enumerate((p0, p1, p2, p3)):
         near[ring_place(me, k)] = piece[...]
@@ -195,7 +209,8 @@
         other[x, :, lanes] = total[away, :].astype(HALF)
 
 
-def mix_kernel(heads, chunks, mine, p0, p1, p2, p3, before, q, k, w, u, p, n, b, gcol, gate, gain, weight, s_out, vn_out, o_out, gated, other, own, pay, total):
+def mix_kernel(heads, chunks, mine, p0, p1, p2, p3, before, q, k, w, u, p, n, b, gcol, gate, gain, weight, s_out, vn_out, o_out, gated, other, own, pay, token, total):
+    token[...] = jnp.zeros(token.shape, FLOAT)
     ranks = pay.shape[0]
     me = mine[2]
     for at, piece in enumerate((p0, p1, p2, p3)):
@@ -272,7 +287,34 @@
         dgain_out[0:1, h * DV : (h + 1) * DV] = dgain[h]
 
 
-def back_kernel(heads, chunks, mine, pay, p0, p1, p2, p3, after, q, k, v, logits, gate_sums, gcol, grow, tri, states, vns, dos, dvns, es, ns, proj, halo, taps, dproj_out, dlogit_out, logit_rows, dtaps_out, sums_out, wide, dconv, late, rowsum):
+def slopes_kernel(heads, chunks, k, v, states, gcol, grow, proj, halo, taps, slopes, inner_out, spread_out, rest, token, wide):
+    token[...] = jnp.zeros(token.shape, FLOAT)
+    kq = heads * DK
+    wide[:HALO, :] = halo[...].astype(FLOAT)
+    wide[HALO:, :] = proj[...].astype(FLOAT)
+    for h in range(heads):
+        for c in range(chunks):
+            span = slice(c * CH, (c + 1) * CH)
+            at = h * chunks + c
+            kl = slice(kq + h * DK, kq + (h + 1) * DK)
+            for lanes in (slice(h * DK, (h + 1) * DK), slice(2 * kq + h * DV, 2 * kq + (h + 1) * DV)):
+                pre = conv_of(wide, taps, c * CH, CH, lanes)
+                sig = sigmoid(pre)
+                slopes[span, lanes] = sig * (1.0 + pre * (1.0 - sig))
+            pre = conv_of(wide, taps, c * CH, CH, kl)
+            sig = sigmoid(pre)
+            act = pre * sig
+            unit = lax.rsqrt(jnp.sum(act * act, axis=-1, keepdims=True) + EPS_NORM)
+            slopes[span, kl] = unit * (sig * (1.0 + pre * (1.0 - sig)))
+            key = k[span, h * DK : (h + 1) * DK]
+            g = gcol[span, h : h + 1]
+            inner_out[at] = mm(key, key, NT)
+            spread_out[at] = decay_matrix(g, grow[at : at + 1, :])
+            vl = slice(h * DV, (h + 1) * DV)
+            rest[span, vl] = v[span, vl].astype(FLOAT) - jnp.exp(g) * mm(key, states[at])
+
+
+def back_kernel(heads, chunks, mine, pay, p0, p1, p2, p3, after, q, k, logits, gate_sums, gcol, tri, states, vns, dos, dvns, es, ns, proj, halo, taps, slopes, inner_in, spread_in, rest, dproj_out, dlogit_out, logit_rows, dtaps_out, sums_out, wide, dconv, late, rowsum):
     ranks = pay.shape[0]
     tokens = chunks * CH
     me = mine[2]
@@ -305,20 +347,19 @@
                 slice(h * DV, (h + 1) * DV),
             )
             grad = grads[h].astype(HALF)
-            query, key, value = q[span, ql], k[span, ql], v[span, ol]
+            query, key = q[span, ql], k[span, ql]
             state, vn, dout = states[at], vns[at], dos[span, ol]
             logit = logits[span, h : h + 1]
             beta = sigmoid(logit)
             g = gcol[span, h : h + 1]
             last = gcol[(c + 1) * CH - 1 : (c + 1) * CH, h : h + 1]
             eg, ed = jnp.exp(g), jnp.exp(last - g)
-            spread = decay_matrix(g, grow[at : at + 1, :])
+            spread = spread_in[at]
             strict = jnp.where(rows > cols, spread, 0.0)
-            inner = mm(key, key, NT)
+            inner = inner_in[at]
             dvn = dvns[at] + ed * mm(key, grad)
             dr = mm(tri[at], dvn, TN)
             drh = dr.astype(HALF)
-            ks = mm(key, state)
             dval = beta * dr
             both = mm(jnp.concatenate([dout, drh], axis=0), state, NT)
             dkeep = mm(vn, grad, NT)
@@ -326,7 +367,7 @@
             dqk = spread * pair[:CH]
             da = -(strict * pair[CH:])
             dkk = beta * da
-            dbeta = jnp.sum(dr * (value.astype(FLOAT) - eg * ks), axis=-1, keepdims=True) + jnp.sum(
+            dbeta = jnp.sum(dr * rest[span, ol], axis=-1, keepdims=True) + jnp.sum(
                 da * inner, axis=-1, keepdims=True
             )
             dqkh = dqk.astype(HALF)
@@ -348,19 +389,10 @@
             far_span = slice(HALO + c * CH, HALO + (c + 1) * CH)
             sums_out[far_span, :] = (gate_sums[span, :] if h == 0 else sums_out[far_span, :]) + extra_sum
             there = slice(HALO + c * CH, HALO + (c + 1) * CH)
-            cq = conv_of(wide, taps, c * CH, CH, ql)
-            sig = sigmoid(cq)
-            dconv[there, ql] = dquery * (sig * (1.0 + cq * (1.0 - sig)))
-            cv = conv_of(wide, taps, c * CH, CH, vl)
-            sig = sigmoid(cv)
-            dconv[there, vl] = dval * (sig * (1.0 + cv * (1.0 - sig)))
-            ck = conv_of(wide, taps, c * CH, CH, kl)
-            sig = sigmoid(ck)
-            act = ck * sig
-            unit = lax.rsqrt(jnp.sum(act * act, axis=-1, keepdims=True) + EPS_NORM)
-            u = act * unit
-            dact = unit * (dkey - u * jnp.sum(dkey * u, axis=-1, keepdims=True))
-            dconv[there, kl] = dact * (sig * (1.0 + ck * (1.0 - sig)))
+            dconv[there, ql] = dquery * slopes[span, ql]
+            dconv[there, vl] = dval * slopes[span, vl]
+            unit = key.astype(FLOAT)
+            dconv[there, kl] = (dkey - unit * jnp.sum(dkey * unit, axis=-1, keepdims=True)) * slopes[span, kl]
     dtaps_out[4:8, :] = jnp.zeros((4, width), FLOAT)
     rowsum[...] = jnp.zeros((HALO + tokens, 1), FLOAT)
     for at in range(0, width, DK):
@@ -430,14 +462,12 @@
     tokens, pairs = chunks * CH, heads * chunks
     return (
         out((tokens, heads * DK), HALF),
-        out((tokens, heads * DK), HALF),
         out((tokens, heads * DV), HALF),
         out((pairs, CH, CH), HALF),
         out((pairs, DK, DK), HALF),
         out((pairs, DK, DV), FLOAT),
         out((pairs, CH, DK), HALF),
         out((pairs, CH, DV), HALF),
-        out((pairs, CH, CH), HALF),
         out((heads, DK + 16, DK + DV), HALF),
     )
 
@@ -570,7 +600,7 @@
     token[...] = jnp.zeros(token.shape, FLOAT)
 
 
-def first_norm_kernel(mine, gain, beta_rows, cot, own, other, normed, factor, rows_out, logits, cot_out, halo_out):
+def first_norm_kernel(mine, gain, beta_rows, own, other, normed, factor, rows_out, logits, halo_out):
     width = own.shape[2]
     rows = rows_out.shape[0]
     own_rows = lane_block(mine[0] * 2 + mine[1], rows)
@@ -588,7 +618,6 @@
         total = total + mm(small, beta_rows[:, lanes], NT)
         rows_out[:, lanes] = ref[x, own_rows, :].astype(FLOAT)
     logits[...] = total
-    cot_out[...] = cot[...]
     halo_out[...] = normed[normed.shape[0] - HALO :, :]
 
 
@@ -668,10 +697,6 @@
     outs[4][...] = jnp.zeros(outs[4].shape, FLOAT)
 
 
-def tile_sum_kernel(own, arrived, total):
-    total[...] = (own[...].astype(FLOAT) + arrived[...].astype(FLOAT)).astype(HALF)
-
-
 def head_scatter(own, other, mine, with_token=False, after=()):
     arrived = rotated(other, "c", 1)
     shape = own.shape[1:]
@@ -679,6 +704,35 @@
     total, *sent, token = run(split_sum_kernel, shapes, (mine, own, arrived), scalars=1, after=after)
     parts = [total] + [rotated(part, "x", d) for d, part in zip(TURNS[1:], sent)]
     return (parts, token) if with_token else parts
+
+
+def swapped(array, mask):
+    return lax.ppermute(array, "x", [(i, i ^ mask) for i in range(4)])
+
+
+def first_half_kernel(mine, own, arrived, keep, send):
+    base = jnp.where(mine[0] < 2, 0, 2)
+    for target, at in ((keep, base), (send, 2 - base)):
+        for i in range(2):
+            target[i] = (own[at + i].astype(FLOAT) + arrived[at + i].astype(FLOAT)).astype(target.dtype)
+
+
+def second_half_kernel(mine, keep, arrived, own, send):
+    at = lax.rem(mine[0], 2)
+    own[...] = keep[at].astype(FLOAT) + arrived[at].astype(FLOAT)
+    send[...] = (keep[1 - at].astype(FLOAT) + arrived[1 - at].astype(FLOAT)).astype(HALF)
+
+
+def head_halving(own, other, mine, after):
+    shape = own.shape[1:]
+    pair = out((2, *shape), HALF)
+    keep, send = run(
+        first_half_kernel, (pair, pair), (mine, own, rotated(other, "c", 1)), scalars=1, after=after
+    )
+    total, send = run(
+        second_half_kernel, (out(shape, FLOAT), out(shape, HALF)), (mine, keep, swapped(send, 2)), scalars=1
+    )
+    return [total, swapped(send, 1)]
 
 
 def added(parts):
@@ -809,15 +863,10 @@
         rows[i] = gain_rows(ref)
 
 
-def quad_sum_kernel(tiles, own, plus, minus):
+def quad_sum_kernel(first, second, third, fourth, own, plus, minus, token):
+    token[...] = jnp.zeros(token.shape, FLOAT)
     for i, target in enumerate((own, plus, minus)):
-        target[...] = (tiles[0, i] + tiles[1, i]) + (tiles[2, i] + tiles[3, i])
-
-
-def gains_over_chips(rows):
-    tiles = lax.all_to_all(jnp.broadcast_to(rows[None], (4, *rows.shape)), "x", 0, 0, tiled=True)
-    own, plus, minus = run(quad_sum_kernel, (out((4, 8, DK), FLOAT),) * 3, (tiles,))
-    return own, turned(plus, True, 1), turned(minus, True, -1)
+        target[...] = (first[i] + second[i]) + (third[i] + fourth[i])
 
 
 def relay_kernel(plus, minus, first, second, plus_out, minus_out, token):
@@ -1041,8 +1090,9 @@
     )(mine, dproj, d_pre, d_logit, sums, in_rows, gate_rows, beta_rows, after)
 
 
-def first_total_kernel(tiles, total, pack):
-    whole = sum(tiles[x].astype(FLOAT) for x in range(4))
+def first_total_kernel(own, arrived, total, pack, token):
+    token[...] = jnp.zeros(token.shape, FLOAT)
+    whole = own[...] + arrived[...].astype(FLOAT)
     total[...] = whole
     pack[:HALO, :] = whole[:HALO]
     at = whole.shape[0] - HALO
@@ -1123,17 +1173,16 @@
     gain_row = mixer_gain.reshape(1, -1)
     first_row = first_gain.reshape(1, -1)
 
-    first_normed, first_factor, my_rows, logits, cot, halo_rows = run(
+    first_normed, first_factor, my_rows, logits, halo_rows = run(
         first_norm_kernel,
         (
             out((tokens, model), HALF),
             out((tokens, 1), FLOAT),
             out((rows, model), FLOAT),
             out((tokens, HALO), FLOAT),
-            out((tokens, width), HALF),
             out((HALO, model), HALF),
         ),
-        (mine, first_row, beta_rows, cotangent, *head_gather(block_input, mine, (token,))),
+        (mine, first_row, beta_rows, *head_gather(block_input, mine, (token,))),
         scalars=1,
         micros=3.0,
     )
@@ -1141,17 +1190,40 @@
     proj = dot_nt(first_normed, in_rows).astype(HALF)
     halo_proj = dot_nt(halo_normed, in_rows).astype(HALF)
     gate_pre = dot_nt(first_normed, gate_rows)
-    q, k, v, tri, n, b, w, u, p, pay, pay_token = run(
+    k, v, tri, n, b, w, u, pay, pay_token = run(
         partial(prepare_kernel, heads, chunks),
         prepare_shapes(heads, chunks) + (token_out,),
         (proj, halo_proj, taps, logits, gcol, grow),
         [pltpu.VMEM((HALO + tokens, cols), FLOAT)],
         micros=8.0,
-        kept=range(9),
+        kept=range(7),
         megs=20,
     )
     near_pieces = ring_pieces(pay, "z")
-    cot_tiles = head_gather(cot, mine, (pay_token,))
+    q, p, query_token = run(
+        partial(query_kernel, heads, chunks),
+        (out((tokens, kq), HALF), out((heads * chunks, CH, CH), HALF), token_out),
+        (proj, halo_proj, taps, k, gcol, grow),
+        [pltpu.VMEM((HALO + tokens, kq), FLOAT)],
+        after=(pay_token,),
+    )
+    before, group, near, group_token = run(
+        partial(group_kernel, heads), group_shapes(heads) + (token_out,), (mine, *near_pieces), scalars=1, after=(gate_pre[:8, :DK], query_token), micros=2.0
+    )
+    half_tiles = out((4, rows, model), HALF)
+    states, vns, mixed, gated, branch_other, branch_own, far, mix_token = run(
+        partial(mix_kernel, heads, chunks),
+        mix_shapes(heads, chunks)[:4] + (half_tiles, half_tiles) + mix_shapes(heads, chunks)[4:] + (token_out,),
+        (mine, *ring_pieces(group, "y"), before, q, k, w, u, p, n, b, gcol, gate_pre, gain_row, mixer_weight),
+        [pltpu.VMEM((tokens, model // 4), FLOAT)],
+        scalars=1,
+        kept=(0, 1, 2, 6),
+        megs=16,
+        micros=4.0,
+    )
+    branch = head_scatter(branch_own, branch_other, mine)
+    (cot,), _ = passed([cotangent], (group_token,))
+    cot_tiles = head_gather(cot, mine, (mix_token,))
     whole_cot, cot_rows, d_product, token = run(
         product_grad_kernel,
         (out((tokens, model), HALF), out((rows, model), HALF), out((hidden_cols, tokens), FLOAT), token_out),
@@ -1159,28 +1231,13 @@
         scalars=1,
         micros=4.0,
     )
-    before, group, near = run(
-        partial(group_kernel, heads), group_shapes(heads), (mine, *near_pieces), scalars=1, after=(gate_pre[:8, :DK],), micros=2.0
-    )
-    half_tiles = out((4, rows, model), HALF)
-    states, vns, mixed, gated, branch_other, branch_own, far = run(
-        partial(mix_kernel, heads, chunks),
-        mix_shapes(heads, chunks)[:4] + (half_tiles, half_tiles) + mix_shapes(heads, chunks)[4:],
-        (mine, *ring_pieces(group, "y"), before, q, k, w, u, p, n, b, gcol, gate_pre, gain_row, mixer_weight),
-        [pltpu.VMEM((tokens, model // 4), FLOAT)],
-        scalars=1,
-        after=(token,),
-        kept=(0, 1, 2, 6),
-        megs=16,
-        micros=4.0,
-    )
-    branch = head_scatter(branch_own, branch_other, mine)
     wide_rows = out((rows, model), FLOAT)
     second_row = second_gain.reshape(1, -1)
     hidden, second_unit, second_factor, own_normed = run(
         hidden_kernel,
         (wide_rows, wide_rows, out((rows, 1), FLOAT), out((rows, model), HALF)),
         (my_rows, second_row, *branch),
+        after=(token,),
     )
     turned_out = out((hidden_cols, tokens), HALF)
     second_normed, product, d_gate, d_up, second_other, second_own, ffn_token = run(
@@ -1243,20 +1300,24 @@
         micros=2.0,
     )
     end_pieces = ring_pieces(group_end, "y")
-    passed_sums, ffn_token = passed(ffn_sums, tuple(end_pieces[1:]))
+    square = out((heads * chunks, CH, CH), FLOAT)
+    *slopes, slope_token = run(
+        partial(slopes_kernel, heads, chunks),
+        (out((tokens, cols), FLOAT), square, square, out((tokens, vd), FLOAT), token_out),
+        (k, v, states, gcol, grow, proj, halo_proj, taps),
+        [pltpu.VMEM((HALO + tokens, cols), FLOAT)],
+        after=(group_token,),
+    )
+    passed_sums, ffn_token = passed(ffn_sums, (*end_pieces[1:], slope_token))
     dproj, d_logit, logit_rows, taps_part, sums = run(
         partial(back_kernel, heads, chunks),
         back_shapes(heads, chunks),
-        (mine, far, *end_pieces, after, q, k, v, logits, gate_sums, gcol, grow, tri, states, vns, dos, dvns, es, n, proj, halo_proj, taps),
+        (mine, far, *end_pieces, after, q, k, logits, gate_sums, gcol, tri, states, vns, dos, dvns, es, n, proj, halo_proj, taps, *slopes),
         back_scratch(heads, chunks),
         scalars=1,
         after=(ffn_token,),
         micros=11.0,
         megs=30,
-    )
-    ffn_grad_out = out((hidden_cols, DK), FLOAT)
-    grad_gate, grad_up, grad_down, ffn_token = run(
-        ffn_unpack_kernel, (ffn_grad_out,) * 3 + (token_out,), second_round(passed_sums), after=(sums[:8],)
     )
     packed = 2 * vd + cols + EXTRA
     tile, half_tile = out((4, packed, DK), HALF), out((4, packed // 2, DK), HALF)
@@ -1266,10 +1327,15 @@
         (mine, first_normed, halo_normed, dproj, logit_rows, taps_part, gain_part, gate_gain, second_gain_part, first_row, in_rows, beta_rows, *mixer_parts),
         [pltpu.VMEM((cols + HALO, HALO + tokens), HALF), pltpu.VMEM((EXTRA, DK), FLOAT)],
         scalars=1,
-        after=(ffn_token,),
         micros=6.0,
         megs=16,
     )
+    ffn_grad_out = out((hidden_cols, DK), FLOAT)
+    grad_gate, grad_up, grad_down, ffn_token = run(
+        ffn_unpack_kernel, (ffn_grad_out,) * 3 + (token_out,), second_round(passed_sums), after=(in_token,)
+    )
+    in_ends, in_token = passed(in_parts[3:], (ffn_token,))
+    in_parts = in_parts[:3] + in_ends
     first_other, first_own, first_token = d_first_tiles(
         mine, dproj, d_gate_pre, d_logit, sums, in_rows, gate_rows, beta_rows, in_token
     )
@@ -1286,22 +1352,18 @@
         after=(first_token, out_token),
     )
     in_group = (in_parts[0], turned(plus, True, 1), turned(minus, True, -1))
-    first_sum = run(
-        tile_sum_kernel,
-        (out((4, tokens + 2 * HALO, width), HALF),),
-        (first_own, rotated(first_other, "c", 1)),
-        after=(in_token,),
-    )[0]
-    first_tiles = lax.all_to_all(first_sum, "x", 0, 0, tiled=True)
-    total, pack = run(
+    own_rows, plus_rows, minus_rows, gain_token = run(
+        quad_sum_kernel, (out((4, 8, DK), FLOAT),) * 3 + (token_out,), ring_pieces(rows_left, "x"), after=(in_token,)
+    )
+    total, pack, first_token = run(
         first_total_kernel,
-        (out((tokens + 2 * HALO, width), FLOAT), out((HALO + 8, width), FLOAT)),
-        (first_tiles,),
+        (out((tokens + 2 * HALO, width), FLOAT), out((HALO + 8, width), FLOAT), token_out),
+        head_halving(first_own, first_other, mine, (gain_token,)),
     )
     *sums_out, sum_token = run(
         last_sum_kernel,
         (out((packed, DK), FLOAT),) + (out((packed, DK), HALF),) * 3 + (token_out,),
-        (mine, *in_group, *gains_over_chips(rows_left)),
+        (mine, *in_group, own_rows, turned(plus_rows, True, 1), turned(minus_rows, True, -1)),
         scalars=1,
     )
     totals = [sums_out[0]] + [turned(sums_out[i], False, TURNS[i]) for i in range(1, 4)]

time: 309 us -> 293 us (0.948)
  the two profiles are of different devices: /device:TPU:1 before, /device:TPU:96 now
where the time goes in v1:
time: 293 us; the launch traced here: 289 us
  Pallas kernels  96.5 us (33%)
  waiting for transfers between devices  93.7 us (32%)
  starting transfers between devices  82.4 us (28%)
  local copies, waits for them, and re-layouts  7.97 us (3%)
  matrix products  6.11 us (2%)
    pallas_call x39, Pallas kernels, run(): pl.pallas_call(body, out_shape=tuple((pltpu.HBM(a.shape, a.dtype) if i in...  82.8 us
    ppermute x45, waiting for transfers between devices, rotated(): lax.ppermute(array, axis, [(i, (i + distance) % size) for i in range(size)])  69.2 us
    ppermute x45, starting transfers between devices, rotated(): lax.ppermute(array, axis, [(i, (i + distance) % size) for i in range(size)])  56.9 us
    ppermute x16, starting transfers between devices, turned(): return lax.ppermute(array, PLANE, pairs)  18.6 us
    ppermute x16, waiting for transfers between devices, turned(): return lax.ppermute(array, PLANE, pairs)  15.4 us
    unnamed x65, local copies, waits for them, and re-layouts  7.44 us
    pallas_call x1, Pallas kernels, d_first_tiles(): pl.pallas_call(d_first_kernel, grid_spec=spec, out_shape=(tiles, tiles, o...  7.18 us
    pallas_call x1, Pallas kernels, down_tiles(): pl.pallas_call(down_kernel, grid_spec=spec, out_shape=(tiles, tiles, out(...  5.91 us
  transfers between devices with their start and end apart: 65, of which 35 were waited for; matrix products, arithmetic and copies ran while one was open for 2% of the time, Pallas kernels for 23%

profile of v1, /device:TPU:96, one launch (start us, length us, event | category | flops | bytes accessed | tf_op | source)
XLA Modules:
  0.0 288.5 jit_solution(6202453122269497884)
XLA Ops:
  1.6 3.0 %collective-permute-start.2 = (bf16[512,256]{1,0:T(8,128)(2,1)}, bf16[512,256]{1,0:T(8,128)(2,1)S(1)}, u32[]{:S(2)}, u32[]{:S(2)}) collective-permute-start(bf16[512,256]{1,0:T(8,128)(2,1)} %refs_3_.3), channel_id=1, source_target_pairs={{0,4},{2,6},{4,0},{6,2},{1,5},{3,7},{5,1},{7,3},{8,12},{10,14},{12... | collective-permute-start | bytes 786440 | tf_op jit(solution)/shard_map/ppermute | solution.py:540
  5.2 2.6 collective-permute-start
  17.9 2.6 collective-permute-done.3.refs_4_
  23.0 2.6 collective-permute-start.4
  30.3 8.2 %shard_map.308 = (bf16[512,256]{1,0:T(8,128)(2,1)}, bf16[512,512]{1,0:T(8,128)(2,1)}, bf16[8,128,128]{2,1,0:T(8,128)(2,1)}, bf16[8,128,128]{2,1,0:T(8,128)(2,1)}...) custom-call(bf16[512,1024]{1,0:T(8,128)(2,1)S(1)} %convolution_conve, ...), custom_call_target="tpu_custom_call" | custom-call | flops 88000000 | tf_op jit(solution)/shard_map/pallas_call | solution.py:430
  44.3 4.2 %collective-permute-done.7.refs_4_ = bf16[2,144,384]{2,1,0:T(8,128)(2,1)S(1)} collective-permute-done((bf16[2,144,384]{2,1,0:T(8,128)(2,1)S(1)}, bf16[2,144,384]{2,1,0:T(8,128)(2,1)S(1)}, u32[]{:S(2)}, u32[]{:S(2)}) %collective-permute-start.7) | collective-permute-done | bytes 221216 | tf_op jit(solution)/shard_map/ppermute | solution.py:540
  52.8 3.3 %collective-permute-start.10 = (bf16[2,144,384]{2,1,0:T(8,128)(2,1)S(1)}, bf16[2,144,384]{2,1,0:T(8,128)(2,1)S(1)}, u32[]{:S(2)}, u32[]{:S(2)}) collective-permute-start(bf16[2,144,384]{2,1,0:T(8,128)(2,1)S(1)} %get-tuple-element.192.refs_1_), channel_id=1, source_target_pairs={{0,64},{32,96},{64,0},{96,32},{1,65},{33,97},{65,1},{97,33},{2,66}... | collective-permute-start | bytes 663560 | tf_op jit(solution)/shard_map/ppermute | solution.py:540
  66.0 5.7 %shard_map.311 = (bf16[8,128,256]{2,1,0:T(8,128)(2,1)}, bf16[8,128,256]{2,1,0:T(8,128)(2,1)}, f32[512,512]{1,0:T(8,128)}, bf16[512,512]{1,0:T(8,128)(2,1)S(1)}, ...) custom-call(s32[4]{0:T(128)S(1)} %pad_add_fusion.refs_0_.mine, ...), custom_call_target="tpu_custom_call" | custom-call | flops 44000000 | tf_op jit(solution)/shard_map/pallas_call | solution.py:430
  82.4 3.2 %collective-permute-done.12.refs_3_ = bf16[64,2048]{1,0:T(8,128)(2,1)S(1)} collective-permute-done((bf16[64,2048]{1,0:T(8,128)(2,1)S(1)}, bf16[64,2048]{1,0:T(8,128)(2,1)S(1)}, u32[]{:S(2)}, u32[]{:S(2)}) %collective-permute-start.12) | collective-permute-done | bytes 262176 | tf_op jit(solution)/shard_map/ppermute | solution.py:540
  85.5 4.9 %collective-permute-done.13.refs_4_ = bf16[64,2048]{1,0:T(8,128)(2,1)S(1)} collective-permute-done((bf16[64,2048]{1,0:T(8,128)(2,1)S(1)}, bf16[64,2048]{1,0:T(8,128)(2,1)S(1)}, u32[]{:S(2)}, u32[]{:S(2)}) %collective-permute-start.13) | collective-permute-done | bytes 262176 | tf_op jit(solution)/shard_map/ppermute | solution.py:540
  96.7 6.5 %collective-permute-done.21.refs_4_ = bf16[64,2048]{1,0:T(8,128)(2,1)S(1)} collective-permute-done((bf16[64,2048]{1,0:T(8,128)(2,1)S(1)}, bf16[64,2048]{1,0:T(8,128)(2,1)S(1)}, u32[]{:S(2)}, u32[]{:S(2)}) %collective-permute-start.21) | collective-permute-done | bytes 262176 | tf_op jit(solution)/shard_map/ppermute | solution.py:540
  103.1 4.2 %collective-permute-done.20.refs_3_ = bf16[64,2048]{1,0:T(8,128)(2,1)S(1)} collective-permute-done((bf16[64,2048]{1,0:T(8,128)(2,1)S(1)}, bf16[64,2048]{1,0:T(8,128)(2,1)S(1)}, u32[]{:S(2)}, u32[]{:S(2)}) %collective-permute-start.20) | collective-permute-done | bytes 262176 | tf_op jit(solution)/shard_map/ppermute | solution.py:540
  108.1 2.6 collective-permute-done.22.refs_2_
  110.7 8.3 %shard_map.318 = (bf16[512,2048]{1,0:T(8,128)(2,1)S(1)}, bf16[704,512]{1,0:T(8,128)(2,1)S(1)}, bf16[704,512]{1,0:T(8,128)(2,1)S(1)}, bf16[704,512]{1,0:T(8,128)(...) custom-call(s32[4]{0:T(128)S(1)} %pad_add_fusion.refs_0_.mine, ...), custom_call_target="tpu_custom_call" | custom-call | flops 99000000 | tf_op jit(solution)/shard_map/pallas_call | solution.py:430
  130.4 3.0 %shard_map.322 = (bf16[4,2112,128]{2,1,0:T(8,128)(2,1)S(1)}, bf16[4,2112,128]{2,1,0:T(8,128)(2,1)S(1)}, f32[8,128]{1,0:T(8,128)S(1)}) custom-call(s32[4]{0:T(128)S(1)} %pad_add_fusion.refs_0_.mine, bf16[512,2048]{1,0:T(8,128)(2,1)S(1)} %get-tuple-element.227.refs_1_, bf16[512,2048]{1,0:T(8,128)(2,1)S(1)} %get-tuple-element.228.refs_2_, ...), custom_call_target="tpu_custom_call" | custom-call | flops 11000000 | tf_op jit(solution)/shard_map/pallas_call | solution.py:430
  133.4 8.9 %collective-permute-done.25.refs_5_ = bf16[64,2048]{1,0:T(8,128)(2,1)S(1)} collective-permute-done((bf16[64,2048]{1,0:T(8,128)(2,1)S(1)}, bf16[64,2048]{1,0:T(8,128)(2,1)S(1)}, u32[]{:S(2)}, u32[]{:S(2)}) %collective-permute-start.25) | collective-permute-done | bytes 262176 | tf_op jit(solution)/shard_map/ppermute | solution.py:540
  151.2 5.9 %shard_map.319 = (bf16[4,512,256]{2,1,0:T(8,128)(2,1)}, bf16[4,512,256]{2,1,0:T(8,128)(2,1)S(1)}, f32[8,128]{1,0:T(8,128)S(1)}) custom-call(s32[4]{0:T(128)S(1)} %pad_add_fusion.refs_0_.mine, bf16[704,512]{1,0:T(8,128)(2,1)S(1)} %get-tuple-element.212.product.refs_5_, bf16[704,2048]{1,0:T(8,128)(2,1)S(1)} %bitcast.36, f32[64,2048]{1,0:T(8,128)S(1)} %get-tuple-element.213.hidden), custom_call_target="tpu_custom_call" | custom-call | flops 44000000 | tf_op jit(solution)/shard_map/pallas_call | solution.py:1029
  157.2 4.9 %collective-permute-done.29.refs_3_ = bf16[64,2048]{1,0:T(8,128)(2,1)S(1)} collective-permute-done((bf16[64,2048]{1,0:T(8,128)(2,1)S(1)}, bf16[64,2048]{1,0:T(8,128)(2,1)S(1)}, u32[]{:S(2)}, u32[]{:S(2)}) %collective-permute-start.29) | collective-permute-done | bytes 262176 | tf_op jit(solution)/shard_map/ppermute | solution.py:540
  163.3 2.6 collective-permute-done.33.refs_2_
  177.0 3.3 %shard_map.328 = (bf16[4,1024,128]{2,1,0:T(8,128)(2,1)S(1)}, bf16[4,1024,128]{2,1,0:T(8,128)(2,1)S(1)}, bf16[4,1024,128]{2,1,0:T(8,128)(2,1)S(1)}, bf16[4,1024,128]{2,1,0:T(8,128)(2,1)S(1)}, f32[1,2048]{1,0:T(1,128)S(1)}) custom-call(s32[4]{0:T(128)S(1)} %pad_add_fusion.refs_0_.mine, bf16[512,2048]{1,0:T(8,128)(2,1)S(1)} %get-tuple-element.242.refs_1_, ...), custom_call_target="tpu_custom_call" | custom-call | flops 55000000 | tf_op jit(solution)/shard_map/pallas_call | solution.py:430
  193.1 3.2 %collective-permute-start.43 = (bf16[2112,128]{1,0:T(8,128)(2,1)}, bf16[2112,128]{1,0:T(8,128)(2,1)S(1)}, u32[]{:S(2)}, u32[]{:S(2)}) collective-permute-start(bf16[2112,128]{1,0:T(8,128)(2,1)} %get-tuple-element.286), channel_id=1, source_target_pairs={{0,96},{1,25},{8,104},{9,1},{16,112},{17,9},{24,120},{25,17},{32,0... | collective-permute-start | bytes 1622024 | tf_op jit(solution)/shard_map/ppermute | solution.py:571
  196.6 7.9 %shard_map.334 = (bf16[528,1024]{1,0:T(8,128)(2,1)S(1)}, f32[512,2]{1,0:T(8,128)S(1)}, f32[16,528]{1,0:T(8,128)S(1)}, f32[8,1024]{1,0:T(8,128)S(1)}, f32[528,1]{1,0:T(8,128)S(1)}) custom-call(s32[4]{0:T(128)S(1)} %pad_add_fusion.refs_0_.mine, bf16[4,2,144,384]{3,2,1,0:T(8,128)(2,1)S(1)} %copy-done.15, bf16[2,128,256]{2,1,0:T(8,128)(2,1)S(1)} %get-tuple-element.253.refs_2_, ...), custom_call_target="tpu_custom_call" | custom-call | flops 121000000 | tf_op jit(solution)/shard_map/pallas_call | solution.py:430
  204.5 4.6 %shard_map.335 = (bf16[4,2112,128]{2,1,0:T(8,128)(2,1)S(1)}, bf16[4,2112,128]{2,1,0:T(8,128)(2,1)S(1)}, bf16[4,2112,128]{2,1,0:T(8,128)(2,1)S(1)}, bf16[4,1056,1...) custom-call(s32[4]{0:T(128)S(1)} %pad_add_fusion.refs_0_.mine, ...), custom_call_target="tpu_custom_call" | custom-call | flops 66000000 | tf_op jit(solution)/shard_map/pallas_call | solution.py:430
  215.9 2.7 collective-permute-start.46
  219.7 7.2 %shard_map.340 = (bf16[4,544,256]{2,1,0:T(8,128)(2,1)S(1)}, bf16[4,544,256]{2,1,0:T(8,128)(2,1)S(1)}, f32[8,128]{1,0:T(8,128)S(1)}) custom-call(s32[4]{0:T(128)S(1)} %pad_add_fusion.refs_0_.mine, bf16[528,1024]{1,0:T(8,128)(2,1)S(1)} %get-tuple-element.273.refs_3_.dproj, bf16[512,512]{1,0:T(8,128)(2,1)S(1)} %get-tuple-element.246.refs_4_.d_pre, ...), custom_call_target="tpu_custom_call" | custom-call | flops 66000000 | tf_op jit(solution)/shard_map/pallas_call | solution.py:1084
  226.9 3.7 %collective-permute-done.46.refs_2_ = bf16[512,256]{1,0:T(8,128)(2,1)S(1)} collective-permute-done((bf16[512,256]{1,0:T(8,128)(2,1)S(1)}, bf16[512,256]{1,0:T(8,128)(2,1)S(1)}, u32[]{:S(2)}, u32[]{:S(2)}) %collective-permute-start.46) | collective-permute-done | bytes 262176 | tf_op jit(solution)/shard_map/ppermute | solution.py:540
  237.1 2.8 collective-permute-start.52
  239.9 3.0 %collective-permute-done.53.refs_3_ = f32[3,4,8,128]{3,2,1,0:T(8,128)S(1)} collective-permute-done((f32[3,4,8,128]{3,2,1,0:T(8,128)S(1)}, f32[3,4,8,128]{3,2,1,0:T(8,128)S(1)}, u32[]{:S(2)}, u32[]{:S(2)}) %collective-permute-start.53) | collective-permute-done | bytes 49184 | tf_op jit(solution)/shard_map/ppermute | solution.py:540
  251.5 9.7 %collective-permute-done.59.refs_5_ = f32[4,8,128]{2,1,0:T(8,128)S(1)} collective-permute-done((f32[4,8,128]{2,1,0:T(8,128)S(1)}, f32[4,8,128]{2,1,0:T(8,128)S(1)}, u32[]{:S(2)}, u32[]{:S(2)}) %collective-permute-start.59) | collective-permute-done | bytes 16416 | tf_op jit(solution)/shard_map/ppermute | solution.py:571
  261.3 2.9 %collective-permute-done.60.refs_6_ = f32[4,8,128]{2,1,0:T(8,128)S(1)} collective-permute-done((f32[4,8,128]{2,1,0:T(8,128)S(1)}, f32[4,8,128]{2,1,0:T(8,128)S(1)}, u32[]{:S(2)}, u32[]{:S(2)}) %collective-permute-start.60) | collective-permute-done | bytes 16416 | tf_op jit(solution)/shard_map/ppermute | solution.py:571
  266.2 2.7 collective-permute-start.62
  272.0 5.4 %collective-permute-done.55.refs_1_ = bf16[544,256]{1,0:T(8,128)(2,1)S(1)} collective-permute-done((bf16[544,256]{1,0:T(8,128)(2,1)S(1)}, bf16[544,256]{1,0:T(8,128)(2,1)S(1)}, u32[]{:S(2)}, u32[]{:S(2)}) %collective-permute-start.55) | collective-permute-done | bytes 278560 | tf_op jit(solution)/shard_map/ppermute | solution.py:710
  (218 shorter events, 140.1 us)
Async XLA Ops:
  1.6 14.7 %collective-permute-start.2 = (bf16[512,256]{1,0:T(8,128)(2,1)}, bf16[512,256]{1,0:T(8,128)(2,1)S(1)}, u32[]{:S(2)}, u32[]{:S(2)}) collective-permute-start(bf16[512,256]{1,0:T(8,128)(2,1)} %refs_3_.3), channel_id=1, source_target_pairs={{0,4},{2,6},{4,0},{6,2},{1,5},{3,7},{5,1},{7,3},{8,12},{10,14},{12... | collective-permute-start | bytes 786440 | tf_op jit(solution)/shard_map/ppermute | solution.py:540
  4.6 12.4 %collective-permute-start.1 = (bf16[512,256]{1,0:T(8,128)(2,1)}, bf16[512,256]{1,0:T(8,128)(2,1)S(1)}, u32[]{:S(2)}, u32[]{:S(2)}) collective-permute-start(bf16[512,256]{1,0:T(8,128)(2,1)} %refs_3_.3), channel_id=1, source_target_pairs={{0,2},{2,4},{4,6},{6,0},{1,3},{3,5},{5,7},{7,1},{8,10},{10,12},{12... | collective-permute-start | bytes 786440 | tf_op jit(solution)/shard_map/ppermute | solution.py:540
  77.1 13.3 %collective-permute-start.13 = (bf16[64,2048]{1,0:T(8,128)(2,1)S(1)}, bf16[64,2048]{1,0:T(8,128)(2,1)S(1)}, u32[]{:S(2)}, u32[]{:S(2)}) collective-permute-start(bf16[64,2048]{1,0:T(8,128)(2,1)S(1)} %get-tuple-element.204), channel_id=1, source_target_pairs={{0,6},{2,0},{4,2},{6,4},{1,7},{3,1},{5,3},{7,5},{8,14},{10,8},{12,... | collective-permute-start | bytes 786440 | tf_op jit(solution)/shard_map/ppermute | solution.py:540
  78.9 13.1 %collective-permute-start.14 = (bf16[64,2048]{1,0:T(8,128)(2,1)S(1)}, bf16[64,2048]{1,0:T(8,128)(2,1)S(1)}, u32[]{:S(2)}, u32[]{:S(2)}) collective-permute-start(bf16[64,2048]{1,0:T(8,128)(2,1)S(1)} %get-tuple-element.205), channel_id=1, source_target_pairs={{0,4},{2,6},{4,0},{6,2},{1,5},{3,7},{5,1},{7,3},{8,12},{10,14},{12... | collective-permute-start | bytes 786440 | tf_op jit(solution)/shard_map/ppermute | solution.py:540
  93.3 14.1 %collective-permute-start.20 = (bf16[64,2048]{1,0:T(8,128)(2,1)S(1)}, bf16[64,2048]{1,0:T(8,128)(2,1)S(1)}, u32[]{:S(2)}, u32[]{:S(2)}) collective-permute-start(bf16[64,2048]{1,0:T(8,128)(2,1)S(1)} %get-tuple-element.210.refs_1_), channel_id=1, source_target_pairs={{0,2},{2,4},{4,6},{6,0},{1,3},{3,5},{5,7},{7,1},{8,10},{10,12},{12... | collective-permute-start | bytes 786440 | tf_op jit(solution)/shard_map/ppermute | solution.py:540
  95.3 12.0 %collective-permute-start.19 = (bf16[64,2048]{1,0:T(8,128)(2,1)S(1)}, bf16[64,2048]{1,0:T(8,128)(2,1)S(1)}, u32[]{:S(2)}, u32[]{:S(2)}) collective-permute-start(bf16[64,2048]{1,0:T(8,128)(2,1)S(1)} %get-tuple-element.210.refs_1_), channel_id=1, source_target_pairs={{0,6},{2,0},{4,2},{6,4},{1,7},{3,1},{5,3},{7,5},{8,14},{10,8},{12,... | collective-permute-start | bytes 786440 | tf_op jit(solution)/shard_map/ppermute | solution.py:540
  124.4 18.4 %collective-permute-start.31 = (bf16[4,1056,128]{2,1,0:T(8,128)(2,1)S(1)}, bf16[4,1056,128]{2,1,0:T(8,128)(2,1)S(1)}, u32[]{:S(2)}, u32[]{:S(2)}) collective-permute-start(bf16[4,1056,128]{2,1,0:T(8,128)(2,1)S(1)} %get-tuple-element.238), channel_id=1, source_target_pairs={{0,8},{1,33},{8,16},{9,41},{16,24},{17,49},{24,0},{25,57},{32,40},... | collective-permute-start | bytes 3244040 | tf_op jit(solution)/shard_map/ppermute | solution.py:571
  126.4 16.4 %collective-permute-start.32 = (bf16[4,1056,128]{2,1,0:T(8,128)(2,1)S(1)}, bf16[4,1056,128]{2,1,0:T(8,128)(2,1)S(1)}, u32[]{:S(2)}, u32[]{:S(2)}) collective-permute-start(bf16[4,1056,128]{2,1,0:T(8,128)(2,1)S(1)} %get-tuple-element.239), channel_id=1, source_target_pairs={{0,24},{1,97},{8,0},{9,105},{16,8},{17,113},{24,16},{25,121},{32,5... | collective-permute-start | bytes 3244040 | tf_op jit(solution)/shard_map/ppermute | solution.py:571
  126.5 15.8 %collective-permute-start.25 = (bf16[64,2048]{1,0:T(8,128)(2,1)S(1)}, bf16[64,2048]{1,0:T(8,128)(2,1)S(1)}, u32[]{:S(2)}, u32[]{:S(2)}) collective-permute-start(bf16[64,2048]{1,0:T(8,128)(2,1)S(1)} %get-tuple-element.224), channel_id=1, source_target_pairs={{0,2},{2,4},{4,6},{6,0},{1,3},{3,5},{5,7},{7,1},{8,10},{10,12},{12... | collective-permute-start | bytes 786440 | tf_op jit(solution)/shard_map/ppermute | solution.py:540
  127.3 15.0 %collective-permute-start.26 = (bf16[64,2048]{1,0:T(8,128)(2,1)S(1)}, bf16[64,2048]{1,0:T(8,128)(2,1)S(1)}, u32[]{:S(2)}, u32[]{:S(2)}) collective-permute-start(bf16[64,2048]{1,0:T(8,128)(2,1)S(1)} %get-tuple-element.225), channel_id=1, source_target_pairs={{0,6},{2,0},{4,2},{6,4},{1,7},{3,1},{5,3},{7,5},{8,14},{10,8},{12,... | collective-permute-start | bytes 786440 | tf_op jit(solution)/shard_map/ppermute | solution.py:540
  129.7 12.6 %collective-permute-start.27 = (bf16[64,2048]{1,0:T(8,128)(2,1)S(1)}, bf16[64,2048]{1,0:T(8,128)(2,1)S(1)}, u32[]{:S(2)}, u32[]{:S(2)}) collective-permute-start(bf16[64,2048]{1,0:T(8,128)(2,1)S(1)} %get-tuple-element.226), channel_id=1, source_target_pairs={{0,4},{2,6},{4,0},{6,2},{1,5},{3,7},{5,1},{7,3},{8,12},{10,14},{12... | collective-permute-start | bytes 786440 | tf_op jit(solution)/shard_map/ppermute | solution.py:540
  144.5 35.7 %collective-permute-start.37 = (bf16[4,2112,128]{2,1,0:T(8,128)(2,1)S(1)}, bf16[4,2112,128]{2,1,0:T(8,128)(2,1)S(1)}, u32[]{:S(2)}, u32[]{:S(2)}) collective-permute-start(bf16[4,2112,128]{2,1,0:T(8,128)(2,1)S(1)} %get-tuple-element.250), channel_id=1, source_target_pairs={{0,8},{1,33},{8,16},{9,41},{16,24},{17,49},{24,0},{25,57},{32,40},... | collective-permute-start | bytes 6488072 | tf_op jit(solution)/shard_map/ppermute | solution.py:571
  146.5 33.7 %collective-permute-start.38 = (bf16[4,2112,128]{2,1,0:T(8,128)(2,1)}, bf16[4,2112,128]{2,1,0:T(8,128)(2,1)S(1)}, u32[]{:S(2)}, u32[]{:S(2)}) collective-permute-start(bf16[4,2112,128]{2,1,0:T(8,128)(2,1)} %get-tuple-element.251), channel_id=1, source_target_pairs={{0,24},{1,97},{8,0},{9,105},{16,8},{17,113},{24,16},{25,121},{32,5... | collective-permute-start | bytes 6488072 | tf_op jit(solution)/shard_map/ppermute | solution.py:571
  148.0 14.2 %collective-permute-start.29 = (bf16[64,2048]{1,0:T(8,128)(2,1)S(1)}, bf16[64,2048]{1,0:T(8,128)(2,1)S(1)}, u32[]{:S(2)}, u32[]{:S(2)}) collective-permute-start(bf16[64,2048]{1,0:T(8,128)(2,1)S(1)} %get-tuple-element.234.refs_1_), channel_id=1, source_target_pairs={{0,2},{2,4},{4,6},{6,0},{1,3},{3,5},{5,7},{7,1},{8,10},{10,12},{12... | collective-permute-start | bytes 786440 | tf_op jit(solution)/shard_map/ppermute | solution.py:540
  150.3 12.2 %collective-permute-start.28 = (bf16[64,2048]{1,0:T(8,128)(2,1)S(1)}, bf16[64,2048]{1,0:T(8,128)(2,1)S(1)}, u32[]{:S(2)}, u32[]{:S(2)}) collective-permute-start(bf16[64,2048]{1,0:T(8,128)(2,1)S(1)} %get-tuple-element.234.refs_1_), channel_id=1, source_target_pairs={{0,6},{2,0},{4,2},{6,4},{1,7},{3,1},{5,3},{7,5},{8,14},{10,8},{12,... | collective-permute-start | bytes 786440 | tf_op jit(solution)/shard_map/ppermute | solution.py:540
  169.9 12.7 %collective-permute-start.36 = (bf16[2,128,256]{2,1,0:T(8,128)(2,1)S(1)}, bf16[2,128,256]{2,1,0:T(8,128)(2,1)S(1)}, u32[]{:S(2)}, u32[]{:S(2)}) collective-permute-start(bf16[2,128,256]{2,1,0:T(8,128)(2,1)S(1)} %get-tuple-element.244.refs_2_), channel_id=1, source_target_pairs={{0,16},{8,24},{16,0},{24,8},{1,17},{9,25},{17,1},{25,9},{2,18},{10... | collective-permute-start | bytes 393224 | tf_op jit(solution)/shard_map/ppermute | solution.py:540
  193.1 16.6 %collective-permute-start.42 = (bf16[2112,128]{1,0:T(8,128)(2,1)}, bf16[2112,128]{1,0:T(8,128)(2,1)S(1)}, u32[]{:S(2)}, u32[]{:S(2)}) collective-permute-start(bf16[2112,128]{1,0:T(8,128)(2,1)} %get-tuple-element.285), channel_id=1, source_target_pairs={{0,32},{1,9},{8,40},{9,17},{16,48},{17,25},{24,56},{25,1},{32,64},... | collective-permute-start | bytes 1622024 | tf_op jit(solution)/shard_map/ppermute | solution.py:571
  193.1 16.6 %collective-permute-start.43 = (bf16[2112,128]{1,0:T(8,128)(2,1)}, bf16[2112,128]{1,0:T(8,128)(2,1)S(1)}, u32[]{:S(2)}, u32[]{:S(2)}) collective-permute-start(bf16[2112,128]{1,0:T(8,128)(2,1)} %get-tuple-element.286), channel_id=1, source_target_pairs={{0,96},{1,25},{8,104},{9,1},{16,112},{17,9},{24,120},{25,17},{32,0... | collective-permute-start | bytes 1622024 | tf_op jit(solution)/shard_map/ppermute | solution.py:571
  196.4 13.3 %collective-permute-start.44 = (bf16[2112,128]{1,0:T(8,128)(2,1)}, bf16[2112,128]{1,0:T(8,128)(2,1)}, u32[]{:S(2)}, u32[]{:S(2)}) collective-permute-start(bf16[2112,128]{1,0:T(8,128)(2,1)} %get-tuple-element.287), channel_id=1, source_target_pairs={{0,64},{1,17},{8,72},{9,25},{16,80},{17,1},{24,88},{25,9},{32,96},... | collective-permute-start | bytes 1622024 | tf_op jit(solution)/shard_map/ppermute | solution.py:571
  196.4 17.8 %collective-permute-start.23 = (bf16[4,512,256]{2,1,0:T(8,128)(2,1)}, bf16[4,512,256]{2,1,0:T(8,128)(2,1)S(1)}, u32[]{:S(2)}, u32[]{:S(2)}) collective-permute-start(bf16[4,512,256]{2,1,0:T(8,128)(2,1)} %get-tuple-element.215), channel_id=1, source_target_pairs={{0,1},{1,0},{2,3},{3,2},{4,5},{5,4},{6,7},{7,6},{8,9},{9,8},{10,11... | collective-permute-start | bytes 3145736 | tf_op jit(solution)/shard_map/ppermute | solution.py:540
  211.8 21.2 %collective-permute-start.49 = (bf16[4,1056,128]{2,1,0:T(8,128)(2,1)S(1)}, bf16[4,1056,128]{2,1,0:T(8,128)(2,1)S(1)}, u32[]{:S(2)}, u32[]{:S(2)}) collective-permute-start(bf16[4,1056,128]{2,1,0:T(8,128)(2,1)S(1)} %get-tuple-element.303), channel_id=1, source_target_pairs={{0,8},{1,33},{8,16},{9,41},{16,24},{17,49},{24,0},{25,57},{32,40},... | collective-permute-start | bytes 3244040 | tf_op jit(solution)/shard_map/ppermute | solution.py:571
  214.1 18.9 %collective-permute-start.50 = (bf16[4,1056,128]{2,1,0:T(8,128)(2,1)S(1)}, bf16[4,1056,128]{2,1,0:T(8,128)(2,1)S(1)}, u32[]{:S(2)}, u32[]{:S(2)}) collective-permute-start(bf16[4,1056,128]{2,1,0:T(8,128)(2,1)S(1)} %get-tuple-element.304), channel_id=1, source_target_pairs={{0,24},{1,97},{8,0},{9,105},{16,8},{17,113},{24,16},{25,121},{32,5... | collective-permute-start | bytes 3244040 | tf_op jit(solution)/shard_map/ppermute | solution.py:571
  215.9 14.7 %collective-permute-start.46 = (bf16[512,256]{1,0:T(8,128)(2,1)S(1)}, bf16[512,256]{1,0:T(8,128)(2,1)S(1)}, u32[]{:S(2)}, u32[]{:S(2)}) collective-permute-start(bf16[512,256]{1,0:T(8,128)(2,1)S(1)} %get-tuple-element.293), channel_id=1, source_target_pairs={{0,6},{2,0},{4,2},{6,4},{1,7},{3,1},{5,3},{7,5},{8,14},{10,8},{12,... | collective-permute-start | bytes 786440 | tf_op jit(solution)/shard_map/ppermute | solution.py:540
  218.6 13.6 %collective-permute-start.47 = (bf16[512,256]{1,0:T(8,128)(2,1)S(1)}, bf16[512,256]{1,0:T(8,128)(2,1)S(1)}, u32[]{:S(2)}, u32[]{:S(2)}) collective-permute-start(bf16[512,256]{1,0:T(8,128)(2,1)S(1)} %get-tuple-element.294), channel_id=1, source_target_pairs={{0,4},{2,6},{4,0},{6,2},{1,5},{3,7},{5,1},{7,3},{8,12},{10,14},{12... | collective-permute-start | bytes 786440 | tf_op jit(solution)/shard_map/ppermute | solution.py:540
  234.3 29.9 %collective-permute-start.57 = (bf16[4,2112,128]{2,1,0:T(8,128)(2,1)S(1)}, bf16[4,2112,128]{2,1,0:T(8,128)(2,1)S(1)}, u32[]{:S(2)}, u32[]{:S(2)}) collective-permute-start(bf16[4,2112,128]{2,1,0:T(8,128)(2,1)S(1)} %get-tuple-element.318), channel_id=1, source_target_pairs={{0,8},{1,33},{8,16},{9,41},{16,24},{17,49},{24,0},{25,57},{32,40},... | collective-permute-start | bytes 6488072 | tf_op jit(solution)/shard_map/ppermute | solution.py:571
  236.1 28.1 %collective-permute-start.58 = (bf16[4,2112,128]{2,1,0:T(8,128)(2,1)S(1)}, bf16[4,2112,128]{2,1,0:T(8,128)(2,1)S(1)}, u32[]{:S(2)}, u32[]{:S(2)}) collective-permute-start(bf16[4,2112,128]{2,1,0:T(8,128)(2,1)S(1)} %get-tuple-element.319), channel_id=1, source_target_pairs={{0,24},{1,97},{8,0},{9,105},{16,8},{17,113},{24,16},{25,121},{32,5... | collective-permute-start | bytes 6488072 | tf_op jit(solution)/shard_map/ppermute | solution.py:571
  247.8 22.2 %collective-permute-start.54 = (bf16[2,544,256]{2,1,0:T(8,128)(2,1)S(1)}, bf16[2,544,256]{2,1,0:T(8,128)(2,1)S(1)}, u32[]{:S(2)}, u32[]{:S(2)}) collective-permute-start(bf16[2,544,256]{2,1,0:T(8,128)(2,1)S(1)} %get-tuple-element.311), channel_id=1, source_target_pairs={{0,4},{2,6},{4,0},{6,2},{1,5},{3,7},{5,1},{7,3},{8,12},{10,14},{12... | collective-permute-start | bytes 1671176 | tf_op jit(solution)/shard_map/ppermute | solution.py:710
  249.0 12.2 %collective-permute-start.59 = (f32[4,8,128]{2,1,0:T(8,128)S(1)}, f32[4,8,128]{2,1,0:T(8,128)S(1)}, u32[]{:S(2)}, u32[]{:S(2)}) collective-permute-start(f32[4,8,128]{2,1,0:T(8,128)S(1)} %get-tuple-element.321), channel_id=1, source_target_pairs={{0,8},{1,33},{8,16},{9,41},{16,24},{17,49},{24,0},{25,57},{32,40},... | collective-permute-start | bytes 49160 | tf_op jit(solution)/shard_map/ppermute | solution.py:571
  251.5 12.7 %collective-permute-start.60 = (f32[4,8,128]{2,1,0:T(8,128)S(1)}, f32[4,8,128]{2,1,0:T(8,128)S(1)}, u32[]{:S(2)}, u32[]{:S(2)}) collective-permute-start(f32[4,8,128]{2,1,0:T(8,128)S(1)} %get-tuple-element.322), channel_id=1, source_target_pairs={{0,24},{1,97},{8,0},{9,105},{16,8},{17,113},{24,16},{25,121},{32,5... | collective-permute-start | bytes 49160 | tf_op jit(solution)/shard_map/ppermute | solution.py:571
  265.7 16.4 %collective-permute-start.61 = (bf16[2112,128]{1,0:T(8,128)(2,1)S(1)}, bf16[2112,128]{1,0:T(8,128)(2,1)S(1)}, u32[]{:S(2)}, u32[]{:S(2)}) collective-permute-start(bf16[2112,128]{1,0:T(8,128)(2,1)S(1)} %get-tuple-element.324), channel_id=1, source_target_pairs={{0,32},{1,9},{8,40},{9,17},{16,48},{17,25},{24,56},{25,1},{32,64},... | collective-permute-start | bytes 1622024 | tf_op jit(solution)/shard_map/ppermute | solution.py:571
  266.2 15.8 %collective-permute-start.62 = (bf16[2112,128]{1,0:T(8,128)(2,1)S(1)}, bf16[2112,128]{1,0:T(8,128)(2,1)S(1)}, u32[]{:S(2)}, u32[]{:S(2)}) collective-permute-start(bf16[2112,128]{1,0:T(8,128)(2,1)S(1)} %get-tuple-element.325), channel_id=1, source_target_pairs={{0,96},{1,25},{8,104},{9,1},{16,112},{17,9},{24,120},{25,17},{32,0... | collective-permute-start | bytes 1622024 | tf_op jit(solution)/shard_map/ppermute | solution.py:571
  269.0 13.1 %collective-permute-start.63 = (bf16[2112,128]{1,0:T(8,128)(2,1)S(1)}, bf16[2112,128]{1,0:T(8,128)(2,1)S(1)}, u32[]{:S(2)}, u32[]{:S(2)}) collective-permute-start(bf16[2112,128]{1,0:T(8,128)(2,1)S(1)} %get-tuple-element.326), channel_id=1, source_target_pairs={{0,64},{1,17},{8,72},{9,25},{16,80},{17,1},{24,88},{25,9},{32,96},... | collective-permute-start | bytes 1622024 | tf_op jit(solution)/shard_map/ppermute | solution.py:571
  (65 other events, 573.1 us)

commit v2 on v1

--- a/solution.py
+++ b/solution.py
@@ -314,7 +314,7 @@
             rest[span, vl] = v[span, vl].astype(FLOAT) - jnp.exp(g) * mm(key, states[at])
 
 
-def back_kernel(heads, chunks, mine, pay, p0, p1, p2, p3, after, q, k, logits, gate_sums, gcol, tri, states, vns, dos, dvns, es, ns, proj, halo, taps, slopes, inner_in, spread_in, rest, dproj_out, dlogit_out, logit_rows, dtaps_out, sums_out, wide, dconv, late, rowsum):
+def back_kernel(heads, chunks, mine, pay, p0, p1, p2, p3, after, q, k, logits, gate_sums, gcol, tri, states, vns, dos, dvns, es, ns, proj, halo, taps, slopes, inner_in, spread_in, rest, dproj_out, halo_out, dlogit_out, logit_rows, dtaps_out, sums_out, wide, dconv, late, rowsum):
     ranks = pay.shape[0]
     tokens = chunks * CH
     me = mine[2]
@@ -406,6 +406,7 @@
             total = total + dconv[3 - j : 3 - j + HALO + tokens, lanes] * taps[j : j + 1, lanes]
         small = total.astype(HALF)
         dproj_out[:, lanes] = small
+        halo_out[:, lanes] = small[:HALO]
         rowsum[...] += jnp.sum(small.astype(FLOAT) * wide[:, lanes], axis=-1, keepdims=True)
     sums_out[HALO:, :] += rowsum[HALO:, :]
     sums_out[:HALO, :] = rowsum[:HALO, :]
@@ -501,6 +502,7 @@
     width = heads * (2 * DK + DV)
     return (
         out((HALO + tokens, width), HALF),
+        out((HALO, width), HALF),
         out((tokens, heads), FLOAT),
         out((HALO, HALO + tokens), FLOAT),
         out((8, width), FLOAT),
@@ -558,6 +560,10 @@
 def head_tiles(mine, own, other):
     core = mine[1]
     return [(2 * x + which, ref, x) for which, ref in ((core, own), (1 - core, other)) for x in range(4)]
+
+
+def copy_kernel(source, target):
+    target[...] = source[...]
 
 
 def turned(array, first, distance):
@@ -710,29 +716,41 @@
     return lax.ppermute(array, "x", [(i, i ^ mask) for i in range(4)])
 
 
-def first_half_kernel(mine, own, arrived, keep, send):
+def first_half_kernel(mine, own, arrived, keep, send, token):
+    token[...] = jnp.zeros(token.shape, FLOAT)
     base = jnp.where(mine[0] < 2, 0, 2)
     for target, at in ((keep, base), (send, 2 - base)):
         for i in range(2):
             target[i] = (own[at + i].astype(FLOAT) + arrived[at + i].astype(FLOAT)).astype(target.dtype)
 
 
-def second_half_kernel(mine, keep, arrived, own, send):
+def second_half_kernel(mine, keep, arrived, own, send, token):
+    token[...] = jnp.zeros(token.shape, FLOAT)
     at = lax.rem(mine[0], 2)
     own[...] = keep[at].astype(FLOAT) + arrived[at].astype(FLOAT)
     send[...] = (keep[1 - at].astype(FLOAT) + arrived[1 - at].astype(FLOAT)).astype(HALF)
 
 
-def head_halving(own, other, mine, after):
-    shape = own.shape[1:]
-    pair = out((2, *shape), HALF)
-    keep, send = run(
-        first_half_kernel, (pair, pair), (mine, own, rotated(other, "c", 1)), scalars=1, after=after
-    )
-    total, send = run(
-        second_half_kernel, (out(shape, FLOAT), out(shape, HALF)), (mine, keep, swapped(send, 2)), scalars=1
-    )
-    return [total, swapped(send, 1)]
+def first_halves(own, other, mine, after):
+    pair = out((2, *own.shape[1:]), HALF)
+    return run(
+        first_half_kernel,
+        (pair, pair, out((8, DK), FLOAT)),
+        (mine, own, rotated(other, "c", 1)),
+        scalars=1,
+        after=after,
+    )
+
+
+def second_halves(keep, arrived, mine, after):
+    shape = keep.shape[1:]
+    return run(
+        second_half_kernel,
+        (out(shape, FLOAT), out(shape, HALF), out((8, DK), FLOAT)),
+        (mine, keep, arrived),
+        scalars=1,
+        after=after,
+    )
 
 
 def added(parts):
@@ -776,7 +794,7 @@
 
 
 def in_grad_kernel(mine, normed, halo, dproj, d_logit, taps, mixer_gain, gate_gain, second_gain, first_gain, in_rows, beta_rows, *refs):
-    early, outs, (token, turned_refs, extra) = refs[:4], refs[4:9], refs[9:]
+    early, outs, (token, gains, turned_refs, extra) = refs[:4], refs[4:9], refs[9:]
     token[...] = jnp.zeros(token.shape, FLOAT)
     cols = dproj.shape[1]
     heads = 2
@@ -805,8 +823,8 @@
                     + gate_gain[:, at]
                 )
                 extra[36 : 36 + heads, :] = beta
-                extra[40:41, :] = gain / first_gain[:, at]
-                extra[41:42, :] = second_gain[:, at]
+                gains[0:1, at] = gain / first_gain[:, at]
+                gains[1:2, at] = second_gain[:, at]
                 store_tile(
                     outs, k, o + i, early[k][o + i], jnp.concatenate([grads[:cols, half], extra[...]], axis=0).astype(HALF)
                 )
@@ -850,6 +868,36 @@
         scalars=1,
         after=(after,),
     )
+
+
+def put_gains_kernel(mine, gains, arrived, *refs):
+    outs, token = refs[-6:-1], refs[-1]
+    token[...] = jnp.zeros(token.shape, FLOAT)
+    count = outs[0].shape[1] - EXTRA + 32
+    for k in range(4):
+        target, rows = (outs[k], count) if k < 3 else (outs[4], count - outs[3].shape[1])
+        here = slice(rows, rows + 16)
+        for o in range(4):
+            old = target[o, here, :].astype(FLOAT)
+            lanes = lane_block(dest_block(mine, k, o), DK)
+            new = gains[:, lanes] + arrived[:, lanes]
+            target[o, here, :] = jnp.concatenate([old[:8], new, old[10:]], axis=0).astype(HALF)
+
+
+def with_gains(mine, parts, gains, arrived, after):
+    vmem = pl.BlockSpec(memory_space=pltpu.VMEM)
+    *parts, token = pl.pallas_call(
+        put_gains_kernel,
+        out_shape=tuple(out(a.shape, a.dtype) for a in parts) + (out((8, DK), FLOAT),),
+        in_specs=[pl.BlockSpec(memory_space=pltpu.SMEM)]
+        + [vmem] * 7
+        + [pl.BlockSpec(memory_space=pl.ANY)] * len(after),
+        out_specs=[vmem] * 6,
+        input_output_aliases={3 + i: i for i in range(5)},
+        compiler_params=pltpu.CompilerParams(vmem_limit_bytes=4 * 2**20),
+        cost_estimate=cost(0.3),
+    )(mine, gains, arrived, *parts, *after)
+    return parts, token
 
 
 def gain_rows(ref):
@@ -969,11 +1017,9 @@
         )
 
 
-def output_kernel(own, first, second, third, total, token):
-    token[...] = jnp.zeros(token.shape, FLOAT)
-    total[...] = (
-        own[...] + first[...].astype(FLOAT) + second[...].astype(FLOAT) + third[...].astype(FLOAT)
-    ).astype(HALF)
+def output_kernel(own, arrived, total, token):
+    token[...] = jnp.zeros(token.shape, FLOAT)
+    total[...] = (own[...] + arrived[...].astype(FLOAT)).astype(HALF)
 
 
 def tile_of(i, mine):
@@ -1035,38 +1081,40 @@
     )(mine, product, weight, hidden)
 
 
-def d_first_kernel(mine, dproj, d_pre, d_logit, sums, in_rows, gate_rows, beta_rows, after, other, own, token, sum_rows):
+def d_first_kernel(mine, dproj, arrived, proj, d_pre, d_logit, sums, in_rows, gate_rows, beta_rows, after, other, own, token, scratch, sum_rows):
     step = pl.program_id(0)
     tokens = d_pre.shape[0]
     width = own.shape[2]
 
     @pl.when(step == 0)
     def _():
-        row = jnp.broadcast_to(sums[HALO:, :], (tokens, DK)).T
+        scratch[: tokens - HALO, :] = dproj[HALO:tokens, :]
+        extra = arrived[...].astype(FLOAT)
+        scratch[tokens - HALO :, :] = (dproj[tokens:, :].astype(FLOAT) + extra).astype(HALF)
+        late = jnp.sum(extra * proj[tokens - HALO :, :].astype(FLOAT), axis=-1, keepdims=True)
+        column = jnp.concatenate([sums[HALO:tokens, :], sums[tokens:, :] + late], axis=0)
+        row = jnp.broadcast_to(column, (tokens, DK)).T
         sum_rows[...] = jnp.zeros(sum_rows.shape, FLOAT)
         for i in range(tokens // width):
             sum_rows[i : i + 1, :] = row[0:1, i * width : (i + 1) * width]
-        sum_rows[2:3, 0:HALO] = jnp.broadcast_to(sums[:HALO, :], (HALO, DK)).T[0:1, :]
-
-    part = mm(dproj[...], in_rows[...])
-    late = mm(d_pre[...], gate_rows[...])
+
+    part = mm(scratch[...], in_rows[...]) + mm(d_pre[...], gate_rows[...])
     for h in range(2):
-        late = late + d_logit[:, h : h + 1] * beta_rows[h : h + 1, :].astype(FLOAT)
+        part = part + d_logit[:, h : h + 1] * beta_rows[h : h + 1, :].astype(FLOAT)
     for target, wanted in ((other, step < 4), (own, step >= 4)):
 
         @pl.when(wanted)
         def _():
-            target[0, :HALO, :] = part[:HALO].astype(HALF)
-            target[0, HALO : HALO + tokens, :] = (part[HALO:] + late).astype(HALF)
-            target[0, HALO + tokens :, :] = sum_rows[...].astype(HALF)
-
-    token[...] = jnp.zeros(token.shape, FLOAT)
-
-
-def d_first_tiles(mine, dproj, d_pre, d_logit, sums, in_rows, gate_rows, beta_rows, after):
+            target[0, :tokens, :] = part.astype(HALF)
+            target[0, tokens:, :] = sum_rows[...].astype(HALF)
+
+    token[...] = jnp.zeros(token.shape, FLOAT)
+
+
+def d_first_tiles(mine, dproj, arrived, proj, d_pre, d_logit, sums, in_rows, gate_rows, beta_rows, after):
     tokens = d_pre.shape[0]
     width = in_rows.shape[1] // 8
-    count = tokens + 2 * HALO
+    count = tokens + HALO
 
     def tile(rows):
         return pl.BlockSpec((rows, width), lambda i, mine: (0, tile_of(i, mine)))
@@ -1074,11 +1122,11 @@
     spec = pltpu.PrefetchScalarGridSpec(
         num_scalar_prefetch=1,
         grid=(8,),
-        in_specs=[whole_block(a.shape) for a in (dproj, d_pre, d_logit, sums)]
+        in_specs=[whole_block(a.shape) for a in (dproj, arrived, proj, d_pre, d_logit, sums)]
         + [tile(in_rows.shape[0]), tile(gate_rows.shape[0]), tile(beta_rows.shape[0])]
         + [pl.BlockSpec(memory_space=pl.ANY)],
         out_specs=tile_outs(count, width) + [whole_block((8, DK))],
-        scratch_shapes=[pltpu.VMEM((HALO, width), FLOAT)],
+        scratch_shapes=[pltpu.VMEM((tokens, dproj.shape[1]), HALF), pltpu.VMEM((HALO, width), FLOAT)],
     )
     tiles = out((4, count, width), HALF)
     return pl.pallas_call(
@@ -1087,32 +1135,21 @@
         out_shape=(tiles, tiles, out((8, DK), FLOAT)),
         compiler_params=pltpu.CompilerParams(vmem_limit_bytes=16 * 2**20),
         cost_estimate=cost(6.0),
-    )(mine, dproj, d_pre, d_logit, sums, in_rows, gate_rows, beta_rows, after)
-
-
-def first_total_kernel(own, arrived, total, pack, token):
-    token[...] = jnp.zeros(token.shape, FLOAT)
-    whole = own[...] + arrived[...].astype(FLOAT)
-    total[...] = whole
-    pack[:HALO, :] = whole[:HALO]
-    at = whole.shape[0] - HALO
-    pack[HALO:, :] = whole[at : at + 8]
-
-
-def input_grad_kernel(mine, total, arrived, block_input, factor, gain, d_branch, grad):
+    )(mine, dproj, arrived, proj, d_pre, d_logit, sums, in_rows, gate_rows, beta_rows, after)
+
+
+def input_grad_kernel(mine, own, arrived, block_input, factor, gain, d_branch, grad):
+    total = own[...] + arrived[...].astype(FLOAT)
     tokens, width = block_input.shape
     columns = []
     for i in range(tokens // width):
-        row = total[HALO + tokens + i : HALO + tokens + i + 1, :]
+        row = total[tokens + i : tokens + i + 1, :]
         columns.append(jnp.broadcast_to(row, (DK, width)).T[:, 0:1])
-    late_row = jnp.broadcast_to(arrived[HALO + 2 : HALO + 3, :], (DK, width)).T[:HALO, 0:1]
     mean = jnp.concatenate(columns, axis=0) / (8 * width)
     scale = factor[...]
     unit = block_input[...].astype(FLOAT) * scale
     gain_own = gain[:, lane_block(mine[0] * 2 + mine[1], width)]
-    grad[...] = d_branch[...].astype(FLOAT) + scale * (total[HALO : HALO + tokens, :] * gain_own - unit * mean)
-    last = slice(tokens - HALO, tokens)
-    grad[last, :] += scale[last] * (arrived[:HALO, :] * gain_own - unit[last] * (late_row / (8 * width)))
+    grad[...] = d_branch[...].astype(FLOAT) + scale * (total[:tokens, :] * gain_own - unit * mean)
 
 
 def next_block(array, distance):
@@ -1222,7 +1259,7 @@
         micros=4.0,
     )
     branch = head_scatter(branch_own, branch_other, mine)
-    (cot,), _ = passed([cotangent], (group_token,))
+    cot = run(copy_kernel, (out((tokens, width), HALF),), (cotangent,), after=(group_token,))[0]
     cot_tiles = head_gather(cot, mine, (mix_token,))
     whole_cot, cot_rows, d_product, token = run(
         product_grad_kernel,
@@ -1300,6 +1337,7 @@
         micros=2.0,
     )
     end_pieces = ring_pieces(group_end, "y")
+    out_keep, out_send, out_token = first_halves(down_own, down_other, mine, (group_token,))
     square = out((heads * chunks, CH, CH), FLOAT)
     *slopes, slope_token = run(
         partial(slopes_kernel, heads, chunks),
@@ -1308,8 +1346,8 @@
         [pltpu.VMEM((HALO + tokens, cols), FLOAT)],
         after=(group_token,),
     )
-    passed_sums, ffn_token = passed(ffn_sums, (*end_pieces[1:], slope_token))
-    dproj, d_logit, logit_rows, taps_part, sums = run(
+    passed_sums, ffn_token = passed(ffn_sums, (*end_pieces[1:], slope_token, out_token))
+    dproj, halo_grad, d_logit, logit_rows, taps_part, sums = run(
         partial(back_kernel, heads, chunks),
         back_shapes(heads, chunks),
         (mine, far, *end_pieces, after, q, k, logits, gate_sums, gcol, tri, states, vns, dos, dvns, es, n, proj, halo_proj, taps, *slopes),
@@ -1321,28 +1359,29 @@
     )
     packed = 2 * vd + cols + EXTRA
     tile, half_tile = out((4, packed, DK), HALF), out((4, packed // 2, DK), HALF)
-    *in_parts, in_token = run(
+    *in_parts, in_token, gains_part = run(
         in_grad_kernel,
-        (tile,) * 3 + (half_tile,) * 2 + (token_out,),
+        (tile,) * 3 + (half_tile,) * 2 + (token_out, out((2, model), FLOAT)),
         (mine, first_normed, halo_normed, dproj, logit_rows, taps_part, gain_part, gate_gain, second_gain_part, first_row, in_rows, beta_rows, *mixer_parts),
         [pltpu.VMEM((cols + HALO, HALO + tokens), HALF), pltpu.VMEM((EXTRA, DK), FLOAT)],
         scalars=1,
         micros=6.0,
         megs=16,
     )
+    out_mine, out_send, out_token = second_halves(out_keep, swapped(out_send, 2), mine, (in_token,))
     ffn_grad_out = out((hidden_cols, DK), FLOAT)
     grad_gate, grad_up, grad_down, ffn_token = run(
-        ffn_unpack_kernel, (ffn_grad_out,) * 3 + (token_out,), second_round(passed_sums), after=(in_token,)
-    )
-    in_ends, in_token = passed(in_parts[3:], (ffn_token,))
-    in_parts = in_parts[:3] + in_ends
+        ffn_unpack_kernel, (ffn_grad_out,) * 3 + (token_out,), second_round(passed_sums), after=(out_token,)
+    )
+    arrived = next_block(halo_grad, -1)
+    in_parts, in_token = with_gains(
+        mine, in_parts, gains_part, rotated(gains_part, "c", 1), (ffn_token, arrived)
+    )
     first_other, first_own, first_token = d_first_tiles(
-        mine, dproj, d_gate_pre, d_logit, sums, in_rows, gate_rows, beta_rows, in_token
+        mine, dproj, arrived, proj, d_gate_pre, d_logit, sums, in_rows, gate_rows, beta_rows, in_token
     )
     output, out_token = run(
-        output_kernel,
-        (out((tokens, width), HALF), token_out),
-        head_scatter(down_own, down_other, mine, after=(in_token,)),
+        output_kernel, (out((tokens, width), HALF), token_out), (out_mine, swapped(out_send, 1))
     )
     tile = out((4, packed, DK), HALF)
     plus, minus, in_token, rows_left = run(
@@ -1355,11 +1394,8 @@
     own_rows, plus_rows, minus_rows, gain_token = run(
         quad_sum_kernel, (out((4, 8, DK), FLOAT),) * 3 + (token_out,), ring_pieces(rows_left, "x"), after=(in_token,)
     )
-    total, pack, first_token = run(
-        first_total_kernel,
-        (out((tokens + 2 * HALO, width), FLOAT), out((HALO + 8, width), FLOAT), token_out),
-        head_halving(first_own, first_other, mine, (gain_token,)),
-    )
+    first_keep, first_send, _ = first_halves(first_own, first_other, mine, (gain_token,))
+    first_mine, first_send, _ = second_halves(first_keep, swapped(first_send, 2), mine, ())
     *sums_out, sum_token = run(
         last_sum_kernel,
         (out((packed, DK), FLOAT),) + (out((packed, DK), HALF),) * 3 + (token_out,),
@@ -1375,10 +1411,9 @@
     grad_input = run(
         input_grad_kernel,
         (out((tokens, width), FLOAT),),
-        (mine, total, next_block(pack, -1), block_input, first_factor, first_row, d_branch_own),
+        (mine, first_mine, swapped(first_send, 1), block_input, first_factor, first_row, d_branch_own),
         scalars=1,
     )[0]
-    both = both + rotated(both, "c", 1)
     return (
         output,
         grad_input,

time: 293 us -> 292 us (level)
  the two profiles are of different devices: /device:TPU:96 before, /device:TPU:2 now
where the time goes in v2:
time: 292 us; the launch traced here: 287 us
  Pallas kernels  94.1 us (32%)
  waiting for transfers between devices  93 us (32%)
  starting transfers between devices  84.9 us (29%)
  local copies, waits for them, and re-layouts  7.05 us (2%)
  matrix products  6.11 us (2%)
    pallas_call x40, Pallas kernels, run(): pl.pallas_call(body, out_shape=tuple((pltpu.HBM(a.shape, a.dtype) if i in...  81.8 us
    ppermute x42, waiting for transfers between devices, rotated(): lax.ppermute(array, axis, [(i, (i + distance) % size) for i in range(size)])  66.2 us
    ppermute x42, starting transfers between devices, rotated(): lax.ppermute(array, axis, [(i, (i + distance) % size) for i in range(size)])  48.2 us
    ppermute x16, starting transfers between devices, turned(): return lax.ppermute(array, PLANE, pairs)  24.3 us
    ppermute x16, waiting for transfers between devices, turned(): return lax.ppermute(array, PLANE, pairs)  19.1 us
    ppermute x4, waiting for transfers between devices, swapped(): return lax.ppermute(array, 'x', [(i, i ^ mask) for i in range(4)])  7.68 us
    pallas_call x1, Pallas kernels, d_first_tiles(): pl.pallas_call(d_first_kernel, grid_spec=spec, out_shape=(tiles, tiles, o...  6.9 us
    ppermute x4, starting transfers between devices, swapped(): return lax.ppermute(array, 'x', [(i, i ^ mask) for i in range(4)])  6.73 us
  transfers between devices with their start and end apart: 64, of which 34 were waited for; matrix products, arithmetic and copies ran while one was open for 2% of the time, Pallas kernels for 23%

profile of v2, /device:TPU:2, one launch (start us, length us, event | category | flops | bytes accessed | tf_op | source)
XLA Modules:
  0.0 286.9 jit_solution(6045583477209440146)
XLA Ops:
  13.3 2.8 collective-permute-done.1.refs_3_
  17.0 2.6 collective-permute-done.3.refs_4_
  22.1 4.3 %collective-permute-start.4 = (bf16[16,2048]{1,0:T(8,128)(2,1)S(1)}, bf16[16,2048]{1,0:T(8,128)(2,1)S(1)}, u32[]{:S(2)}, u32[]{:S(2)}) collective-permute-start(bf16[16,2048]{1,0:T(8,128)(2,1)S(1)} %get-tuple-element.187), channel_id=1, source_target_pairs={{0,8},{8,16},{16,24},{24,32},{32,40},{40,48},{48,56},{56,64},{64,7... | collective-permute-start | bytes 196616 | tf_op jit(solution)/shard_map/ppermute | solution.py:1158
  30.0 8.3 %shard_map.308 = (bf16[512,256]{1,0:T(8,128)(2,1)}, bf16[512,512]{1,0:T(8,128)(2,1)}, bf16[8,128,128]{2,1,0:T(8,128)(2,1)}, bf16[8,128,128]{2,1,0:T(8,128)(2,1)}...) custom-call(bf16[512,1024]{1,0:T(8,128)(2,1)S(1)} %convolution_conve, ...), custom_call_target="tpu_custom_call" | custom-call | flops 88000000 | tf_op jit(solution)/shard_map/pallas_call | solution.py:431
  38.2 3.6 %collective-permute-start.7 = (bf16[2,144,384]{2,1,0:T(8,128)(2,1)S(1)}, bf16[2,144,384]{2,1,0:T(8,128)(2,1)S(1)}, u32[]{:S(2)}, u32[]{:S(2)}) collective-permute-start(bf16[2,144,384]{2,1,0:T(8,128)(2,1)S(1)} %get-tuple-element.191.refs_1_), channel_id=1, source_target_pairs={{0,16},{8,24},{16,0},{24,8},{1,17},{9,25},{17,1},{25,9},{2,18},{10... | collective-permute-start | bytes 663560 | tf_op jit(solution)/shard_map/ppermute | solution.py:542
  42.6 2.6 collective-permute-start.5
  48.1 3.9 %collective-permute-done.6.refs_3_ = bf16[2,144,384]{2,1,0:T(8,128)(2,1)S(1)} collective-permute-done((bf16[2,144,384]{2,1,0:T(8,128)(2,1)S(1)}, bf16[2,144,384]{2,1,0:T(8,128)(2,1)S(1)}, u32[]{:S(2)}, u32[]{:S(2)}) %collective-permute-start.6) | collective-permute-done | bytes 221216 | tf_op jit(solution)/shard_map/ppermute | solution.py:542
  53.3 3.7 %collective-permute-start.10 = (bf16[2,144,384]{2,1,0:T(8,128)(2,1)S(1)}, bf16[2,144,384]{2,1,0:T(8,128)(2,1)S(1)}, u32[]{:S(2)}, u32[]{:S(2)}) collective-permute-start(bf16[2,144,384]{2,1,0:T(8,128)(2,1)S(1)} %get-tuple-element.196.refs_1_), channel_id=1, source_target_pairs={{0,64},{32,96},{64,0},{96,32},{1,65},{33,97},{65,1},{97,33},{2,66}... | collective-permute-start | bytes 663560 | tf_op jit(solution)/shard_map/ppermute | solution.py:542
  68.6 5.7 %shard_map.311 = (bf16[8,128,256]{2,1,0:T(8,128)(2,1)}, bf16[8,128,256]{2,1,0:T(8,128)(2,1)}, f32[512,512]{1,0:T(8,128)}, bf16[512,512]{1,0:T(8,128)(2,1)S(1)}, ...) custom-call(s32[4]{0:T(128)S(1)} %pad_add_fusion.refs_0_.mine, ...), custom_call_target="tpu_custom_call" | custom-call | flops 44000000 | tf_op jit(solution)/shard_map/pallas_call | solution.py:431
  87.3 6.6 %collective-permute-done.14.refs_5_ = bf16[64,2048]{1,0:T(8,128)(2,1)S(1)} collective-permute-done((bf16[64,2048]{1,0:T(8,128)(2,1)S(1)}, bf16[64,2048]{1,0:T(8,128)(2,1)S(1)}, u32[]{:S(2)}, u32[]{:S(2)}) %collective-permute-start.14) | collective-permute-done | bytes 262176 | tf_op jit(solution)/shard_map/ppermute | solution.py:542
  98.3 6.8 %collective-permute-done.21.refs_4_ = bf16[64,2048]{1,0:T(8,128)(2,1)S(1)} collective-permute-done((bf16[64,2048]{1,0:T(8,128)(2,1)S(1)}, bf16[64,2048]{1,0:T(8,128)(2,1)S(1)}, u32[]{:S(2)}, u32[]{:S(2)}) %collective-permute-start.21) | collective-permute-done | bytes 262176 | tf_op jit(solution)/shard_map/ppermute | solution.py:542
  109.3 2.6 collective-permute-done.22.refs_2_
  112.0 8.3 %shard_map.318 = (bf16[512,2048]{1,0:T(8,128)(2,1)S(1)}, bf16[704,512]{1,0:T(8,128)(2,1)S(1)}, bf16[704,512]{1,0:T(8,128)(2,1)S(1)}, bf16[704,512]{1,0:T(8,128)(...) custom-call(s32[4]{0:T(128)S(1)} %pad_add_fusion.refs_0_.mine, ...), custom_call_target="tpu_custom_call" | custom-call | flops 99000000 | tf_op jit(solution)/shard_map/pallas_call | solution.py:431
  126.0 2.9 %collective-permute-start.32 = (bf16[4,1056,128]{2,1,0:T(8,128)(2,1)S(1)}, bf16[4,1056,128]{2,1,0:T(8,128)(2,1)S(1)}, u32[]{:S(2)}, u32[]{:S(2)}) collective-permute-start(bf16[4,1056,128]{2,1,0:T(8,128)(2,1)S(1)} %get-tuple-element.241), channel_id=1, source_target_pairs={{0,24},{1,97},{8,0},{9,105},{16,8},{17,113},{24,16},{25,121},{32,5... | collective-permute-start | bytes 3244040 | tf_op jit(solution)/shard_map/ppermute | solution.py:577
  132.9 3.0 %shard_map.322 = (bf16[4,2112,128]{2,1,0:T(8,128)(2,1)S(1)}, bf16[4,2112,128]{2,1,0:T(8,128)(2,1)S(1)}, f32[8,128]{1,0:T(8,128)S(1)}) custom-call(s32[4]{0:T(128)S(1)} %pad_add_fusion.refs_0_.mine, bf16[512,2048]{1,0:T(8,128)(2,1)S(1)} %get-tuple-element.229.refs_1_, bf16[512,2048]{1,0:T(8,128)(2,1)S(1)} %get-tuple-element.230.refs_2_, ...), custom_call_target="tpu_custom_call" | custom-call | flops 11000000 | tf_op jit(solution)/shard_map/pallas_call | solution.py:431
  138.2 5.4 %collective-permute-done.27.refs_7_ = bf16[64,2048]{1,0:T(8,128)(2,1)S(1)} collective-permute-done((bf16[64,2048]{1,0:T(8,128)(2,1)S(1)}, bf16[64,2048]{1,0:T(8,128)(2,1)S(1)}, u32[]{:S(2)}, u32[]{:S(2)}) %collective-permute-start.27) | collective-permute-done | bytes 262176 | tf_op jit(solution)/shard_map/ppermute | solution.py:542
  146.1 2.9 %collective-permute-start.38 = (bf16[4,2112,128]{2,1,0:T(8,128)(2,1)}, bf16[4,2112,128]{2,1,0:T(8,128)(2,1)S(1)}, u32[]{:S(2)}, u32[]{:S(2)}) collective-permute-start(bf16[4,2112,128]{2,1,0:T(8,128)(2,1)} %get-tuple-element.253), channel_id=1, source_target_pairs={{0,24},{1,97},{8,0},{9,105},{16,8},{17,113},{24,16},{25,121},{32,5... | collective-permute-start | bytes 6488072 | tf_op jit(solution)/shard_map/ppermute | solution.py:577
  149.0 3.0 %collective-permute-start.30 = (bf16[64,2048]{1,0:T(8,128)(2,1)S(1)}, bf16[64,2048]{1,0:T(8,128)(2,1)S(1)}, u32[]{:S(2)}, u32[]{:S(2)}) collective-permute-start(bf16[64,2048]{1,0:T(8,128)(2,1)S(1)} %get-tuple-element.236.refs_1_), channel_id=1, source_target_pairs={{0,4},{2,6},{4,0},{6,2},{1,5},{3,7},{5,1},{7,3},{8,12},{10,14},{12... | collective-permute-start | bytes 786440 | tf_op jit(solution)/shard_map/ppermute | solution.py:542
  154.0 4.8 %shard_map.319 = (bf16[4,512,256]{2,1,0:T(8,128)(2,1)S(1)}, bf16[4,512,256]{2,1,0:T(8,128)(2,1)S(1)}, f32[8,128]{1,0:T(8,128)S(1)}) custom-call(s32[4]{0:T(128)S(1)} %pad_add_fusion.refs_0_.mine, bf16[704,512]{1,0:T(8,128)(2,1)S(1)} %get-tuple-element.215.product.refs_5_, bf16[704,2048]{1,0:T(8,128)(2,1)S(1)} %bitcast.36, ...), custom_call_target="tpu_custom_call" | custom-call | flops 44000000 | tf_op jit(solution)/shard_map/pallas_call | solution.py:1075
  169.7 2.8 collective-permute-start.36
  178.3 3.3 %shard_map.328 = (bf16[4,1024,128]{2,1,0:T(8,128)(2,1)S(1)}, bf16[4,1024,128]{2,1,0:T(8,128)(2,1)S(1)}, bf16[4,1024,128]{2,1,0:T(8,128)(2,1)S(1)}, bf16[4,1024,128]{2,1,0:T(8,128)(2,1)S(1)}, f32[1,2048]{1,0:T(1,128)S(1)}) custom-call(s32[4]{0:T(128)S(1)} %pad_add_fusion.refs_0_.mine, bf16[512,2048]{1,0:T(8,128)(2,1)S(1)} %get-tuple-element.244.refs_1_, ...), custom_call_target="tpu_custom_call" | custom-call | flops 55000000 | tf_op jit(solution)/shard_map/pallas_call | solution.py:431
  193.6 3.2 %collective-permute-start.47 = (bf16[2112,128]{1,0:T(8,128)(2,1)S(1)}, bf16[2112,128]{1,0:T(8,128)(2,1)S(1)}, u32[]{:S(2)}, u32[]{:S(2)}) collective-permute-start(bf16[2112,128]{1,0:T(8,128)(2,1)S(1)} %get-tuple-element.303), channel_id=1, source_target_pairs={{0,96},{1,25},{8,104},{9,1},{16,112},{17,9},{24,120},{25,17},{32,0... | collective-permute-start | bytes 1622024 | tf_op jit(solution)/shard_map/ppermute | solution.py:577
  196.8 5.0 %collective-permute-start.39 = (bf16[2,512,256]{2,1,0:T(8,128)(2,1)S(1)}, bf16[2,512,256]{2,1,0:T(8,128)(2,1)}, u32[]{:S(2)}, u32[]{:S(2)}) collective-permute-start(bf16[2,512,256]{2,1,0:T(8,128)(2,1)S(1)} %get-tuple-element.257), channel_id=1, source_target_pairs={{0,4},{2,6},{4,0},{6,2},{1,5},{3,7},{5,1},{7,3},{8,12},{10,14},{12... | collective-permute-start | bytes 1572872 | tf_op jit(solution)/shard_map/ppermute | solution.py:716
  201.8 8.0 %shard_map.335 = (bf16[528,1024]{1,0:T(8,128)(2,1)S(1)}, bf16[16,1024]{1,0:T(8,128)(2,1)S(1)}, f32[512,2]{1,0:T(8,128)S(1)}, f32[16,528]{1,0:T(8,128)S(1)}, f32[8,1024]{1,0:T(8,128)S(1)}, /*index=5*/f32[528,1]{1,0:T(8,128)S(1)}) custom-call(s32[4]{0:T(128)S(1)} %pad_add_fusion.refs_0_.mine, bf16[4,2,144,384]{3,2,1,0:T(8,128)(2,1)S(1)} %copy-done.15, ...), custom_call_target="tpu_custom_call" | custom-call | flops 121000000 | tf_op jit(solution)/shard_map/pallas_call | solution.py:431
  211.1 4.6 %shard_map.336 = (bf16[4,2112,128]{2,1,0:T(8,128)(2,1)S(1)}, bf16[4,2112,128]{2,1,0:T(8,128)(2,1)S(1)}, bf16[4,2112,128]{2,1,0:T(8,128)(2,1)S(1)}, bf16[4,1056,1...) custom-call(s32[4]{0:T(128)S(1)} %pad_add_fusion.refs_0_.mine, ...), custom_call_target="tpu_custom_call" | custom-call | flops 66000000 | tf_op jit(solution)/shard_map/pallas_call | solution.py:431
  218.8 2.7 collective-permute-start.50
  222.4 6.9 %shard_map.341 = (bf16[4,528,256]{2,1,0:T(8,128)(2,1)S(1)}, bf16[4,528,256]{2,1,0:T(8,128)(2,1)S(1)}, f32[8,128]{1,0:T(8,128)S(1)}) custom-call(s32[4]{0:T(128)S(1)} %pad_add_fusion.refs_0_.mine, bf16[528,1024]{1,0:T(8,128)(2,1)S(1)} %get-tuple-element.279.refs_3_.dproj, bf16[16,1024]{1,0:T(8,128)(2,1)S(1)} %collective-permute-done.44.refs_6_.arrived, ...), custom_call_target="tpu_custom_call" | custom-call | flops 66000000 | tf_op jit(solution)/shard_map/pallas_call | solution.py:1132
  231.2 4.0 %collective-permute-done.50.refs_3_ = bf16[4,1056,128]{2,1,0:T(8,128)(2,1)S(1)} collective-permute-done((bf16[4,1056,128]{2,1,0:T(8,128)(2,1)S(1)}, bf16[4,1056,128]{2,1,0:T(8,128)(2,1)S(1)}, u32[]{:S(2)}, u32[]{:S(2)}) %collective-permute-start.50) | collective-permute-done | bytes 1081376 | tf_op jit(solution)/shard_map/ppermute | solution.py:577
  241.3 5.6 %collective-permute-done.54.refs_3_ = f32[3,4,8,128]{3,2,1,0:T(8,128)S(1)} collective-permute-done((f32[3,4,8,128]{3,2,1,0:T(8,128)S(1)}, f32[3,4,8,128]{3,2,1,0:T(8,128)S(1)}, u32[]{:S(2)}, u32[]{:S(2)}) %collective-permute-start.54) | collective-permute-done | bytes 49184 | tf_op jit(solution)/shard_map/ppermute | solution.py:542
  246.9 4.1 %collective-permute-done.52.refs_1_ = f32[3,4,8,128]{3,2,1,0:T(8,128)S(1)} collective-permute-done((f32[3,4,8,128]{3,2,1,0:T(8,128)S(1)}, f32[3,4,8,128]{3,2,1,0:T(8,128)S(1)}, u32[]{:S(2)}, u32[]{:S(2)}) %collective-permute-start.52) | collective-permute-done | bytes 49184 | tf_op jit(solution)/shard_map/ppermute | solution.py:542
  256.9 9.2 %collective-permute-done.59.refs_5_ = f32[4,8,128]{2,1,0:T(8,128)S(1)} collective-permute-done((f32[4,8,128]{2,1,0:T(8,128)S(1)}, f32[4,8,128]{2,1,0:T(8,128)S(1)}, u32[]{:S(2)}, u32[]{:S(2)}) %collective-permute-start.59) | collective-permute-done | bytes 16416 | tf_op jit(solution)/shard_map/ppermute | solution.py:577
  274.3 6.5 %collective-permute-done.56.refs_2_ = bf16[528,256]{1,0:T(8,128)(2,1)S(1)} collective-permute-done((bf16[528,256]{1,0:T(8,128)(2,1)S(1)}, bf16[528,256]{1,0:T(8,128)(2,1)S(1)}, u32[]{:S(2)}, u32[]{:S(2)}) %collective-permute-start.56) | collective-permute-done | bytes 270368 | tf_op jit(solution)/shard_map/ppermute | solution.py:716
  (224 shorter events, 135.4 us)
Async XLA Ops:
  0.7 12.7 %collective-permute-start.2 = (bf16[512,256]{1,0:T(8,128)(2,1)}, bf16[512,256]{1,0:T(8,128)(2,1)S(1)}, u32[]{:S(2)}, u32[]{:S(2)}) collective-permute-start(bf16[512,256]{1,0:T(8,128)(2,1)} %refs_3_.3), channel_id=1, source_target_pairs={{0,4},{2,6},{4,0},{6,2},{1,5},{3,7},{5,1},{7,3},{8,12},{10,14},{12... | collective-permute-start | bytes 786440 | tf_op jit(solution)/shard_map/ppermute | solution.py:542
  2.9 13.3 %collective-permute-start.1 = (bf16[512,256]{1,0:T(8,128)(2,1)}, bf16[512,256]{1,0:T(8,128)(2,1)S(1)}, u32[]{:S(2)}, u32[]{:S(2)}) collective-permute-start(bf16[512,256]{1,0:T(8,128)(2,1)} %refs_3_.3), channel_id=1, source_target_pairs={{0,2},{2,4},{4,6},{6,0},{1,3},{3,5},{5,7},{7,1},{8,10},{10,12},{12... | collective-permute-start | bytes 786440 | tf_op jit(solution)/shard_map/ppermute | solution.py:542
  2.9 13.3 %collective-permute-start = (bf16[512,256]{1,0:T(8,128)(2,1)}, bf16[512,256]{1,0:T(8,128)(2,1)S(1)}, u32[]{:S(2)}, u32[]{:S(2)}) collective-permute-start(bf16[512,256]{1,0:T(8,128)(2,1)} %refs_3_.3), channel_id=1, source_target_pairs={{0,6},{2,0},{4,2},{6,4},{1,7},{3,1},{5,3},{7,5},{8,14},{10,8},{12,... | collective-permute-start | bytes 786440 | tf_op jit(solution)/shard_map/ppermute | solution.py:542
  60.2 14.0 %collective-permute-start.17 = (bf16[512,256]{1,0:T(8,128)(2,1)S(1)}, bf16[512,256]{1,0:T(8,128)(2,1)S(1)}, u32[]{:S(2)}, u32[]{:S(2)}) collective-permute-start(bf16[512,256]{1,0:T(8,128)(2,1)S(1)} %shard_map.313.refs_1_), channel_id=1, source_target_pairs={{0,4},{2,6},{4,0},{6,2},{1,5},{3,7},{5,1},{7,3},{8,12},{10,14},{12... | collective-permute-start | bytes 786440 | tf_op jit(solution)/shard_map/ppermute | solution.py:542
  62.4 11.9 %collective-permute-start.16 = (bf16[512,256]{1,0:T(8,128)(2,1)S(1)}, bf16[512,256]{1,0:T(8,128)(2,1)S(1)}, u32[]{:S(2)}, u32[]{:S(2)}) collective-permute-start(bf16[512,256]{1,0:T(8,128)(2,1)S(1)} %shard_map.313.refs_1_), channel_id=1, source_target_pairs={{0,2},{2,4},{4,6},{6,0},{1,3},{3,5},{5,7},{7,1},{8,10},{10,12},{12... | collective-permute-start | bytes 786440 | tf_op jit(solution)/shard_map/ppermute | solution.py:542
  63.3 11.2 %collective-permute-start.15 = (bf16[512,256]{1,0:T(8,128)(2,1)S(1)}, bf16[512,256]{1,0:T(8,128)(2,1)S(1)}, u32[]{:S(2)}, u32[]{:S(2)}) collective-permute-start(bf16[512,256]{1,0:T(8,128)(2,1)S(1)} %shard_map.313.refs_1_), channel_id=1, source_target_pairs={{0,6},{2,0},{4,2},{6,4},{1,7},{3,1},{5,3},{7,5},{8,14},{10,8},{12,... | collective-permute-start | bytes 786440 | tf_op jit(solution)/shard_map/ppermute | solution.py:542
  80.2 13.7 %collective-permute-start.14 = (bf16[64,2048]{1,0:T(8,128)(2,1)S(1)}, bf16[64,2048]{1,0:T(8,128)(2,1)S(1)}, u32[]{:S(2)}, u32[]{:S(2)}) collective-permute-start(bf16[64,2048]{1,0:T(8,128)(2,1)S(1)} %get-tuple-element.209), channel_id=1, source_target_pairs={{0,4},{2,6},{4,0},{6,2},{1,5},{3,7},{5,1},{7,3},{8,12},{10,14},{12... | collective-permute-start | bytes 786440 | tf_op jit(solution)/shard_map/ppermute | solution.py:542
  94.2 10.9 %collective-permute-start.21 = (bf16[64,2048]{1,0:T(8,128)(2,1)S(1)}, bf16[64,2048]{1,0:T(8,128)(2,1)S(1)}, u32[]{:S(2)}, u32[]{:S(2)}) collective-permute-start(bf16[64,2048]{1,0:T(8,128)(2,1)S(1)} %get-tuple-element.213.refs_1_), channel_id=1, source_target_pairs={{0,4},{2,6},{4,0},{6,2},{1,5},{3,7},{5,1},{7,3},{8,12},{10,14},{12... | collective-permute-start | bytes 786440 | tf_op jit(solution)/shard_map/ppermute | solution.py:542
  96.1 11.1 %collective-permute-start.20 = (bf16[64,2048]{1,0:T(8,128)(2,1)S(1)}, bf16[64,2048]{1,0:T(8,128)(2,1)S(1)}, u32[]{:S(2)}, u32[]{:S(2)}) collective-permute-start(bf16[64,2048]{1,0:T(8,128)(2,1)S(1)} %get-tuple-element.213.refs_1_), channel_id=1, source_target_pairs={{0,2},{2,4},{4,6},{6,0},{1,3},{3,5},{5,7},{7,1},{8,10},{10,12},{12... | collective-permute-start | bytes 786440 | tf_op jit(solution)/shard_map/ppermute | solution.py:542
  96.6 12.0 %collective-permute-start.19 = (bf16[64,2048]{1,0:T(8,128)(2,1)S(1)}, bf16[64,2048]{1,0:T(8,128)(2,1)S(1)}, u32[]{:S(2)}, u32[]{:S(2)}) collective-permute-start(bf16[64,2048]{1,0:T(8,128)(2,1)S(1)} %get-tuple-element.213.refs_1_), channel_id=1, source_target_pairs={{0,6},{2,0},{4,2},{6,4},{1,7},{3,1},{5,3},{7,5},{8,14},{10,8},{12,... | collective-permute-start | bytes 786440 | tf_op jit(solution)/shard_map/ppermute | solution.py:542
  125.6 18.5 %collective-permute-start.31 = (bf16[4,1056,128]{2,1,0:T(8,128)(2,1)S(1)}, bf16[4,1056,128]{2,1,0:T(8,128)(2,1)S(1)}, u32[]{:S(2)}, u32[]{:S(2)}) collective-permute-start(bf16[4,1056,128]{2,1,0:T(8,128)(2,1)S(1)} %get-tuple-element.240), channel_id=1, source_target_pairs={{0,8},{1,33},{8,16},{9,41},{16,24},{17,49},{24,0},{25,57},{32,40},... | collective-permute-start | bytes 3244040 | tf_op jit(solution)/shard_map/ppermute | solution.py:577
  126.0 18.1 %collective-permute-start.32 = (bf16[4,1056,128]{2,1,0:T(8,128)(2,1)S(1)}, bf16[4,1056,128]{2,1,0:T(8,128)(2,1)S(1)}, u32[]{:S(2)}, u32[]{:S(2)}) collective-permute-start(bf16[4,1056,128]{2,1,0:T(8,128)(2,1)S(1)} %get-tuple-element.241), channel_id=1, source_target_pairs={{0,24},{1,97},{8,0},{9,105},{16,8},{17,113},{24,16},{25,121},{32,5... | collective-permute-start | bytes 3244040 | tf_op jit(solution)/shard_map/ppermute | solution.py:577
  130.9 12.7 %collective-permute-start.27 = (bf16[64,2048]{1,0:T(8,128)(2,1)S(1)}, bf16[64,2048]{1,0:T(8,128)(2,1)S(1)}, u32[]{:S(2)}, u32[]{:S(2)}) collective-permute-start(bf16[64,2048]{1,0:T(8,128)(2,1)S(1)} %get-tuple-element.228), channel_id=1, source_target_pairs={{0,4},{2,6},{4,0},{6,2},{1,5},{3,7},{5,1},{7,3},{8,12},{10,14},{12... | collective-permute-start | bytes 786440 | tf_op jit(solution)/shard_map/ppermute | solution.py:542
  145.8 27.9 %collective-permute-start.37 = (bf16[4,2112,128]{2,1,0:T(8,128)(2,1)S(1)}, bf16[4,2112,128]{2,1,0:T(8,128)(2,1)S(1)}, u32[]{:S(2)}, u32[]{:S(2)}) collective-permute-start(bf16[4,2112,128]{2,1,0:T(8,128)(2,1)S(1)} %get-tuple-element.252), channel_id=1, source_target_pairs={{0,8},{1,33},{8,16},{9,41},{16,24},{17,49},{24,0},{25,57},{32,40},... | collective-permute-start | bytes 6488072 | tf_op jit(solution)/shard_map/ppermute | solution.py:577
  146.1 35.5 %collective-permute-start.38 = (bf16[4,2112,128]{2,1,0:T(8,128)(2,1)}, bf16[4,2112,128]{2,1,0:T(8,128)(2,1)S(1)}, u32[]{:S(2)}, u32[]{:S(2)}) collective-permute-start(bf16[4,2112,128]{2,1,0:T(8,128)(2,1)} %get-tuple-element.253), channel_id=1, source_target_pairs={{0,24},{1,97},{8,0},{9,105},{16,8},{17,113},{24,16},{25,121},{32,5... | collective-permute-start | bytes 6488072 | tf_op jit(solution)/shard_map/ppermute | solution.py:577
  162.9 27.7 %collective-permute-start.23 = (bf16[4,512,256]{2,1,0:T(8,128)(2,1)S(1)}, bf16[4,512,256]{2,1,0:T(8,128)(2,1)S(1)}, u32[]{:S(2)}, u32[]{:S(2)}) collective-permute-start(bf16[4,512,256]{2,1,0:T(8,128)(2,1)S(1)} %get-tuple-element.218), channel_id=1, source_target_pairs={{0,1},{1,0},{2,3},{3,2},{4,5},{5,4},{6,7},{7,6},{8,9},{9,8},{10,11... | collective-permute-start | bytes 3145736 | tf_op jit(solution)/shard_map/ppermute | solution.py:542
  169.7 13.3 %collective-permute-start.36 = (bf16[2,128,256]{2,1,0:T(8,128)(2,1)S(1)}, bf16[2,128,256]{2,1,0:T(8,128)(2,1)S(1)}, u32[]{:S(2)}, u32[]{:S(2)}) collective-permute-start(bf16[2,128,256]{2,1,0:T(8,128)(2,1)S(1)} %get-tuple-element.246.refs_2_), channel_id=1, source_target_pairs={{0,16},{8,24},{16,0},{24,8},{1,17},{9,25},{17,1},{25,9},{2,18},{10... | collective-permute-start | bytes 393224 | tf_op jit(solution)/shard_map/ppermute | solution.py:542
  172.5 10.5 %collective-permute-start.35 = (bf16[2,128,256]{2,1,0:T(8,128)(2,1)S(1)}, bf16[2,128,256]{2,1,0:T(8,128)(2,1)S(1)}, u32[]{:S(2)}, u32[]{:S(2)}) collective-permute-start(bf16[2,128,256]{2,1,0:T(8,128)(2,1)S(1)} %get-tuple-element.246.refs_2_), channel_id=1, source_target_pairs={{0,8},{8,16},{16,24},{24,0},{1,9},{9,17},{17,25},{25,1},{2,10},{10... | collective-permute-start | bytes 393224 | tf_op jit(solution)/shard_map/ppermute | solution.py:542
  193.6 23.5 %collective-permute-start.46 = (bf16[2112,128]{1,0:T(8,128)(2,1)S(1)}, bf16[2112,128]{1,0:T(8,128)(2,1)S(1)}, u32[]{:S(2)}, u32[]{:S(2)}) collective-permute-start(bf16[2112,128]{1,0:T(8,128)(2,1)S(1)} %get-tuple-element.302), channel_id=1, source_target_pairs={{0,32},{1,9},{8,40},{9,17},{16,48},{17,25},{24,56},{25,1},{32,64},... | collective-permute-start | bytes 1622024 | tf_op jit(solution)/shard_map/ppermute | solution.py:577
  193.6 23.5 %collective-permute-start.47 = (bf16[2112,128]{1,0:T(8,128)(2,1)S(1)}, bf16[2112,128]{1,0:T(8,128)(2,1)S(1)}, u32[]{:S(2)}, u32[]{:S(2)}) collective-permute-start(bf16[2112,128]{1,0:T(8,128)(2,1)S(1)} %get-tuple-element.303), channel_id=1, source_target_pairs={{0,96},{1,25},{8,104},{9,1},{16,112},{17,9},{24,120},{25,17},{32,0... | collective-permute-start | bytes 1622024 | tf_op jit(solution)/shard_map/ppermute | solution.py:577
  196.8 20.2 %collective-permute-start.48 = (bf16[2112,128]{1,0:T(8,128)(2,1)S(1)}, bf16[2112,128]{1,0:T(8,128)(2,1)S(1)}, u32[]{:S(2)}, u32[]{:S(2)}) collective-permute-start(bf16[2112,128]{1,0:T(8,128)(2,1)S(1)} %get-tuple-element.304), channel_id=1, source_target_pairs={{0,64},{1,17},{8,72},{9,25},{16,80},{17,1},{24,88},{25,9},{32,96},... | collective-permute-start | bytes 1622024 | tf_op jit(solution)/shard_map/ppermute | solution.py:577
  196.8 18.9 %collective-permute-start.39 = (bf16[2,512,256]{2,1,0:T(8,128)(2,1)S(1)}, bf16[2,512,256]{2,1,0:T(8,128)(2,1)}, u32[]{:S(2)}, u32[]{:S(2)}) collective-permute-start(bf16[2,512,256]{2,1,0:T(8,128)(2,1)S(1)} %get-tuple-element.257), channel_id=1, source_target_pairs={{0,4},{2,6},{4,0},{6,2},{1,5},{3,7},{5,1},{7,3},{8,12},{10,14},{12... | collective-permute-start | bytes 1572872 | tf_op jit(solution)/shard_map/ppermute | solution.py:716
  218.8 16.4 %collective-permute-start.50 = (bf16[4,1056,128]{2,1,0:T(8,128)(2,1)S(1)}, bf16[4,1056,128]{2,1,0:T(8,128)(2,1)S(1)}, u32[]{:S(2)}, u32[]{:S(2)}) collective-permute-start(bf16[4,1056,128]{2,1,0:T(8,128)(2,1)S(1)} %get-tuple-element.313), channel_id=1, source_target_pairs={{0,8},{1,33},{8,16},{9,41},{16,24},{17,49},{24,0},{25,57},{32,40},... | collective-permute-start | bytes 3244040 | tf_op jit(solution)/shard_map/ppermute | solution.py:577
  221.5 15.2 %collective-permute-start.51 = (bf16[4,1056,128]{2,1,0:T(8,128)(2,1)S(1)}, bf16[4,1056,128]{2,1,0:T(8,128)(2,1)S(1)}, u32[]{:S(2)}, u32[]{:S(2)}) collective-permute-start(bf16[4,1056,128]{2,1,0:T(8,128)(2,1)S(1)} %get-tuple-element.314), channel_id=1, source_target_pairs={{0,24},{1,97},{8,0},{9,105},{16,8},{17,113},{24,16},{25,121},{32,5... | collective-permute-start | bytes 3244040 | tf_op jit(solution)/shard_map/ppermute | solution.py:577
  237.9 29.0 %collective-permute-start.57 = (bf16[4,2112,128]{2,1,0:T(8,128)(2,1)S(1)}, bf16[4,2112,128]{2,1,0:T(8,128)(2,1)S(1)}, u32[]{:S(2)}, u32[]{:S(2)}) collective-permute-start(bf16[4,2112,128]{2,1,0:T(8,128)(2,1)S(1)} %get-tuple-element.326), channel_id=1, source_target_pairs={{0,8},{1,33},{8,16},{9,41},{16,24},{17,49},{24,0},{25,57},{32,40},... | collective-permute-start | bytes 6488072 | tf_op jit(solution)/shard_map/ppermute | solution.py:577
  240.0 26.9 %collective-permute-start.58 = (bf16[4,2112,128]{2,1,0:T(8,128)(2,1)S(1)}, bf16[4,2112,128]{2,1,0:T(8,128)(2,1)S(1)}, u32[]{:S(2)}, u32[]{:S(2)}) collective-permute-start(bf16[4,2112,128]{2,1,0:T(8,128)(2,1)S(1)} %get-tuple-element.327), channel_id=1, source_target_pairs={{0,24},{1,97},{8,0},{9,105},{16,8},{17,113},{24,16},{25,121},{32,5... | collective-permute-start | bytes 6488072 | tf_op jit(solution)/shard_map/ppermute | solution.py:577
  252.2 21.0 %collective-permute-start.55 = (bf16[2,528,256]{2,1,0:T(8,128)(2,1)S(1)}, bf16[2,528,256]{2,1,0:T(8,128)(2,1)S(1)}, u32[]{:S(2)}, u32[]{:S(2)}) collective-permute-start(bf16[2,528,256]{2,1,0:T(8,128)(2,1)S(1)} %get-tuple-element.321), channel_id=1, source_target_pairs={{0,4},{2,6},{4,0},{6,2},{1,5},{3,7},{5,1},{7,3},{8,12},{10,14},{12... | collective-permute-start | bytes 1622024 | tf_op jit(solution)/shard_map/ppermute | solution.py:716
  253.7 12.5 %collective-permute-start.59 = (f32[4,8,128]{2,1,0:T(8,128)S(1)}, f32[4,8,128]{2,1,0:T(8,128)S(1)}, u32[]{:S(2)}, u32[]{:S(2)}) collective-permute-start(f32[4,8,128]{2,1,0:T(8,128)S(1)} %get-tuple-element.329), channel_id=1, source_target_pairs={{0,8},{1,33},{8,16},{9,41},{16,24},{17,49},{24,0},{25,57},{32,40},... | collective-permute-start | bytes 49160 | tf_op jit(solution)/shard_map/ppermute | solution.py:577
  254.5 12.5 %collective-permute-start.60 = (f32[4,8,128]{2,1,0:T(8,128)S(1)}, f32[4,8,128]{2,1,0:T(8,128)S(1)}, u32[]{:S(2)}, u32[]{:S(2)}) collective-permute-start(f32[4,8,128]{2,1,0:T(8,128)S(1)} %get-tuple-element.330), channel_id=1, source_target_pairs={{0,24},{1,97},{8,0},{9,105},{16,8},{17,113},{24,16},{25,121},{32,5... | collective-permute-start | bytes 49160 | tf_op jit(solution)/shard_map/ppermute | solution.py:577
  268.5 16.4 %collective-permute-start.61 = (bf16[2112,128]{1,0:T(8,128)(2,1)S(1)}, bf16[2112,128]{1,0:T(8,128)(2,1)S(1)}, u32[]{:S(2)}, u32[]{:S(2)}) collective-permute-start(bf16[2112,128]{1,0:T(8,128)(2,1)S(1)} %get-tuple-element.332), channel_id=1, source_target_pairs={{0,32},{1,9},{8,40},{9,17},{16,48},{17,25},{24,56},{25,1},{32,64},... | collective-permute-start | bytes 1622024 | tf_op jit(solution)/shard_map/ppermute | solution.py:577
  269.9 14.9 %collective-permute-start.62 = (bf16[2112,128]{1,0:T(8,128)(2,1)S(1)}, bf16[2112,128]{1,0:T(8,128)(2,1)S(1)}, u32[]{:S(2)}, u32[]{:S(2)}) collective-permute-start(bf16[2112,128]{1,0:T(8,128)(2,1)S(1)} %get-tuple-element.333), channel_id=1, source_target_pairs={{0,96},{1,25},{8,104},{9,1},{16,112},{17,9},{24,120},{25,17},{32,0... | collective-permute-start | bytes 1622024 | tf_op jit(solution)/shard_map/ppermute | solution.py:577
  271.7 13.1 %collective-permute-start.63 = (bf16[2112,128]{1,0:T(8,128)(2,1)S(1)}, bf16[2112,128]{1,0:T(8,128)(2,1)S(1)}, u32[]{:S(2)}, u32[]{:S(2)}) collective-permute-start(bf16[2112,128]{1,0:T(8,128)(2,1)S(1)} %get-tuple-element.334), channel_id=1, source_target_pairs={{0,64},{1,17},{8,72},{9,25},{16,80},{17,1},{24,88},{25,9},{32,96},... | collective-permute-start | bytes 1622024 | tf_op jit(solution)/shard_map/ppermute | solution.py:577
  (69 other events, 614.0 us)

commit v3 on v2

--- a/solution.py
+++ b/solution.py
@@ -1292,9 +1292,9 @@
         micros=9.0,
         megs=20,
     )
-    second_parts, token = head_scatter(second_own, second_other, mine, True)
     grad_args = (mine, whole_cot, second_normed, d_gate, d_up, product)
-    *ffn_ends, token = ffn_grads((3,), *grad_args, token)
+    *ffn_ends, token = ffn_grads((3,), *grad_args, ffn_token)
+    second_parts, token = head_scatter(second_own, second_other, mine, True, (token,))
     ffn_plus, ffn_minus, token = ffn_grads((1, 2), *grad_args, token)
     d_hidden, second_gain_part, back_token = run(
         second_back_kernel,
@@ -1304,10 +1304,11 @@
     )
     ffn_group, ffn_token = relayed([None, ffn_plus, ffn_minus, *ffn_ends], (back_token,), 3.0)
     down_other, down_own, down_token = down_tiles(mine, product, swiglu_down.T, hidden)
+    ffn_own, own_token = ffn_grads((0,), *grad_args, back_token)
     d_branch, d_branch_own = run(
         join_rows_kernel,
         (out((tokens, model), HALF), out((tokens, width), HALF)),
-        (mine, *head_gather(d_hidden, mine, (down_token, ffn_token))),
+        (mine, *head_gather(d_hidden, mine, (down_token, ffn_token, own_token))),
         scalars=1,
     )
     d_gated = jnp.dot(d_branch, mixer_weight, preferred_element_type=FLOAT)
@@ -1317,7 +1318,6 @@
         (d_gated, mixed, gate_pre, gain_row, q, w, p, n, gcol),
         micros=4.0,
     )
-    ffn_own, token = ffn_grads((0,), *grad_args, gate_sums[:8])
     *ffn_sums, ffn_token = seq_sums((ffn_own, *ffn_group[1:]), (), mine, (), 3.0)
     tile = out((4, 2 * vd, DK), HALF)
     *mixer_parts, gate_gain = run(

time: 292 us -> 287 us (0.983)
  waiting for transfers between devices: 93 us -> 86.7 us
  starting transfers between devices: 84.9 us -> 88 us
    ppermute x42, waiting for transfers between devices: 66.2 us -> 59.7 us  [rotated(): lax.ppermute(array, axis, [(i, (i + distance) % size) for i in range(size)])]
    ppermute x42, starting transfers between devices: 48.2 us -> 52 us  [rotated(): lax.ppermute(array, axis, [(i, (i + distance) % size) for i in range(size)])]
    unnamed x74 -> x66, local copies, waits for them, and re-layouts: 6.52 us -> 6.49 us
  transfers between devices with their start and end apart: 64 -> 64, of which waited for: 34 -> 31; matrix products, arithmetic and copies ran while one was open for 2% -> 2% of each run, Pallas kernels for 23% -> 24%
where the time goes in v3:
time: 287 us; the launch traced here: 283 us
  Pallas kernels  93.2 us (32%)
  starting transfers between devices  88 us (31%)
  waiting for transfers between devices  86.7 us (30%)
  local copies, waits for them, and re-layouts  7.02 us (2%)
  matrix products  6.11 us (2%)
    pallas_call x40, Pallas kernels, run(): pl.pallas_call(body, out_shape=tuple((pltpu.HBM(a.shape, a.dtype) if i in...  80.9 us
    ppermute x42, waiting for transfers between devices, rotated(): lax.ppermute(array, axis, [(i, (i + distance) % size) for i in range(size)])  59.7 us
    ppermute x42, starting transfers between devices, rotated(): lax.ppermute(array, axis, [(i, (i + distance) % size) for i in range(size)])  52 us
    ppermute x16, starting transfers between devices, turned(): return lax.ppermute(array, PLANE, pairs)  25.3 us
    ppermute x16, waiting for transfers between devices, turned(): return lax.ppermute(array, PLANE, pairs)  19.5 us
    ppermute x4, waiting for transfers between devices, swapped(): return lax.ppermute(array, 'x', [(i, i ^ mask) for i in range(4)])  7.49 us
    pallas_call x1, Pallas kernels, d_first_tiles(): pl.pallas_call(d_first_kernel, grid_spec=spec, out_shape=(tiles, tiles, o...  6.9 us
    unnamed x66, local copies, waits for them, and re-layouts  6.49 us
  transfers between devices with their start and end apart: 64, of which 31 were waited for; matrix products, arithmetic and copies ran while one was open for 2% of the time, Pallas kernels for 24%

profile of v3, /device:TPU:2, one launch (start us, length us, event | category | flops | bytes accessed | tf_op | source)
XLA Modules:
  0.0 282.8 jit_solution(5863771143893553807)
XLA Ops:
  13.3 2.8 %collective-permute-done.1.refs_3_ = bf16[512,256]{1,0:T(8,128)(2,1)S(1)} collective-permute-done((bf16[512,256]{1,0:T(8,128)(2,1)}, bf16[512,256]{1,0:T(8,128)(2,1)S(1)}, u32[]{:S(2)}, u32[]{:S(2)}) %collective-permute-start.1) | collective-permute-done | bytes 262176 | tf_op jit(solution)/shard_map/ppermute | solution.py:542
  22.1 4.3 %collective-permute-start.4 = (bf16[16,2048]{1,0:T(8,128)(2,1)S(1)}, bf16[16,2048]{1,0:T(8,128)(2,1)S(1)}, u32[]{:S(2)}, u32[]{:S(2)}) collective-permute-start(bf16[16,2048]{1,0:T(8,128)(2,1)S(1)} %get-tuple-element.189), channel_id=1, source_target_pairs={{0,8},{8,16},{16,24},{24,32},{32,40},{40,48},{48,56},{56,64},{64,7... | collective-permute-start | bytes 196616 | tf_op jit(solution)/shard_map/ppermute | solution.py:1158
  30.0 8.2 %shard_map.308 = (bf16[512,256]{1,0:T(8,128)(2,1)}, bf16[512,512]{1,0:T(8,128)(2,1)}, bf16[8,128,128]{2,1,0:T(8,128)(2,1)}, bf16[8,128,128]{2,1,0:T(8,128)(2,1)}...) custom-call(bf16[512,1024]{1,0:T(8,128)(2,1)S(1)} %convolution_conve, ...), custom_call_target="tpu_custom_call" | custom-call | flops 88000000 | tf_op jit(solution)/shard_map/pallas_call | solution.py:431
  38.2 3.6 %collective-permute-start.7 = (bf16[2,144,384]{2,1,0:T(8,128)(2,1)S(1)}, bf16[2,144,384]{2,1,0:T(8,128)(2,1)S(1)}, u32[]{:S(2)}, u32[]{:S(2)}) collective-permute-start(bf16[2,144,384]{2,1,0:T(8,128)(2,1)S(1)} %get-tuple-element.193.refs_1_), channel_id=1, source_target_pairs={{0,16},{8,24},{16,0},{24,8},{1,17},{9,25},{17,1},{25,9},{2,18},{10... | collective-permute-start | bytes 663560 | tf_op jit(solution)/shard_map/ppermute | solution.py:542
  48.0 3.9 %collective-permute-done.6.refs_3_ = bf16[2,144,384]{2,1,0:T(8,128)(2,1)S(1)} collective-permute-done((bf16[2,144,384]{2,1,0:T(8,128)(2,1)S(1)}, bf16[2,144,384]{2,1,0:T(8,128)(2,1)S(1)}, u32[]{:S(2)}, u32[]{:S(2)}) %collective-permute-start.6) | collective-permute-done | bytes 221216 | tf_op jit(solution)/shard_map/ppermute | solution.py:542
  53.2 3.7 %collective-permute-start.10 = (bf16[2,144,384]{2,1,0:T(8,128)(2,1)S(1)}, bf16[2,144,384]{2,1,0:T(8,128)(2,1)S(1)}, u32[]{:S(2)}, u32[]{:S(2)}) collective-permute-start(bf16[2,144,384]{2,1,0:T(8,128)(2,1)S(1)} %get-tuple-element.198.refs_1_), channel_id=1, source_target_pairs={{0,64},{32,96},{64,0},{96,32},{1,65},{33,97},{65,1},{97,33},{2,66}... | collective-permute-start | bytes 663560 | tf_op jit(solution)/shard_map/ppermute | solution.py:542
  68.6 5.6 %shard_map.311 = (bf16[8,128,256]{2,1,0:T(8,128)(2,1)}, bf16[8,128,256]{2,1,0:T(8,128)(2,1)}, f32[512,512]{1,0:T(8,128)}, bf16[512,512]{1,0:T(8,128)(2,1)S(1)}, ...) custom-call(s32[4]{0:T(128)S(1)} %pad_add_fusion.refs_0_.mine, ...), custom_call_target="tpu_custom_call" | custom-call | flops 44000000 | tf_op jit(solution)/shard_map/pallas_call | solution.py:431
  87.3 6.6 %collective-permute-done.14.refs_5_ = bf16[64,2048]{1,0:T(8,128)(2,1)S(1)} collective-permute-done((bf16[64,2048]{1,0:T(8,128)(2,1)S(1)}, bf16[64,2048]{1,0:T(8,128)(2,1)S(1)}, u32[]{:S(2)}, u32[]{:S(2)}) %collective-permute-start.14) | collective-permute-done | bytes 262176 | tf_op jit(solution)/shard_map/ppermute | solution.py:542
  98.3 6.8 %collective-permute-done.21.refs_4_ = bf16[64,2048]{1,0:T(8,128)(2,1)S(1)} collective-permute-done((bf16[64,2048]{1,0:T(8,128)(2,1)S(1)}, bf16[64,2048]{1,0:T(8,128)(2,1)S(1)}, u32[]{:S(2)}, u32[]{:S(2)}) %collective-permute-start.21) | collective-permute-done | bytes 262176 | tf_op jit(solution)/shard_map/ppermute | solution.py:542
  109.3 2.6 collective-permute-done.22.refs_2_
  111.9 7.8 %shard_map.318 = (bf16[512,2048]{1,0:T(8,128)(2,1)S(1)}, bf16[704,512]{1,0:T(8,128)(2,1)S(1)}, bf16[704,512]{1,0:T(8,128)(2,1)S(1)}, bf16[704,512]{1,0:T(8,128)(...) custom-call(s32[4]{0:T(128)S(1)} %pad_add_fusion.refs_0_.mine, ...), custom_call_target="tpu_custom_call" | custom-call | flops 99000000 | tf_op jit(solution)/shard_map/pallas_call | solution.py:431
  122.2 2.9 %collective-permute-start.32 = (bf16[4,1056,128]{2,1,0:T(8,128)(2,1)S(1)}, bf16[4,1056,128]{2,1,0:T(8,128)(2,1)S(1)}, u32[]{:S(2)}, u32[]{:S(2)}) collective-permute-start(bf16[4,1056,128]{2,1,0:T(8,128)(2,1)S(1)} %get-tuple-element.244), channel_id=1, source_target_pairs={{0,24},{1,97},{8,0},{9,105},{16,8},{17,113},{24,16},{25,121},{32,5... | collective-permute-start | bytes 3244040 | tf_op jit(solution)/shard_map/ppermute | solution.py:577
  130.0 3.0 %shard_map.322 = (bf16[4,2112,128]{2,1,0:T(8,128)(2,1)S(1)}, bf16[4,2112,128]{2,1,0:T(8,128)(2,1)S(1)}, f32[8,128]{1,0:T(8,128)S(1)}) custom-call(s32[4]{0:T(128)S(1)} %pad_add_fusion.refs_0_.mine, bf16[512,2048]{1,0:T(8,128)(2,1)S(1)} %get-tuple-element.227.refs_1_, bf16[512,2048]{1,0:T(8,128)(2,1)S(1)} %get-tuple-element.228.refs_2_, ...), custom_call_target="tpu_custom_call" | custom-call | flops 11000000 | tf_op jit(solution)/shard_map/pallas_call | solution.py:431
  135.2 5.7 %collective-permute-done.27.refs_7_ = bf16[64,2048]{1,0:T(8,128)(2,1)S(1)} collective-permute-done((bf16[64,2048]{1,0:T(8,128)(2,1)S(1)}, bf16[64,2048]{1,0:T(8,128)(2,1)S(1)}, u32[]{:S(2)}, u32[]{:S(2)}) %collective-permute-start.27) | collective-permute-done | bytes 262176 | tf_op jit(solution)/shard_map/ppermute | solution.py:542
  143.4 2.9 %collective-permute-start.38 = (bf16[4,2112,128]{2,1,0:T(8,128)(2,1)S(1)}, bf16[4,2112,128]{2,1,0:T(8,128)(2,1)S(1)}, u32[]{:S(2)}, u32[]{:S(2)}) collective-permute-start(bf16[4,2112,128]{2,1,0:T(8,128)(2,1)S(1)} %get-tuple-element.256), channel_id=1, source_target_pairs={{0,24},{1,97},{8,0},{9,105},{16,8},{17,113},{24,16},{25,121},{32,5... | collective-permute-start | bytes 6488072 | tf_op jit(solution)/shard_map/ppermute | solution.py:577
  146.3 3.0 %collective-permute-start.30 = (bf16[64,2048]{1,0:T(8,128)(2,1)S(1)}, bf16[64,2048]{1,0:T(8,128)(2,1)S(1)}, u32[]{:S(2)}, u32[]{:S(2)}) collective-permute-start(bf16[64,2048]{1,0:T(8,128)(2,1)S(1)} %get-tuple-element.239.refs_1_), channel_id=1, source_target_pairs={{0,4},{2,6},{4,0},{6,2},{1,5},{3,7},{5,1},{7,3},{8,12},{10,14},{12... | collective-permute-start | bytes 786440 | tf_op jit(solution)/shard_map/ppermute | solution.py:542
  151.3 4.8 %shard_map.319 = (bf16[4,512,256]{2,1,0:T(8,128)(2,1)S(1)}, bf16[4,512,256]{2,1,0:T(8,128)(2,1)S(1)}, f32[8,128]{1,0:T(8,128)S(1)}) custom-call(s32[4]{0:T(128)S(1)} %pad_add_fusion.refs_0_.mine, bf16[704,512]{1,0:T(8,128)(2,1)S(1)} %get-tuple-element.217.product.refs_5_, bf16[704,2048]{1,0:T(8,128)(2,1)S(1)} %bitcast.36, ...), custom_call_target="tpu_custom_call" | custom-call | flops 44000000 | tf_op jit(solution)/shard_map/pallas_call | solution.py:1075
  167.2 2.8 collective-permute-start.36
  173.4 3.3 %shard_map.329 = (bf16[4,1024,128]{2,1,0:T(8,128)(2,1)S(1)}, bf16[4,1024,128]{2,1,0:T(8,128)(2,1)S(1)}, bf16[4,1024,128]{2,1,0:T(8,128)(2,1)S(1)}, bf16[4,1024,128]{2,1,0:T(8,128)(2,1)S(1)}, f32[1,2048]{1,0:T(1,128)S(1)}) custom-call(s32[4]{0:T(128)S(1)} %pad_add_fusion.refs_0_.mine, bf16[512,2048]{1,0:T(8,128)(2,1)S(1)} %get-tuple-element.248.refs_1_, ...), custom_call_target="tpu_custom_call" | custom-call | flops 55000000 | tf_op jit(solution)/shard_map/pallas_call | solution.py:431
  179.9 3.2 %collective-permute-start.42 = (bf16[2,128,256]{2,1,0:T(8,128)(2,1)S(1)}, bf16[2,128,256]{2,1,0:T(8,128)(2,1)S(1)}, u32[]{:S(2)}, u32[]{:S(2)}) collective-permute-start(bf16[2,128,256]{2,1,0:T(8,128)(2,1)S(1)} %get-tuple-element.262.refs_2_), channel_id=1, source_target_pairs={{0,64},{32,96},{64,0},{96,32},{1,65},{33,97},{65,1},{97,33},{2,66}... | collective-permute-start | bytes 393224 | tf_op jit(solution)/shard_map/ppermute | solution.py:542
  183.5 2.8 collective-permute-start.40
  190.5 3.2 %collective-permute-start.47 = (bf16[2112,128]{1,0:T(8,128)(2,1)S(1)}, bf16[2112,128]{1,0:T(8,128)(2,1)S(1)}, u32[]{:S(2)}, u32[]{:S(2)}) collective-permute-start(bf16[2112,128]{1,0:T(8,128)(2,1)S(1)} %get-tuple-element.307), channel_id=1, source_target_pairs={{0,96},{1,25},{8,104},{9,1},{16,112},{17,9},{24,120},{25,17},{32,0... | collective-permute-start | bytes 1622024 | tf_op jit(solution)/shard_map/ppermute | solution.py:577
  194.0 3.1 %collective-permute-start.39 = (bf16[2,512,256]{2,1,0:T(8,128)(2,1)}, bf16[2,512,256]{2,1,0:T(8,128)(2,1)S(1)}, u32[]{:S(2)}, u32[]{:S(2)}) collective-permute-start(bf16[2,512,256]{2,1,0:T(8,128)(2,1)} %get-tuple-element.260), channel_id=1, source_target_pairs={{0,4},{2,6},{4,0},{6,2},{1,5},{3,7},{5,1},{7,3},{8,12},{10,14},{12... | collective-permute-start | bytes 1572872 | tf_op jit(solution)/shard_map/ppermute | solution.py:716
  197.1 8.0 %shard_map.335 = (bf16[528,1024]{1,0:T(8,128)(2,1)S(1)}, bf16[16,1024]{1,0:T(8,128)(2,1)S(1)}, f32[512,2]{1,0:T(8,128)S(1)}, f32[16,528]{1,0:T(8,128)S(1)}, f32[8,1024]{1,0:T(8,128)S(1)}, /*index=5*/f32[528,1]{1,0:T(8,128)S(1)}) custom-call(s32[4]{0:T(128)S(1)} %pad_add_fusion.refs_0_.mine, bf16[4,2,144,384]{3,2,1,0:T(8,128)(2,1)S(1)} %copy-done.15, ...), custom_call_target="tpu_custom_call" | custom-call | flops 121000000 | tf_op jit(solution)/shard_map/pallas_call | solution.py:431
  206.4 4.6 %shard_map.336 = (bf16[4,2112,128]{2,1,0:T(8,128)(2,1)S(1)}, bf16[4,2112,128]{2,1,0:T(8,128)(2,1)S(1)}, bf16[4,2112,128]{2,1,0:T(8,128)(2,1)S(1)}, bf16[4,1056,1...) custom-call(s32[4]{0:T(128)S(1)} %pad_add_fusion.refs_0_.mine, ...), custom_call_target="tpu_custom_call" | custom-call | flops 66000000 | tf_op jit(solution)/shard_map/pallas_call | solution.py:431
  213.6 2.7 collective-permute-start.50
  217.2 6.9 %shard_map.341 = (bf16[4,528,256]{2,1,0:T(8,128)(2,1)S(1)}, bf16[4,528,256]{2,1,0:T(8,128)(2,1)S(1)}, f32[8,128]{1,0:T(8,128)S(1)}) custom-call(s32[4]{0:T(128)S(1)} %pad_add_fusion.refs_0_.mine, bf16[528,1024]{1,0:T(8,128)(2,1)S(1)} %get-tuple-element.283.refs_3_.dproj, bf16[16,1024]{1,0:T(8,128)(2,1)S(1)} %collective-permute-done.44.refs_6_.arrived, ...), custom_call_target="tpu_custom_call" | custom-call | flops 66000000 | tf_op jit(solution)/shard_map/pallas_call | solution.py:1132
  225.8 4.2 %collective-permute-done.50.refs_3_ = bf16[4,1056,128]{2,1,0:T(8,128)(2,1)S(1)} collective-permute-done((bf16[4,1056,128]{2,1,0:T(8,128)(2,1)S(1)}, bf16[4,1056,128]{2,1,0:T(8,128)(2,1)S(1)}, u32[]{:S(2)}, u32[]{:S(2)}) %collective-permute-start.50) | collective-permute-done | bytes 1081376 | tf_op jit(solution)/shard_map/ppermute | solution.py:577
  236.6 5.1 %collective-permute-done.54.refs_3_ = f32[3,4,8,128]{3,2,1,0:T(8,128)S(1)} collective-permute-done((f32[3,4,8,128]{3,2,1,0:T(8,128)S(1)}, f32[3,4,8,128]{3,2,1,0:T(8,128)S(1)}, u32[]{:S(2)}, u32[]{:S(2)}) %collective-permute-start.54) | collective-permute-done | bytes 49184 | tf_op jit(solution)/shard_map/ppermute | solution.py:542
  241.7 4.1 %collective-permute-done.52.refs_1_ = f32[3,4,8,128]{3,2,1,0:T(8,128)S(1)} collective-permute-done((f32[3,4,8,128]{3,2,1,0:T(8,128)S(1)}, f32[3,4,8,128]{3,2,1,0:T(8,128)S(1)}, u32[]{:S(2)}, u32[]{:S(2)}) %collective-permute-start.52) | collective-permute-done | bytes 49184 | tf_op jit(solution)/shard_map/ppermute | solution.py:542
  252.0 8.9 %collective-permute-done.59.refs_5_ = f32[4,8,128]{2,1,0:T(8,128)S(1)} collective-permute-done((f32[4,8,128]{2,1,0:T(8,128)S(1)}, f32[4,8,128]{2,1,0:T(8,128)S(1)}, u32[]{:S(2)}, u32[]{:S(2)}) %collective-permute-start.59) | collective-permute-done | bytes 16416 | tf_op jit(solution)/shard_map/ppermute | solution.py:577
  269.5 6.5 %collective-permute-done.56.refs_2_ = bf16[528,256]{1,0:T(8,128)(2,1)S(1)} collective-permute-done((bf16[528,256]{1,0:T(8,128)(2,1)S(1)}, bf16[528,256]{1,0:T(8,128)(2,1)S(1)}, u32[]{:S(2)}, u32[]{:S(2)}) %collective-permute-start.56) | collective-permute-done | bytes 270368 | tf_op jit(solution)/shard_map/ppermute | solution.py:716
  (215 shorter events, 133.3 us)
Async XLA Ops:
  0.7 12.7 %collective-permute-start.2 = (bf16[512,256]{1,0:T(8,128)(2,1)}, bf16[512,256]{1,0:T(8,128)(2,1)S(1)}, u32[]{:S(2)}, u32[]{:S(2)}) collective-permute-start(bf16[512,256]{1,0:T(8,128)(2,1)} %refs_3_.3), channel_id=1, source_target_pairs={{0,4},{2,6},{4,0},{6,2},{1,5},{3,7},{5,1},{7,3},{8,12},{10,14},{12... | collective-permute-start | bytes 786440 | tf_op jit(solution)/shard_map/ppermute | solution.py:542
  2.9 13.3 %collective-permute-start.1 = (bf16[512,256]{1,0:T(8,128)(2,1)}, bf16[512,256]{1,0:T(8,128)(2,1)S(1)}, u32[]{:S(2)}, u32[]{:S(2)}) collective-permute-start(bf16[512,256]{1,0:T(8,128)(2,1)} %refs_3_.3), channel_id=1, source_target_pairs={{0,2},{2,4},{4,6},{6,0},{1,3},{3,5},{5,7},{7,1},{8,10},{10,12},{12... | collective-permute-start | bytes 786440 | tf_op jit(solution)/shard_map/ppermute | solution.py:542
  2.9 13.3 %collective-permute-start = (bf16[512,256]{1,0:T(8,128)(2,1)}, bf16[512,256]{1,0:T(8,128)(2,1)S(1)}, u32[]{:S(2)}, u32[]{:S(2)}) collective-permute-start(bf16[512,256]{1,0:T(8,128)(2,1)} %refs_3_.3), channel_id=1, source_target_pairs={{0,6},{2,0},{4,2},{6,4},{1,7},{3,1},{5,3},{7,5},{8,14},{10,8},{12,... | collective-permute-start | bytes 786440 | tf_op jit(solution)/shard_map/ppermute | solution.py:542
  60.2 14.0 %collective-permute-start.17 = (bf16[512,256]{1,0:T(8,128)(2,1)S(1)}, bf16[512,256]{1,0:T(8,128)(2,1)S(1)}, u32[]{:S(2)}, u32[]{:S(2)}) collective-permute-start(bf16[512,256]{1,0:T(8,128)(2,1)S(1)} %shard_map.313.refs_1_), channel_id=1, source_target_pairs={{0,4},{2,6},{4,0},{6,2},{1,5},{3,7},{5,1},{7,3},{8,12},{10,14},{12... | collective-permute-start | bytes 786440 | tf_op jit(solution)/shard_map/ppermute | solution.py:542
  62.3 11.9 %collective-permute-start.16 = (bf16[512,256]{1,0:T(8,128)(2,1)S(1)}, bf16[512,256]{1,0:T(8,128)(2,1)S(1)}, u32[]{:S(2)}, u32[]{:S(2)}) collective-permute-start(bf16[512,256]{1,0:T(8,128)(2,1)S(1)} %shard_map.313.refs_1_), channel_id=1, source_target_pairs={{0,2},{2,4},{4,6},{6,0},{1,3},{3,5},{5,7},{7,1},{8,10},{10,12},{12... | collective-permute-start | bytes 786440 | tf_op jit(solution)/shard_map/ppermute | solution.py:542
  63.2 11.2 %collective-permute-start.15 = (bf16[512,256]{1,0:T(8,128)(2,1)S(1)}, bf16[512,256]{1,0:T(8,128)(2,1)S(1)}, u32[]{:S(2)}, u32[]{:S(2)}) collective-permute-start(bf16[512,256]{1,0:T(8,128)(2,1)S(1)} %shard_map.313.refs_1_), channel_id=1, source_target_pairs={{0,6},{2,0},{4,2},{6,4},{1,7},{3,1},{5,3},{7,5},{8,14},{10,8},{12,... | collective-permute-start | bytes 786440 | tf_op jit(solution)/shard_map/ppermute | solution.py:542
  80.2 13.7 %collective-permute-start.14 = (bf16[64,2048]{1,0:T(8,128)(2,1)S(1)}, bf16[64,2048]{1,0:T(8,128)(2,1)S(1)}, u32[]{:S(2)}, u32[]{:S(2)}) collective-permute-start(bf16[64,2048]{1,0:T(8,128)(2,1)S(1)} %get-tuple-element.211), channel_id=1, source_target_pairs={{0,4},{2,6},{4,0},{6,2},{1,5},{3,7},{5,1},{7,3},{8,12},{10,14},{12... | collective-permute-start | bytes 786440 | tf_op jit(solution)/shard_map/ppermute | solution.py:542
  94.2 10.9 %collective-permute-start.21 = (bf16[64,2048]{1,0:T(8,128)(2,1)S(1)}, bf16[64,2048]{1,0:T(8,128)(2,1)S(1)}, u32[]{:S(2)}, u32[]{:S(2)}) collective-permute-start(bf16[64,2048]{1,0:T(8,128)(2,1)S(1)} %get-tuple-element.215.refs_1_), channel_id=1, source_target_pairs={{0,4},{2,6},{4,0},{6,2},{1,5},{3,7},{5,1},{7,3},{8,12},{10,14},{12... | collective-permute-start | bytes 786440 | tf_op jit(solution)/shard_map/ppermute | solution.py:542
  96.1 11.1 %collective-permute-start.20 = (bf16[64,2048]{1,0:T(8,128)(2,1)S(1)}, bf16[64,2048]{1,0:T(8,128)(2,1)S(1)}, u32[]{:S(2)}, u32[]{:S(2)}) collective-permute-start(bf16[64,2048]{1,0:T(8,128)(2,1)S(1)} %get-tuple-element.215.refs_1_), channel_id=1, source_target_pairs={{0,2},{2,4},{4,6},{6,0},{1,3},{3,5},{5,7},{7,1},{8,10},{10,12},{12... | collective-permute-start | bytes 786440 | tf_op jit(solution)/shard_map/ppermute | solution.py:542
  96.6 12.0 %collective-permute-start.19 = (bf16[64,2048]{1,0:T(8,128)(2,1)S(1)}, bf16[64,2048]{1,0:T(8,128)(2,1)S(1)}, u32[]{:S(2)}, u32[]{:S(2)}) collective-permute-start(bf16[64,2048]{1,0:T(8,128)(2,1)S(1)} %get-tuple-element.215.refs_1_), channel_id=1, source_target_pairs={{0,6},{2,0},{4,2},{6,4},{1,7},{3,1},{5,3},{7,5},{8,14},{10,8},{12,... | collective-permute-start | bytes 786440 | tf_op jit(solution)/shard_map/ppermute | solution.py:542
  121.9 19.5 %collective-permute-start.31 = (bf16[4,1056,128]{2,1,0:T(8,128)(2,1)S(1)}, bf16[4,1056,128]{2,1,0:T(8,128)(2,1)S(1)}, u32[]{:S(2)}, u32[]{:S(2)}) collective-permute-start(bf16[4,1056,128]{2,1,0:T(8,128)(2,1)S(1)} %get-tuple-element.243), channel_id=1, source_target_pairs={{0,8},{1,33},{8,16},{9,41},{16,24},{17,49},{24,0},{25,57},{32,40},... | collective-permute-start | bytes 3244040 | tf_op jit(solution)/shard_map/ppermute | solution.py:577
  122.2 19.2 %collective-permute-start.32 = (bf16[4,1056,128]{2,1,0:T(8,128)(2,1)S(1)}, bf16[4,1056,128]{2,1,0:T(8,128)(2,1)S(1)}, u32[]{:S(2)}, u32[]{:S(2)}) collective-permute-start(bf16[4,1056,128]{2,1,0:T(8,128)(2,1)S(1)} %get-tuple-element.244), channel_id=1, source_target_pairs={{0,24},{1,97},{8,0},{9,105},{16,8},{17,113},{24,16},{25,121},{32,5... | collective-permute-start | bytes 3244040 | tf_op jit(solution)/shard_map/ppermute | solution.py:577
  128.0 12.9 %collective-permute-start.27 = (bf16[64,2048]{1,0:T(8,128)(2,1)S(1)}, bf16[64,2048]{1,0:T(8,128)(2,1)S(1)}, u32[]{:S(2)}, u32[]{:S(2)}) collective-permute-start(bf16[64,2048]{1,0:T(8,128)(2,1)S(1)} %get-tuple-element.236), channel_id=1, source_target_pairs={{0,4},{2,6},{4,0},{6,2},{1,5},{3,7},{5,1},{7,3},{8,12},{10,14},{12... | collective-permute-start | bytes 786440 | tf_op jit(solution)/shard_map/ppermute | solution.py:542
  143.1 28.2 %collective-permute-start.37 = (bf16[4,2112,128]{2,1,0:T(8,128)(2,1)}, bf16[4,2112,128]{2,1,0:T(8,128)(2,1)S(1)}, u32[]{:S(2)}, u32[]{:S(2)}) collective-permute-start(bf16[4,2112,128]{2,1,0:T(8,128)(2,1)} %get-tuple-element.255), channel_id=1, source_target_pairs={{0,8},{1,33},{8,16},{9,41},{16,24},{17,49},{24,0},{25,57},{32,40},... | collective-permute-start | bytes 6488072 | tf_op jit(solution)/shard_map/ppermute | solution.py:577
  143.4 33.2 %collective-permute-start.38 = (bf16[4,2112,128]{2,1,0:T(8,128)(2,1)S(1)}, bf16[4,2112,128]{2,1,0:T(8,128)(2,1)S(1)}, u32[]{:S(2)}, u32[]{:S(2)}) collective-permute-start(bf16[4,2112,128]{2,1,0:T(8,128)(2,1)S(1)} %get-tuple-element.256), channel_id=1, source_target_pairs={{0,24},{1,97},{8,0},{9,105},{16,8},{17,113},{24,16},{25,121},{32,5... | collective-permute-start | bytes 6488072 | tf_op jit(solution)/shard_map/ppermute | solution.py:577
  146.3 11.7 %collective-permute-start.30 = (bf16[64,2048]{1,0:T(8,128)(2,1)S(1)}, bf16[64,2048]{1,0:T(8,128)(2,1)S(1)}, u32[]{:S(2)}, u32[]{:S(2)}) collective-permute-start(bf16[64,2048]{1,0:T(8,128)(2,1)S(1)} %get-tuple-element.239.refs_1_), channel_id=1, source_target_pairs={{0,4},{2,6},{4,0},{6,2},{1,5},{3,7},{5,1},{7,3},{8,12},{10,14},{12... | collective-permute-start | bytes 786440 | tf_op jit(solution)/shard_map/ppermute | solution.py:542
  160.5 28.4 %collective-permute-start.23 = (bf16[4,512,256]{2,1,0:T(8,128)(2,1)S(1)}, bf16[4,512,256]{2,1,0:T(8,128)(2,1)S(1)}, u32[]{:S(2)}, u32[]{:S(2)}) collective-permute-start(bf16[4,512,256]{2,1,0:T(8,128)(2,1)S(1)} %get-tuple-element.220), channel_id=1, source_target_pairs={{0,1},{1,0},{2,3},{3,2},{4,5},{5,4},{6,7},{7,6},{8,9},{9,8},{10,11... | collective-permute-start | bytes 3145736 | tf_op jit(solution)/shard_map/ppermute | solution.py:542
  167.2 10.9 %collective-permute-start.36 = (bf16[2,128,256]{2,1,0:T(8,128)(2,1)S(1)}, bf16[2,128,256]{2,1,0:T(8,128)(2,1)S(1)}, u32[]{:S(2)}, u32[]{:S(2)}) collective-permute-start(bf16[2,128,256]{2,1,0:T(8,128)(2,1)S(1)} %get-tuple-element.250.refs_2_), channel_id=1, source_target_pairs={{0,16},{8,24},{16,0},{24,8},{1,17},{9,25},{17,1},{25,9},{2,18},{10... | collective-permute-start | bytes 393224 | tf_op jit(solution)/shard_map/ppermute | solution.py:542
  190.4 21.4 %collective-permute-start.46 = (bf16[2112,128]{1,0:T(8,128)(2,1)S(1)}, bf16[2112,128]{1,0:T(8,128)(2,1)S(1)}, u32[]{:S(2)}, u32[]{:S(2)}) collective-permute-start(bf16[2112,128]{1,0:T(8,128)(2,1)S(1)} %get-tuple-element.306), channel_id=1, source_target_pairs={{0,32},{1,9},{8,40},{9,17},{16,48},{17,25},{24,56},{25,1},{32,64},... | collective-permute-start | bytes 1622024 | tf_op jit(solution)/shard_map/ppermute | solution.py:577
  190.5 21.3 %collective-permute-start.47 = (bf16[2112,128]{1,0:T(8,128)(2,1)S(1)}, bf16[2112,128]{1,0:T(8,128)(2,1)S(1)}, u32[]{:S(2)}, u32[]{:S(2)}) collective-permute-start(bf16[2112,128]{1,0:T(8,128)(2,1)S(1)} %get-tuple-element.307), channel_id=1, source_target_pairs={{0,96},{1,25},{8,104},{9,1},{16,112},{17,9},{24,120},{25,17},{32,0... | collective-permute-start | bytes 1622024 | tf_op jit(solution)/shard_map/ppermute | solution.py:577
  193.7 18.1 %collective-permute-start.48 = (bf16[2112,128]{1,0:T(8,128)(2,1)S(1)}, bf16[2112,128]{1,0:T(8,128)(2,1)S(1)}, u32[]{:S(2)}, u32[]{:S(2)}) collective-permute-start(bf16[2112,128]{1,0:T(8,128)(2,1)S(1)} %get-tuple-element.308), channel_id=1, source_target_pairs={{0,64},{1,17},{8,72},{9,25},{16,80},{17,1},{24,88},{25,9},{32,96},... | collective-permute-start | bytes 1622024 | tf_op jit(solution)/shard_map/ppermute | solution.py:577
  194.0 17.1 %collective-permute-start.39 = (bf16[2,512,256]{2,1,0:T(8,128)(2,1)}, bf16[2,512,256]{2,1,0:T(8,128)(2,1)S(1)}, u32[]{:S(2)}, u32[]{:S(2)}) collective-permute-start(bf16[2,512,256]{2,1,0:T(8,128)(2,1)} %get-tuple-element.260), channel_id=1, source_target_pairs={{0,4},{2,6},{4,0},{6,2},{1,5},{3,7},{5,1},{7,3},{8,12},{10,14},{12... | collective-permute-start | bytes 1572872 | tf_op jit(solution)/shard_map/ppermute | solution.py:716
  213.6 16.4 %collective-permute-start.50 = (bf16[4,1056,128]{2,1,0:T(8,128)(2,1)S(1)}, bf16[4,1056,128]{2,1,0:T(8,128)(2,1)S(1)}, u32[]{:S(2)}, u32[]{:S(2)}) collective-permute-start(bf16[4,1056,128]{2,1,0:T(8,128)(2,1)S(1)} %get-tuple-element.317), channel_id=1, source_target_pairs={{0,8},{1,33},{8,16},{9,41},{16,24},{17,49},{24,0},{25,57},{32,40},... | collective-permute-start | bytes 3244040 | tf_op jit(solution)/shard_map/ppermute | solution.py:577
  216.3 15.2 %collective-permute-start.51 = (bf16[4,1056,128]{2,1,0:T(8,128)(2,1)S(1)}, bf16[4,1056,128]{2,1,0:T(8,128)(2,1)S(1)}, u32[]{:S(2)}, u32[]{:S(2)}) collective-permute-start(bf16[4,1056,128]{2,1,0:T(8,128)(2,1)S(1)} %get-tuple-element.318), channel_id=1, source_target_pairs={{0,24},{1,97},{8,0},{9,105},{16,8},{17,113},{24,16},{25,121},{32,5... | collective-permute-start | bytes 3244040 | tf_op jit(solution)/shard_map/ppermute | solution.py:577
  232.7 28.8 %collective-permute-start.57 = (bf16[4,2112,128]{2,1,0:T(8,128)(2,1)S(1)}, bf16[4,2112,128]{2,1,0:T(8,128)(2,1)S(1)}, u32[]{:S(2)}, u32[]{:S(2)}) collective-permute-start(bf16[4,2112,128]{2,1,0:T(8,128)(2,1)S(1)} %get-tuple-element.330), channel_id=1, source_target_pairs={{0,8},{1,33},{8,16},{9,41},{16,24},{17,49},{24,0},{25,57},{32,40},... | collective-permute-start | bytes 6488072 | tf_op jit(solution)/shard_map/ppermute | solution.py:577
  234.6 26.9 %collective-permute-start.58 = (bf16[4,2112,128]{2,1,0:T(8,128)(2,1)S(1)}, bf16[4,2112,128]{2,1,0:T(8,128)(2,1)S(1)}, u32[]{:S(2)}, u32[]{:S(2)}) collective-permute-start(bf16[4,2112,128]{2,1,0:T(8,128)(2,1)S(1)} %get-tuple-element.331), channel_id=1, source_target_pairs={{0,24},{1,97},{8,0},{9,105},{16,8},{17,113},{24,16},{25,121},{32,5... | collective-permute-start | bytes 6488072 | tf_op jit(solution)/shard_map/ppermute | solution.py:577
  247.0 21.5 %collective-permute-start.55 = (bf16[2,528,256]{2,1,0:T(8,128)(2,1)S(1)}, bf16[2,528,256]{2,1,0:T(8,128)(2,1)S(1)}, u32[]{:S(2)}, u32[]{:S(2)}) collective-permute-start(bf16[2,528,256]{2,1,0:T(8,128)(2,1)S(1)} %get-tuple-element.325), channel_id=1, source_target_pairs={{0,4},{2,6},{4,0},{6,2},{1,5},{3,7},{5,1},{7,3},{8,12},{10,14},{12... | collective-permute-start | bytes 1622024 | tf_op jit(solution)/shard_map/ppermute | solution.py:716
  248.7 12.2 %collective-permute-start.59 = (f32[4,8,128]{2,1,0:T(8,128)S(1)}, f32[4,8,128]{2,1,0:T(8,128)S(1)}, u32[]{:S(2)}, u32[]{:S(2)}) collective-permute-start(f32[4,8,128]{2,1,0:T(8,128)S(1)} %get-tuple-element.333), channel_id=1, source_target_pairs={{0,8},{1,33},{8,16},{9,41},{16,24},{17,49},{24,0},{25,57},{32,40},... | collective-permute-start | bytes 49160 | tf_op jit(solution)/shard_map/ppermute | solution.py:577
  249.4 12.2 %collective-permute-start.60 = (f32[4,8,128]{2,1,0:T(8,128)S(1)}, f32[4,8,128]{2,1,0:T(8,128)S(1)}, u32[]{:S(2)}, u32[]{:S(2)}) collective-permute-start(f32[4,8,128]{2,1,0:T(8,128)S(1)} %get-tuple-element.334), channel_id=1, source_target_pairs={{0,24},{1,97},{8,0},{9,105},{16,8},{17,113},{24,16},{25,121},{32,5... | collective-permute-start | bytes 49160 | tf_op jit(solution)/shard_map/ppermute | solution.py:577
  263.1 14.6 %collective-permute-start.61 = (bf16[2112,128]{1,0:T(8,128)(2,1)S(1)}, bf16[2112,128]{1,0:T(8,128)(2,1)S(1)}, u32[]{:S(2)}, u32[]{:S(2)}) collective-permute-start(bf16[2112,128]{1,0:T(8,128)(2,1)S(1)} %get-tuple-element.336), channel_id=1, source_target_pairs={{0,32},{1,9},{8,40},{9,17},{16,48},{17,25},{24,56},{25,1},{32,64},... | collective-permute-start | bytes 1622024 | tf_op jit(solution)/shard_map/ppermute | solution.py:577
  264.5 14.5 %collective-permute-start.62 = (bf16[2112,128]{1,0:T(8,128)(2,1)S(1)}, bf16[2112,128]{1,0:T(8,128)(2,1)S(1)}, u32[]{:S(2)}, u32[]{:S(2)}) collective-permute-start(bf16[2112,128]{1,0:T(8,128)(2,1)S(1)} %get-tuple-element.337), channel_id=1, source_target_pairs={{0,96},{1,25},{8,104},{9,1},{16,112},{17,9},{24,120},{25,17},{32,0... | collective-permute-start | bytes 1622024 | tf_op jit(solution)/shard_map/ppermute | solution.py:577
  266.3 14.4 %collective-permute-start.63 = (bf16[2112,128]{1,0:T(8,128)(2,1)S(1)}, bf16[2112,128]{1,0:T(8,128)(2,1)S(1)}, u32[]{:S(2)}, u32[]{:S(2)}) collective-permute-start(bf16[2112,128]{1,0:T(8,128)(2,1)S(1)} %get-tuple-element.338), channel_id=1, source_target_pairs={{0,64},{1,17},{8,72},{9,25},{16,80},{17,1},{24,88},{25,9},{32,96},... | collective-permute-start | bytes 1622024 | tf_op jit(solution)/shard_map/ppermute | solution.py:577
  (65 other events, 571.9 us)

commit v4 on v3

--- a/solution.py
+++ b/solution.py
@@ -731,12 +731,12 @@
     send[...] = (keep[1 - at].astype(FLOAT) + arrived[1 - at].astype(FLOAT)).astype(HALF)
 
 
-def first_halves(own, other, mine, after):
+def first_halves(own, arrived, mine, after):
     pair = out((2, *own.shape[1:]), HALF)
     return run(
         first_half_kernel,
         (pair, pair, out((8, DK), FLOAT)),
-        (mine, own, rotated(other, "c", 1)),
+        (mine, own, arrived),
         scalars=1,
         after=after,
     )
@@ -1311,11 +1311,13 @@
         (mine, *head_gather(d_hidden, mine, (down_token, ffn_token, own_token))),
         scalars=1,
     )
+    down_arrived = rotated(down_other, "c", 1)
     d_gated = jnp.dot(d_branch, mixer_weight, preferred_element_type=FLOAT)
     dos, dvns, es, d_gate_pre, gain_part, gate_sums, ends = run(
         partial(gate_back_kernel, heads, chunks),
         gate_back_shapes(heads, chunks),
         (d_gated, mixed, gate_pre, gain_row, q, w, p, n, gcol),
+        after=(down_arrived,),
         micros=4.0,
     )
     *ffn_sums, ffn_token = seq_sums((ffn_own, *ffn_group[1:]), (), mine, (), 3.0)
@@ -1337,7 +1339,7 @@
         micros=2.0,
     )
     end_pieces = ring_pieces(group_end, "y")
-    out_keep, out_send, out_token = first_halves(down_own, down_other, mine, (group_token,))
+    out_keep, out_send, out_token = first_halves(down_own, down_arrived, mine, (group_token,))
     square = out((heads * chunks, CH, CH), FLOAT)
     *slopes, slope_token = run(
         partial(slopes_kernel, heads, chunks),
@@ -1394,7 +1396,7 @@
     own_rows, plus_rows, minus_rows, gain_token = run(
         quad_sum_kernel, (out((4, 8, DK), FLOAT),) * 3 + (token_out,), ring_pieces(rows_left, "x"), after=(in_token,)
     )
-    first_keep, first_send, _ = first_halves(first_own, first_other, mine, (gain_token,))
+    first_keep, first_send, _ = first_halves(first_own, rotated(first_other, "c", 1), mine, (gain_token,))
     first_mine, first_send, _ = second_halves(first_keep, swapped(first_send, 2), mine, ())
     *sums_out, sum_token = run(
         last_sum_kernel,

time: 287 us -> 285 us (level)
  transfers between devices with their start and end apart: 64 -> 64, of which waited for: 31 -> 31; matrix products, arithmetic and copies ran while one was open for 2% -> 2% of each run, Pallas kernels for 24% -> 23%
where the time goes in v4:
time: 285 us; the launch traced here: 280 us
  Pallas kernels  92.1 us (32%)
  starting transfers between devices  87.7 us (31%)
  waiting for transfers between devices  85.9 us (30%)
  local copies, waits for them, and re-layouts  7.01 us (2%)
  matrix products  6.1 us (2%)
    pallas_call x40, Pallas kernels, run(): pl.pallas_call(body, out_shape=tuple((pltpu.HBM(a.shape, a.dtype) if i in...  79.8 us
    ppermute x42, waiting for transfers between devices, rotated(): lax.ppermute(array, axis, [(i, (i + distance) % size) for i in range(size)])  61.1 us
    ppermute x42, starting transfers between devices, rotated(): lax.ppermute(array, axis, [(i, (i + distance) % size) for i in range(size)])  50.9 us
    ppermute x16, starting transfers between devices, turned(): return lax.ppermute(array, PLANE, pairs)  26 us
    ppermute x16, waiting for transfers between devices, turned(): return lax.ppermute(array, PLANE, pairs)  18.1 us
    pallas_call x1, Pallas kernels, d_first_tiles(): pl.pallas_call(d_first_kernel, grid_spec=spec, out_shape=(tiles, tiles, o...  6.9 us
    ppermute x4, waiting for transfers between devices, swapped(): return lax.ppermute(array, 'x', [(i, i ^ mask) for i in range(4)])  6.66 us
    unnamed x66, local copies, waits for them, and re-layouts  6.48 us
  transfers between devices with their start and end apart: 64, of which 31 were waited for; matrix products, arithmetic and copies ran while one was open for 2% of the time, Pallas kernels for 23%

profile of v4, /device:TPU:2, one launch (start us, length us, event | category | flops | bytes accessed | tf_op | source)
XLA Modules:
  0.0 280.5 jit_solution(11029755984629765655)
XLA Ops:
  13.3 2.8 %collective-permute-done.1.refs_3_ = bf16[512,256]{1,0:T(8,128)(2,1)S(1)} collective-permute-done((bf16[512,256]{1,0:T(8,128)(2,1)}, bf16[512,256]{1,0:T(8,128)(2,1)S(1)}, u32[]{:S(2)}, u32[]{:S(2)}) %collective-permute-start.1) | collective-permute-done | bytes 262176 | tf_op jit(solution)/shard_map/ppermute | solution.py:542
  22.1 4.3 %collective-permute-start.4 = (bf16[16,2048]{1,0:T(8,128)(2,1)S(1)}, bf16[16,2048]{1,0:T(8,128)(2,1)S(1)}, u32[]{:S(2)}, u32[]{:S(2)}) collective-permute-start(bf16[16,2048]{1,0:T(8,128)(2,1)S(1)} %get-tuple-element.189), channel_id=1, source_target_pairs={{0,8},{8,16},{16,24},{24,32},{32,40},{40,48},{48,56},{56,64},{64,7... | collective-permute-start | bytes 196616 | tf_op jit(solution)/shard_map/ppermute | solution.py:1158
  30.0 8.2 %shard_map.308 = (bf16[512,256]{1,0:T(8,128)(2,1)}, bf16[512,512]{1,0:T(8,128)(2,1)}, bf16[8,128,128]{2,1,0:T(8,128)(2,1)}, bf16[8,128,128]{2,1,0:T(8,128)(2,1)}...) custom-call(bf16[512,1024]{1,0:T(8,128)(2,1)S(1)} %convolution_conve, ...), custom_call_target="tpu_custom_call" | custom-call | flops 88000000 | tf_op jit(solution)/shard_map/pallas_call | solution.py:431
  38.2 3.6 %collective-permute-start.7 = (bf16[2,144,384]{2,1,0:T(8,128)(2,1)S(1)}, bf16[2,144,384]{2,1,0:T(8,128)(2,1)S(1)}, u32[]{:S(2)}, u32[]{:S(2)}) collective-permute-start(bf16[2,144,384]{2,1,0:T(8,128)(2,1)S(1)} %get-tuple-element.193.refs_1_), channel_id=1, source_target_pairs={{0,16},{8,24},{16,0},{24,8},{1,17},{9,25},{17,1},{25,9},{2,18},{10... | collective-permute-start | bytes 663560 | tf_op jit(solution)/shard_map/ppermute | solution.py:542
  48.0 3.9 %collective-permute-done.6.refs_3_ = bf16[2,144,384]{2,1,0:T(8,128)(2,1)S(1)} collective-permute-done((bf16[2,144,384]{2,1,0:T(8,128)(2,1)S(1)}, bf16[2,144,384]{2,1,0:T(8,128)(2,1)S(1)}, u32[]{:S(2)}, u32[]{:S(2)}) %collective-permute-start.6) | collective-permute-done | bytes 221216 | tf_op jit(solution)/shard_map/ppermute | solution.py:542
  53.2 3.7 %collective-permute-start.10 = (bf16[2,144,384]{2,1,0:T(8,128)(2,1)S(1)}, bf16[2,144,384]{2,1,0:T(8,128)(2,1)S(1)}, u32[]{:S(2)}, u32[]{:S(2)}) collective-permute-start(bf16[2,144,384]{2,1,0:T(8,128)(2,1)S(1)} %get-tuple-element.198.refs_1_), channel_id=1, source_target_pairs={{0,64},{32,96},{64,0},{96,32},{1,65},{33,97},{65,1},{97,33},{2,66}... | collective-permute-start | bytes 663560 | tf_op jit(solution)/shard_map/ppermute | solution.py:542
  68.6 5.7 %shard_map.311 = (bf16[8,128,256]{2,1,0:T(8,128)(2,1)}, bf16[8,128,256]{2,1,0:T(8,128)(2,1)}, f32[512,512]{1,0:T(8,128)}, bf16[512,512]{1,0:T(8,128)(2,1)S(1)}, ...) custom-call(s32[4]{0:T(128)S(1)} %pad_add_fusion.refs_0_.mine, ...), custom_call_target="tpu_custom_call" | custom-call | flops 44000000 | tf_op jit(solution)/shard_map/pallas_call | solution.py:431
  87.3 6.6 %collective-permute-done.14.refs_5_ = bf16[64,2048]{1,0:T(8,128)(2,1)S(1)} collective-permute-done((bf16[64,2048]{1,0:T(8,128)(2,1)S(1)}, bf16[64,2048]{1,0:T(8,128)(2,1)S(1)}, u32[]{:S(2)}, u32[]{:S(2)}) %collective-permute-start.14) | collective-permute-done | bytes 262176 | tf_op jit(solution)/shard_map/ppermute | solution.py:542
  98.3 6.8 %collective-permute-done.21.refs_4_ = bf16[64,2048]{1,0:T(8,128)(2,1)S(1)} collective-permute-done((bf16[64,2048]{1,0:T(8,128)(2,1)S(1)}, bf16[64,2048]{1,0:T(8,128)(2,1)S(1)}, u32[]{:S(2)}, u32[]{:S(2)}) %collective-permute-start.21) | collective-permute-done | bytes 262176 | tf_op jit(solution)/shard_map/ppermute | solution.py:542
  111.9 7.8 %shard_map.318 = (bf16[512,2048]{1,0:T(8,128)(2,1)S(1)}, bf16[704,512]{1,0:T(8,128)(2,1)S(1)}, bf16[704,512]{1,0:T(8,128)(2,1)S(1)}, bf16[704,512]{1,0:T(8,128)(...) custom-call(s32[4]{0:T(128)S(1)} %pad_add_fusion.refs_0_.mine, ...), custom_call_target="tpu_custom_call" | custom-call | flops 99000000 | tf_op jit(solution)/shard_map/pallas_call | solution.py:431
  122.2 2.9 %collective-permute-start.32 = (bf16[4,1056,128]{2,1,0:T(8,128)(2,1)S(1)}, bf16[4,1056,128]{2,1,0:T(8,128)(2,1)S(1)}, u32[]{:S(2)}, u32[]{:S(2)}) collective-permute-start(bf16[4,1056,128]{2,1,0:T(8,128)(2,1)S(1)} %get-tuple-element.244), channel_id=1, source_target_pairs={{0,24},{1,97},{8,0},{9,105},{16,8},{17,113},{24,16},{25,121},{32,5... | collective-permute-start | bytes 3244040 | tf_op jit(solution)/shard_map/ppermute | solution.py:577
  130.0 3.0 %shard_map.322 = (bf16[4,2112,128]{2,1,0:T(8,128)(2,1)S(1)}, bf16[4,2112,128]{2,1,0:T(8,128)(2,1)S(1)}, f32[8,128]{1,0:T(8,128)S(1)}) custom-call(s32[4]{0:T(128)S(1)} %pad_add_fusion.refs_0_.mine, bf16[512,2048]{1,0:T(8,128)(2,1)S(1)} %get-tuple-element.227.refs_1_, bf16[512,2048]{1,0:T(8,128)(2,1)S(1)} %get-tuple-element.228.refs_2_, ...), custom_call_target="tpu_custom_call" | custom-call | flops 11000000 | tf_op jit(solution)/shard_map/pallas_call | solution.py:431
  135.2 5.7 %collective-permute-done.27.refs_7_ = bf16[64,2048]{1,0:T(8,128)(2,1)S(1)} collective-permute-done((bf16[64,2048]{1,0:T(8,128)(2,1)S(1)}, bf16[64,2048]{1,0:T(8,128)(2,1)S(1)}, u32[]{:S(2)}, u32[]{:S(2)}) %collective-permute-start.27) | collective-permute-done | bytes 262176 | tf_op jit(solution)/shard_map/ppermute | solution.py:542
  142.4 2.9 %collective-permute-start.38 = (bf16[4,2112,128]{2,1,0:T(8,128)(2,1)S(1)}, bf16[4,2112,128]{2,1,0:T(8,128)(2,1)S(1)}, u32[]{:S(2)}, u32[]{:S(2)}) collective-permute-start(bf16[4,2112,128]{2,1,0:T(8,128)(2,1)S(1)} %get-tuple-element.256), channel_id=1, source_target_pairs={{0,24},{1,97},{8,0},{9,105},{16,8},{17,113},{24,16},{25,121},{32,5... | collective-permute-start | bytes 6488072 | tf_op jit(solution)/shard_map/ppermute | solution.py:577
  145.3 3.0 %collective-permute-start.30 = (bf16[64,2048]{1,0:T(8,128)(2,1)S(1)}, bf16[64,2048]{1,0:T(8,128)(2,1)S(1)}, u32[]{:S(2)}, u32[]{:S(2)}) collective-permute-start(bf16[64,2048]{1,0:T(8,128)(2,1)S(1)} %get-tuple-element.239.refs_1_), channel_id=1, source_target_pairs={{0,4},{2,6},{4,0},{6,2},{1,5},{3,7},{5,1},{7,3},{8,12},{10,14},{12... | collective-permute-start | bytes 786440 | tf_op jit(solution)/shard_map/ppermute | solution.py:542
  150.3 4.8 %shard_map.319 = (bf16[4,512,256]{2,1,0:T(8,128)(2,1)S(1)}, bf16[4,512,256]{2,1,0:T(8,128)(2,1)S(1)}, f32[8,128]{1,0:T(8,128)S(1)}) custom-call(s32[4]{0:T(128)S(1)} %pad_add_fusion.refs_0_.mine, bf16[704,512]{1,0:T(8,128)(2,1)S(1)} %get-tuple-element.217.product.refs_5_, bf16[704,2048]{1,0:T(8,128)(2,1)S(1)} %bitcast.36, ...), custom_call_target="tpu_custom_call" | custom-call | flops 44000000 | tf_op jit(solution)/shard_map/pallas_call | solution.py:1075
  166.2 2.8 collective-permute-start.36
  169.0 3.4 %collective-permute-start.34 = (bf16[2,128,256]{2,1,0:T(8,128)(2,1)S(1)}, bf16[2,128,256]{2,1,0:T(8,128)(2,1)S(1)}, u32[]{:S(2)}, u32[]{:S(2)}) collective-permute-start(bf16[2,128,256]{2,1,0:T(8,128)(2,1)S(1)} %get-tuple-element.250.refs_2_), channel_id=1, source_target_pairs={{0,24},{8,0},{16,8},{24,16},{1,25},{9,1},{17,9},{25,17},{2,26},{10... | collective-permute-start | bytes 393224 | tf_op jit(solution)/shard_map/ppermute | solution.py:542
  172.4 3.3 %shard_map.329 = (bf16[4,1024,128]{2,1,0:T(8,128)(2,1)S(1)}, bf16[4,1024,128]{2,1,0:T(8,128)(2,1)S(1)}, bf16[4,1024,128]{2,1,0:T(8,128)(2,1)S(1)}, bf16[4,1024,128]{2,1,0:T(8,128)(2,1)S(1)}, f32[1,2048]{1,0:T(1,128)S(1)}) custom-call(s32[4]{0:T(128)S(1)} %pad_add_fusion.refs_0_.mine, bf16[512,2048]{1,0:T(8,128)(2,1)S(1)} %get-tuple-element.248.refs_1_, ...), custom_call_target="tpu_custom_call" | custom-call | flops 55000000 | tf_op jit(solution)/shard_map/pallas_call | solution.py:431
  187.6 3.2 %collective-permute-start.47 = (bf16[2112,128]{1,0:T(8,128)(2,1)S(1)}, bf16[2112,128]{1,0:T(8,128)(2,1)S(1)}, u32[]{:S(2)}, u32[]{:S(2)}) collective-permute-start(bf16[2112,128]{1,0:T(8,128)(2,1)S(1)} %get-tuple-element.307), channel_id=1, source_target_pairs={{0,96},{1,25},{8,104},{9,1},{16,112},{17,9},{24,120},{25,17},{32,0... | collective-permute-start | bytes 1622024 | tf_op jit(solution)/shard_map/ppermute | solution.py:577
  190.9 3.1 %collective-permute-start.39 = (bf16[2,512,256]{2,1,0:T(8,128)(2,1)}, bf16[2,512,256]{2,1,0:T(8,128)(2,1)S(1)}, u32[]{:S(2)}, u32[]{:S(2)}) collective-permute-start(bf16[2,512,256]{2,1,0:T(8,128)(2,1)} %get-tuple-element.260), channel_id=1, source_target_pairs={{0,4},{2,6},{4,0},{6,2},{1,5},{3,7},{5,1},{7,3},{8,12},{10,14},{12... | collective-permute-start | bytes 1572872 | tf_op jit(solution)/shard_map/ppermute | solution.py:716
  194.0 8.0 %shard_map.335 = (bf16[528,1024]{1,0:T(8,128)(2,1)S(1)}, bf16[16,1024]{1,0:T(8,128)(2,1)S(1)}, f32[512,2]{1,0:T(8,128)S(1)}, f32[16,528]{1,0:T(8,128)S(1)}, f32[8,1024]{1,0:T(8,128)S(1)}, /*index=5*/f32[528,1]{1,0:T(8,128)S(1)}) custom-call(s32[4]{0:T(128)S(1)} %pad_add_fusion.refs_0_.mine, bf16[4,2,144,384]{3,2,1,0:T(8,128)(2,1)S(1)} %copy-done.15, ...), custom_call_target="tpu_custom_call" | custom-call | flops 121000000 | tf_op jit(solution)/shard_map/pallas_call | solution.py:431
  203.3 4.6 %shard_map.336 = (bf16[4,2112,128]{2,1,0:T(8,128)(2,1)S(1)}, bf16[4,2112,128]{2,1,0:T(8,128)(2,1)S(1)}, bf16[4,2112,128]{2,1,0:T(8,128)(2,1)S(1)}, bf16[4,1056,1...) custom-call(s32[4]{0:T(128)S(1)} %pad_add_fusion.refs_0_.mine, ...), custom_call_target="tpu_custom_call" | custom-call | flops 66000000 | tf_op jit(solution)/shard_map/pallas_call | solution.py:431
  214.0 6.9 %shard_map.341 = (bf16[4,528,256]{2,1,0:T(8,128)(2,1)S(1)}, bf16[4,528,256]{2,1,0:T(8,128)(2,1)S(1)}, f32[8,128]{1,0:T(8,128)S(1)}) custom-call(s32[4]{0:T(128)S(1)} %pad_add_fusion.refs_0_.mine, bf16[528,1024]{1,0:T(8,128)(2,1)S(1)} %get-tuple-element.283.refs_3_.dproj, bf16[16,1024]{1,0:T(8,128)(2,1)S(1)} %collective-permute-done.44.refs_6_.arrived, ...), custom_call_target="tpu_custom_call" | custom-call | flops 66000000 | tf_op jit(solution)/shard_map/pallas_call | solution.py:1132
  221.9 5.0 %collective-permute-done.50.refs_3_ = bf16[4,1056,128]{2,1,0:T(8,128)(2,1)S(1)} collective-permute-done((bf16[4,1056,128]{2,1,0:T(8,128)(2,1)S(1)}, bf16[4,1056,128]{2,1,0:T(8,128)(2,1)S(1)}, u32[]{:S(2)}, u32[]{:S(2)}) %collective-permute-start.50) | collective-permute-done | bytes 1081376 | tf_op jit(solution)/shard_map/ppermute | solution.py:577
  234.3 5.0 %collective-permute-done.54.refs_3_ = f32[3,4,8,128]{3,2,1,0:T(8,128)S(1)} collective-permute-done((f32[3,4,8,128]{3,2,1,0:T(8,128)S(1)}, f32[3,4,8,128]{3,2,1,0:T(8,128)S(1)}, u32[]{:S(2)}, u32[]{:S(2)}) %collective-permute-start.54) | collective-permute-done | bytes 49184 | tf_op jit(solution)/shard_map/ppermute | solution.py:542
  239.3 4.1 %collective-permute-done.52.refs_1_ = f32[3,4,8,128]{3,2,1,0:T(8,128)S(1)} collective-permute-done((f32[3,4,8,128]{3,2,1,0:T(8,128)S(1)}, f32[3,4,8,128]{3,2,1,0:T(8,128)S(1)}, u32[]{:S(2)}, u32[]{:S(2)}) %collective-permute-start.52) | collective-permute-done | bytes 49184 | tf_op jit(solution)/shard_map/ppermute | solution.py:542
  246.3 3.2 %collective-permute-start.60 = (f32[4,8,128]{2,1,0:T(8,128)S(1)}, f32[4,8,128]{2,1,0:T(8,128)S(1)}, u32[]{:S(2)}, u32[]{:S(2)}) collective-permute-start(f32[4,8,128]{2,1,0:T(8,128)S(1)} %get-tuple-element.334), channel_id=1, source_target_pairs={{0,24},{1,97},{8,0},{9,105},{16,8},{17,113},{24,16},{25,121},{32,5... | collective-permute-start | bytes 49160 | tf_op jit(solution)/shard_map/ppermute | solution.py:577
  249.6 8.2 %collective-permute-done.59.refs_5_ = f32[4,8,128]{2,1,0:T(8,128)S(1)} collective-permute-done((f32[4,8,128]{2,1,0:T(8,128)S(1)}, f32[4,8,128]{2,1,0:T(8,128)S(1)}, u32[]{:S(2)}, u32[]{:S(2)}) %collective-permute-start.59) | collective-permute-done | bytes 16416 | tf_op jit(solution)/shard_map/ppermute | solution.py:577
  259.4 2.9 %collective-permute-start.61 = (bf16[2112,128]{1,0:T(8,128)(2,1)S(1)}, bf16[2112,128]{1,0:T(8,128)(2,1)S(1)}, u32[]{:S(2)}, u32[]{:S(2)}) collective-permute-start(bf16[2112,128]{1,0:T(8,128)(2,1)S(1)} %get-tuple-element.336), channel_id=1, source_target_pairs={{0,32},{1,9},{8,40},{9,17},{16,48},{17,25},{24,56},{25,1},{32,64},... | collective-permute-start | bytes 1622024 | tf_op jit(solution)/shard_map/ppermute | solution.py:577
  266.9 6.5 %collective-permute-done.56.refs_2_ = bf16[528,256]{1,0:T(8,128)(2,1)S(1)} collective-permute-done((bf16[528,256]{1,0:T(8,128)(2,1)S(1)}, bf16[528,256]{1,0:T(8,128)(2,1)S(1)}, u32[]{:S(2)}, u32[]{:S(2)}) %collective-permute-start.56) | collective-permute-done | bytes 270368 | tf_op jit(solution)/shard_map/ppermute | solution.py:716
  275.1 3.4 %collective-permute-done.63.refs_3_ = bf16[2112,128]{1,0:T(8,128)(2,1)S(1)} collective-permute-done((bf16[2112,128]{1,0:T(8,128)(2,1)S(1)}, bf16[2112,128]{1,0:T(8,128)(2,1)S(1)}, u32[]{:S(2)}, u32[]{:S(2)}) %collective-permute-start.63) | collective-permute-done | bytes 540704 | tf_op jit(solution)/shard_map/ppermute | solution.py:577
  (215 shorter events, 129.5 us)
Async XLA Ops:
  0.7 12.7 %collective-permute-start.2 = (bf16[512,256]{1,0:T(8,128)(2,1)}, bf16[512,256]{1,0:T(8,128)(2,1)S(1)}, u32[]{:S(2)}, u32[]{:S(2)}) collective-permute-start(bf16[512,256]{1,0:T(8,128)(2,1)} %refs_3_.3), channel_id=1, source_target_pairs={{0,4},{2,6},{4,0},{6,2},{1,5},{3,7},{5,1},{7,3},{8,12},{10,14},{12... | collective-permute-start | bytes 786440 | tf_op jit(solution)/shard_map/ppermute | solution.py:542
  2.9 13.3 %collective-permute-start.1 = (bf16[512,256]{1,0:T(8,128)(2,1)}, bf16[512,256]{1,0:T(8,128)(2,1)S(1)}, u32[]{:S(2)}, u32[]{:S(2)}) collective-permute-start(bf16[512,256]{1,0:T(8,128)(2,1)} %refs_3_.3), channel_id=1, source_target_pairs={{0,2},{2,4},{4,6},{6,0},{1,3},{3,5},{5,7},{7,1},{8,10},{10,12},{12... | collective-permute-start | bytes 786440 | tf_op jit(solution)/shard_map/ppermute | solution.py:542
  2.9 13.3 %collective-permute-start = (bf16[512,256]{1,0:T(8,128)(2,1)}, bf16[512,256]{1,0:T(8,128)(2,1)S(1)}, u32[]{:S(2)}, u32[]{:S(2)}) collective-permute-start(bf16[512,256]{1,0:T(8,128)(2,1)} %refs_3_.3), channel_id=1, source_target_pairs={{0,6},{2,0},{4,2},{6,4},{1,7},{3,1},{5,3},{7,5},{8,14},{10,8},{12,... | collective-permute-start | bytes 786440 | tf_op jit(solution)/shard_map/ppermute | solution.py:542
  60.2 14.1 %collective-permute-start.17 = (bf16[512,256]{1,0:T(8,128)(2,1)S(1)}, bf16[512,256]{1,0:T(8,128)(2,1)S(1)}, u32[]{:S(2)}, u32[]{:S(2)}) collective-permute-start(bf16[512,256]{1,0:T(8,128)(2,1)S(1)} %shard_map.313.refs_1_), channel_id=1, source_target_pairs={{0,4},{2,6},{4,0},{6,2},{1,5},{3,7},{5,1},{7,3},{8,12},{10,14},{12... | collective-permute-start | bytes 786440 | tf_op jit(solution)/shard_map/ppermute | solution.py:542
  62.3 11.9 %collective-permute-start.16 = (bf16[512,256]{1,0:T(8,128)(2,1)S(1)}, bf16[512,256]{1,0:T(8,128)(2,1)S(1)}, u32[]{:S(2)}, u32[]{:S(2)}) collective-permute-start(bf16[512,256]{1,0:T(8,128)(2,1)S(1)} %shard_map.313.refs_1_), channel_id=1, source_target_pairs={{0,2},{2,4},{4,6},{6,0},{1,3},{3,5},{5,7},{7,1},{8,10},{10,12},{12... | collective-permute-start | bytes 786440 | tf_op jit(solution)/shard_map/ppermute | solution.py:542
  63.2 11.2 %collective-permute-start.15 = (bf16[512,256]{1,0:T(8,128)(2,1)S(1)}, bf16[512,256]{1,0:T(8,128)(2,1)S(1)}, u32[]{:S(2)}, u32[]{:S(2)}) collective-permute-start(bf16[512,256]{1,0:T(8,128)(2,1)S(1)} %shard_map.313.refs_1_), channel_id=1, source_target_pairs={{0,6},{2,0},{4,2},{6,4},{1,7},{3,1},{5,3},{7,5},{8,14},{10,8},{12,... | collective-permute-start | bytes 786440 | tf_op jit(solution)/shard_map/ppermute | solution.py:542
  80.2 13.7 %collective-permute-start.14 = (bf16[64,2048]{1,0:T(8,128)(2,1)S(1)}, bf16[64,2048]{1,0:T(8,128)(2,1)S(1)}, u32[]{:S(2)}, u32[]{:S(2)}) collective-permute-start(bf16[64,2048]{1,0:T(8,128)(2,1)S(1)} %get-tuple-element.211), channel_id=1, source_target_pairs={{0,4},{2,6},{4,0},{6,2},{1,5},{3,7},{5,1},{7,3},{8,12},{10,14},{12... | collective-permute-start | bytes 786440 | tf_op jit(solution)/shard_map/ppermute | solution.py:542
  94.2 10.9 %collective-permute-start.21 = (bf16[64,2048]{1,0:T(8,128)(2,1)S(1)}, bf16[64,2048]{1,0:T(8,128)(2,1)S(1)}, u32[]{:S(2)}, u32[]{:S(2)}) collective-permute-start(bf16[64,2048]{1,0:T(8,128)(2,1)S(1)} %get-tuple-element.215.refs_1_), channel_id=1, source_target_pairs={{0,4},{2,6},{4,0},{6,2},{1,5},{3,7},{5,1},{7,3},{8,12},{10,14},{12... | collective-permute-start | bytes 786440 | tf_op jit(solution)/shard_map/ppermute | solution.py:542
  96.1 11.1 %collective-permute-start.20 = (bf16[64,2048]{1,0:T(8,128)(2,1)S(1)}, bf16[64,2048]{1,0:T(8,128)(2,1)S(1)}, u32[]{:S(2)}, u32[]{:S(2)}) collective-permute-start(bf16[64,2048]{1,0:T(8,128)(2,1)S(1)} %get-tuple-element.215.refs_1_), channel_id=1, source_target_pairs={{0,2},{2,4},{4,6},{6,0},{1,3},{3,5},{5,7},{7,1},{8,10},{10,12},{12... | collective-permute-start | bytes 786440 | tf_op jit(solution)/shard_map/ppermute | solution.py:542
  96.6 12.0 %collective-permute-start.19 = (bf16[64,2048]{1,0:T(8,128)(2,1)S(1)}, bf16[64,2048]{1,0:T(8,128)(2,1)S(1)}, u32[]{:S(2)}, u32[]{:S(2)}) collective-permute-start(bf16[64,2048]{1,0:T(8,128)(2,1)S(1)} %get-tuple-element.215.refs_1_), channel_id=1, source_target_pairs={{0,6},{2,0},{4,2},{6,4},{1,7},{3,1},{5,3},{7,5},{8,14},{10,8},{12,... | collective-permute-start | bytes 786440 | tf_op jit(solution)/shard_map/ppermute | solution.py:542
  121.9 19.5 %collective-permute-start.31 = (bf16[4,1056,128]{2,1,0:T(8,128)(2,1)S(1)}, bf16[4,1056,128]{2,1,0:T(8,128)(2,1)S(1)}, u32[]{:S(2)}, u32[]{:S(2)}) collective-permute-start(bf16[4,1056,128]{2,1,0:T(8,128)(2,1)S(1)} %get-tuple-element.243), channel_id=1, source_target_pairs={{0,8},{1,33},{8,16},{9,41},{16,24},{17,49},{24,0},{25,57},{32,40},... | collective-permute-start | bytes 3244040 | tf_op jit(solution)/shard_map/ppermute | solution.py:577
  122.2 19.2 %collective-permute-start.32 = (bf16[4,1056,128]{2,1,0:T(8,128)(2,1)S(1)}, bf16[4,1056,128]{2,1,0:T(8,128)(2,1)S(1)}, u32[]{:S(2)}, u32[]{:S(2)}) collective-permute-start(bf16[4,1056,128]{2,1,0:T(8,128)(2,1)S(1)} %get-tuple-element.244), channel_id=1, source_target_pairs={{0,24},{1,97},{8,0},{9,105},{16,8},{17,113},{24,16},{25,121},{32,5... | collective-permute-start | bytes 3244040 | tf_op jit(solution)/shard_map/ppermute | solution.py:577
  128.1 12.9 %collective-permute-start.27 = (bf16[64,2048]{1,0:T(8,128)(2,1)S(1)}, bf16[64,2048]{1,0:T(8,128)(2,1)S(1)}, u32[]{:S(2)}, u32[]{:S(2)}) collective-permute-start(bf16[64,2048]{1,0:T(8,128)(2,1)S(1)} %get-tuple-element.236), channel_id=1, source_target_pairs={{0,4},{2,6},{4,0},{6,2},{1,5},{3,7},{5,1},{7,3},{8,12},{10,14},{12... | collective-permute-start | bytes 786440 | tf_op jit(solution)/shard_map/ppermute | solution.py:542
  142.0 33.6 %collective-permute-start.37 = (bf16[4,2112,128]{2,1,0:T(8,128)(2,1)S(1)}, bf16[4,2112,128]{2,1,0:T(8,128)(2,1)S(1)}, u32[]{:S(2)}, u32[]{:S(2)}) collective-permute-start(bf16[4,2112,128]{2,1,0:T(8,128)(2,1)S(1)} %get-tuple-element.255), channel_id=1, source_target_pairs={{0,8},{1,33},{8,16},{9,41},{16,24},{17,49},{24,0},{25,57},{32,40},... | collective-permute-start | bytes 6488072 | tf_op jit(solution)/shard_map/ppermute | solution.py:577
  142.4 33.3 %collective-permute-start.38 = (bf16[4,2112,128]{2,1,0:T(8,128)(2,1)S(1)}, bf16[4,2112,128]{2,1,0:T(8,128)(2,1)S(1)}, u32[]{:S(2)}, u32[]{:S(2)}) collective-permute-start(bf16[4,2112,128]{2,1,0:T(8,128)(2,1)S(1)} %get-tuple-element.256), channel_id=1, source_target_pairs={{0,24},{1,97},{8,0},{9,105},{16,8},{17,113},{24,16},{25,121},{32,5... | collective-permute-start | bytes 6488072 | tf_op jit(solution)/shard_map/ppermute | solution.py:577
  145.3 11.7 %collective-permute-start.30 = (bf16[64,2048]{1,0:T(8,128)(2,1)S(1)}, bf16[64,2048]{1,0:T(8,128)(2,1)S(1)}, u32[]{:S(2)}, u32[]{:S(2)}) collective-permute-start(bf16[64,2048]{1,0:T(8,128)(2,1)S(1)} %get-tuple-element.239.refs_1_), channel_id=1, source_target_pairs={{0,4},{2,6},{4,0},{6,2},{1,5},{3,7},{5,1},{7,3},{8,12},{10,14},{12... | collective-permute-start | bytes 786440 | tf_op jit(solution)/shard_map/ppermute | solution.py:542
  166.2 10.9 %collective-permute-start.36 = (bf16[2,128,256]{2,1,0:T(8,128)(2,1)S(1)}, bf16[2,128,256]{2,1,0:T(8,128)(2,1)S(1)}, u32[]{:S(2)}, u32[]{:S(2)}) collective-permute-start(bf16[2,128,256]{2,1,0:T(8,128)(2,1)S(1)} %get-tuple-element.250.refs_2_), channel_id=1, source_target_pairs={{0,16},{8,24},{16,0},{24,8},{1,17},{9,25},{17,1},{25,9},{2,18},{10... | collective-permute-start | bytes 393224 | tf_op jit(solution)/shard_map/ppermute | solution.py:542
  187.6 21.1 %collective-permute-start.46 = (bf16[2112,128]{1,0:T(8,128)(2,1)S(1)}, bf16[2112,128]{1,0:T(8,128)(2,1)S(1)}, u32[]{:S(2)}, u32[]{:S(2)}) collective-permute-start(bf16[2112,128]{1,0:T(8,128)(2,1)S(1)} %get-tuple-element.306), channel_id=1, source_target_pairs={{0,32},{1,9},{8,40},{9,17},{16,48},{17,25},{24,56},{25,1},{32,64},... | collective-permute-start | bytes 1622024 | tf_op jit(solution)/shard_map/ppermute | solution.py:577
  187.6 21.1 %collective-permute-start.47 = (bf16[2112,128]{1,0:T(8,128)(2,1)S(1)}, bf16[2112,128]{1,0:T(8,128)(2,1)S(1)}, u32[]{:S(2)}, u32[]{:S(2)}) collective-permute-start(bf16[2112,128]{1,0:T(8,128)(2,1)S(1)} %get-tuple-element.307), channel_id=1, source_target_pairs={{0,96},{1,25},{8,104},{9,1},{16,112},{17,9},{24,120},{25,17},{32,0... | collective-permute-start | bytes 1622024 | tf_op jit(solution)/shard_map/ppermute | solution.py:577
  190.9 17.9 %collective-permute-start.48 = (bf16[2112,128]{1,0:T(8,128)(2,1)S(1)}, bf16[2112,128]{1,0:T(8,128)(2,1)S(1)}, u32[]{:S(2)}, u32[]{:S(2)}) collective-permute-start(bf16[2112,128]{1,0:T(8,128)(2,1)S(1)} %get-tuple-element.308), channel_id=1, source_target_pairs={{0,64},{1,17},{8,72},{9,25},{16,80},{17,1},{24,88},{25,9},{32,96},... | collective-permute-start | bytes 1622024 | tf_op jit(solution)/shard_map/ppermute | solution.py:577
  190.9 17.1 %collective-permute-start.39 = (bf16[2,512,256]{2,1,0:T(8,128)(2,1)}, bf16[2,512,256]{2,1,0:T(8,128)(2,1)S(1)}, u32[]{:S(2)}, u32[]{:S(2)}) collective-permute-start(bf16[2,512,256]{2,1,0:T(8,128)(2,1)} %get-tuple-element.260), channel_id=1, source_target_pairs={{0,4},{2,6},{4,0},{6,2},{1,5},{3,7},{5,1},{7,3},{8,12},{10,14},{12... | collective-permute-start | bytes 1572872 | tf_op jit(solution)/shard_map/ppermute | solution.py:716
  210.5 16.4 %collective-permute-start.50 = (bf16[4,1056,128]{2,1,0:T(8,128)(2,1)S(1)}, bf16[4,1056,128]{2,1,0:T(8,128)(2,1)S(1)}, u32[]{:S(2)}, u32[]{:S(2)}) collective-permute-start(bf16[4,1056,128]{2,1,0:T(8,128)(2,1)S(1)} %get-tuple-element.317), channel_id=1, source_target_pairs={{0,8},{1,33},{8,16},{9,41},{16,24},{17,49},{24,0},{25,57},{32,40},... | collective-permute-start | bytes 3244040 | tf_op jit(solution)/shard_map/ppermute | solution.py:577
  213.2 15.2 %collective-permute-start.51 = (bf16[4,1056,128]{2,1,0:T(8,128)(2,1)S(1)}, bf16[4,1056,128]{2,1,0:T(8,128)(2,1)S(1)}, u32[]{:S(2)}, u32[]{:S(2)}) collective-permute-start(bf16[4,1056,128]{2,1,0:T(8,128)(2,1)S(1)} %get-tuple-element.318), channel_id=1, source_target_pairs={{0,24},{1,97},{8,0},{9,105},{16,8},{17,113},{24,16},{25,121},{32,5... | collective-permute-start | bytes 3244040 | tf_op jit(solution)/shard_map/ppermute | solution.py:577
  229.6 28.3 %collective-permute-start.57 = (bf16[4,2112,128]{2,1,0:T(8,128)(2,1)S(1)}, bf16[4,2112,128]{2,1,0:T(8,128)(2,1)S(1)}, u32[]{:S(2)}, u32[]{:S(2)}) collective-permute-start(bf16[4,2112,128]{2,1,0:T(8,128)(2,1)S(1)} %get-tuple-element.330), channel_id=1, source_target_pairs={{0,8},{1,33},{8,16},{9,41},{16,24},{17,49},{24,0},{25,57},{32,40},... | collective-permute-start | bytes 6488072 | tf_op jit(solution)/shard_map/ppermute | solution.py:577
  231.0 26.9 %collective-permute-start.58 = (bf16[4,2112,128]{2,1,0:T(8,128)(2,1)S(1)}, bf16[4,2112,128]{2,1,0:T(8,128)(2,1)S(1)}, u32[]{:S(2)}, u32[]{:S(2)}) collective-permute-start(bf16[4,2112,128]{2,1,0:T(8,128)(2,1)S(1)} %get-tuple-element.331), channel_id=1, source_target_pairs={{0,24},{1,97},{8,0},{9,105},{16,8},{17,113},{24,16},{25,121},{32,5... | collective-permute-start | bytes 6488072 | tf_op jit(solution)/shard_map/ppermute | solution.py:577
  232.9 10.5 %collective-permute-start.49 = (bf16[4,528,256]{2,1,0:T(8,128)(2,1)S(1)}, bf16[4,528,256]{2,1,0:T(8,128)(2,1)S(1)}, u32[]{:S(2)}, u32[]{:S(2)}) collective-permute-start(bf16[4,528,256]{2,1,0:T(8,128)(2,1)S(1)} %get-tuple-element.313), channel_id=1, source_target_pairs={{0,1},{1,0},{2,3},{3,2},{4,5},{5,4},{6,7},{7,6},{8,9},{9,8},{10,11... | collective-permute-start | bytes 3244040 | tf_op jit(solution)/shard_map/ppermute | solution.py:542
  244.5 21.2 %collective-permute-start.55 = (bf16[2,528,256]{2,1,0:T(8,128)(2,1)S(1)}, bf16[2,528,256]{2,1,0:T(8,128)(2,1)S(1)}, u32[]{:S(2)}, u32[]{:S(2)}) collective-permute-start(bf16[2,528,256]{2,1,0:T(8,128)(2,1)S(1)} %get-tuple-element.325), channel_id=1, source_target_pairs={{0,4},{2,6},{4,0},{6,2},{1,5},{3,7},{5,1},{7,3},{8,12},{10,14},{12... | collective-permute-start | bytes 1622024 | tf_op jit(solution)/shard_map/ppermute | solution.py:716
  246.3 11.5 %collective-permute-start.59 = (f32[4,8,128]{2,1,0:T(8,128)S(1)}, f32[4,8,128]{2,1,0:T(8,128)S(1)}, u32[]{:S(2)}, u32[]{:S(2)}) collective-permute-start(f32[4,8,128]{2,1,0:T(8,128)S(1)} %get-tuple-element.333), channel_id=1, source_target_pairs={{0,8},{1,33},{8,16},{9,41},{16,24},{17,49},{24,0},{25,57},{32,40},... | collective-permute-start | bytes 49160 | tf_op jit(solution)/shard_map/ppermute | solution.py:577
  246.3 11.5 %collective-permute-start.60 = (f32[4,8,128]{2,1,0:T(8,128)S(1)}, f32[4,8,128]{2,1,0:T(8,128)S(1)}, u32[]{:S(2)}, u32[]{:S(2)}) collective-permute-start(f32[4,8,128]{2,1,0:T(8,128)S(1)} %get-tuple-element.334), channel_id=1, source_target_pairs={{0,24},{1,97},{8,0},{9,105},{16,8},{17,113},{24,16},{25,121},{32,5... | collective-permute-start | bytes 49160 | tf_op jit(solution)/shard_map/ppermute | solution.py:577
  259.4 15.7 %collective-permute-start.61 = (bf16[2112,128]{1,0:T(8,128)(2,1)S(1)}, bf16[2112,128]{1,0:T(8,128)(2,1)S(1)}, u32[]{:S(2)}, u32[]{:S(2)}) collective-permute-start(bf16[2112,128]{1,0:T(8,128)(2,1)S(1)} %get-tuple-element.336), channel_id=1, source_target_pairs={{0,32},{1,9},{8,40},{9,17},{16,48},{17,25},{24,56},{25,1},{32,64},... | collective-permute-start | bytes 1622024 | tf_op jit(solution)/shard_map/ppermute | solution.py:577
  262.3 12.8 %collective-permute-start.62 = (bf16[2112,128]{1,0:T(8,128)(2,1)S(1)}, bf16[2112,128]{1,0:T(8,128)(2,1)S(1)}, u32[]{:S(2)}, u32[]{:S(2)}) collective-permute-start(bf16[2112,128]{1,0:T(8,128)(2,1)S(1)} %get-tuple-element.337), channel_id=1, source_target_pairs={{0,96},{1,25},{8,104},{9,1},{16,112},{17,9},{24,120},{25,17},{32,0... | collective-permute-start | bytes 1622024 | tf_op jit(solution)/shard_map/ppermute | solution.py:577
  263.8 14.6 %collective-permute-start.63 = (bf16[2112,128]{1,0:T(8,128)(2,1)S(1)}, bf16[2112,128]{1,0:T(8,128)(2,1)S(1)}, u32[]{:S(2)}, u32[]{:S(2)}) collective-permute-start(bf16[2112,128]{1,0:T(8,128)(2,1)S(1)} %get-tuple-element.338), channel_id=1, source_target_pairs={{0,64},{1,17},{8,72},{9,25},{16,80},{17,1},{24,88},{25,9},{32,96},... | collective-permute-start | bytes 1622024 | tf_op jit(solution)/shard_map/ppermute | solution.py:577
  (65 other events, 565.4 us)
